TPU v7x, 768 devices: a whole 4x8x12 slice. The times are simulated.
768 devices in a mesh: circ: 16 (over x, z_lo), rad: 6 (over z_hi, core), mode: 8 (over y).
Axes of the slice: x: 4, y: 8, z: 12 (z_hi: 3, z_lo: 4; z = z_hi * 4 + z_lo), core: 2. Of those that a mesh axis runs over, the one named last changes fastest.
Arguments:
- adjoint_prev: float32 [3, 64, 48, 2048], P(None, 'circ', 'rad', 'mode'), may hold values from -6 to 6
- cell_class: int32 [64, 48, 2048], P('circ', 'rad', 'mode'), may hold values from 0 to 7
- class_moduli: float32 [8], replicated, may hold values from 0.2 to 5
- flow_sens: float32 [16, 6, 8, 8, 3, 512], P('circ', 'rad', 'mode'), may hold values from -12 to 12
- flow_nodes: int32 [16, 6, 8, 8, 512], P('circ', 'rad', 'mode'), may hold values from 0 to 8191
- flow_count: int32 [16, 6, 8, 8], P('circ', 'rad', 'mode'), may hold values from 64 to 512, as said below
- surf_ids: int32 [16, 6, 8, 512], P('circ', 'rad', 'mode'), may hold values from 0 to 8191
- mode_shapes: float32 [16, 6, 8, 24, 3, 512], P('circ', 'rad', 'mode'), may hold values from -0.03125 to 0.03125
Outputs:
- adjoint: float32 [3, 64, 48, 2048], P(None, 'circ', 'rad', 'mode')
- gen_force: float32 [24, 16], P('mode', 'circ')
Inputs may be any that keep to these rules, and one draw needn't show every extreme that they name: In each group of devices that share c and r, one destination d, drawn, has flow_count equal to 512 from every source k; all other counts lie in 64 to 256. `flow_nodes`: A cell index within a block, last dimension fastest. `surf_ids`: A cell index within the listing block, last dimension fastest.
All inputs are finite; a program needn't handle non-finite values.
Results may differ from a plain program's by a relative error of at most 0.0003.
Values sent between devices are 32-bit elements; how exact they have to be, the bound alone decides.
No kernel may reach another device: no remote copies, remote signals or barrier semaphores. Data moves between devices by JAX's collectives and lax.ppermute only.
A program may use at most 32 MiB of HBM per device.

v0:
```python
import jax
import jax.numpy as jnp
from jax import lax
from jax.sharding import PartitionSpec as P

coupling = 0.5
relaxation = 0.6


def extended(cells, sides, width):
    for axis, dim in sides:
        count = lax.axis_size(axis)
        head = lax.slice_in_dim(cells, 0, width, axis=dim)
        tail = lax.slice_in_dim(cells, cells.shape[dim] - width, cells.shape[dim], axis=dim)
        cells = jnp.concatenate(
            [
                lax.ppermute(tail, axis, [(i, (i + 1) % count) for i in range(count)]),
                cells,
                lax.ppermute(head, axis, [((i + 1) % count, i) for i in range(count)]),
            ],
            axis=dim,
        )
    return cells


def neighbour_offsets():
    return [
        (a, b, c)
        for a in (-1, 0, 1)
        for b in (-1, 0, 1)
        for c in (-1, 0, 1)
        if (a, b, c) != (0, 0, 0)
    ]


def relax(lam_pad, e_pad, rhs):
    s1, s2, s3 = e_pad.shape

    def near(array, dx, dy, dz):
        return array[..., 1 + dx : s1 - 1 + dx, 1 + dy : s2 - 1 + dy, 1 + dz : s3 - 1 + dz]

    centre = near(lam_pad, 0, 0, 0)
    e_centre = near(e_pad, 0, 0, 0)
    action = jnp.zeros_like(centre)
    diagonal = jnp.zeros_like(centre)
    for dx, dy, dz in neighbour_offsets():
        square = float(dx * dx + dy * dy + dz * dz)
        link = 0.5 / square * (e_centre + near(e_pad, dx, dy, dz))
        diff = centre - near(lam_pad, dx, dy, dz)
        along = (dx * diff[0] + dy * diff[1] + dz * diff[2]) / square
        direction = jnp.array([dx, dy, dz], jnp.float32)[:, None, None, None]
        action = action + link[None] * (diff + coupling * direction * along[None])
        diagonal = diagonal + link[None] * (1.0 + coupling * direction * direction / square)
    return centre + relaxation * (rhs - action) / diagonal


def keep_vector(length, width, position_index, position_count):
    position = jnp.arange(length)
    at_start = position_index == 0
    at_end = position_index == position_count - 1
    dropped = at_start & (position < width) | at_end & (position >= length - width)
    return jnp.where(dropped, 0.0, 1.0).astype(jnp.float32)


def clear_outside(padded, width):
    rad_keep = keep_vector(padded.shape[-2], width, lax.axis_index("rad"), lax.axis_size("rad"))
    axial_keep = keep_vector(padded.shape[-1], width, lax.axis_index("mode"), lax.axis_size("mode"))
    return padded * rad_keep[:, None] * axial_keep[None, :]


def on_device(
    adjoint_prev, cell_class, class_moduli, flow_sens, flow_nodes, flow_count, surf_ids, mode_shapes
):
    ncomp, ncirc, nrad, naxial = adjoint_prev.shape
    cells = ncirc * nrad * naxial
    moduli = jnp.zeros(cell_class.shape, jnp.float32)
    for level in range(class_moduli.shape[0]):
        moduli = moduli + jnp.where(cell_class == level, class_moduli[level], jnp.float32(0.0))
    live = lax.broadcasted_iota(jnp.int32, flow_nodes.shape, 4) < flow_count[..., None]
    masked = jnp.where(live[:, :, :, :, None, :], flow_sens, jnp.float32(0.0))
    got_values, got_nodes = (
        lax.all_to_all(masked, "mode", split_axis=3, concat_axis=3, tiled=True),
        lax.all_to_all(flow_nodes, "mode", split_axis=3, concat_axis=3, tiled=True),
    )
    flat_values = jnp.moveaxis(got_values[0, 0, 0], 1, 0).reshape(3, -1)
    flat_nodes = got_nodes[0, 0, 0].reshape(-1)
    rhs = jnp.zeros((3, cells), jnp.float32).at[:, flat_nodes].add(flat_values)
    rhs = rhs.reshape(3, ncirc, nrad, naxial)
    stacked = jnp.concatenate([adjoint_prev, moduli[None]], axis=0)
    padded = extended(stacked, (("circ", 1), ("rad", 2), ("mode", 3)), 1)
    padded = clear_outside(padded, 1)
    middle = relax(padded[:3], padded[3], rhs)
    beside_all = extended(middle, (("circ", 1), ("rad", 2), ("mode", 3)), 1)
    final = relax(clear_outside(beside_all, 1), padded[3], rhs)
    flat_final = final.reshape(3, cells)
    picked = flat_final[:, surf_ids[0, 0, 0]]
    partial_force = jnp.einsum(
        "mps,ps->m", mode_shapes[0, 0, 0], picked, precision=lax.Precision.HIGHEST
    )
    owned = partial_force.shape[0] // lax.axis_size("mode")
    summed = lax.psum(partial_force, ("rad", "mode"))
    own_force = lax.dynamic_slice_in_dim(summed, lax.axis_index("mode") * owned, owned)
    return (final, own_force.reshape(owned, 1))


def solution(mesh):
    in_specs = (
        P(None, "circ", "rad", "mode"),
        P("circ", "rad", "mode"),
        P(),
        P("circ", "rad", "mode", None, None, None),
        P("circ", "rad", "mode", None, None),
        P("circ", "rad", "mode", None),
        P("circ", "rad", "mode", None),
        P("circ", "rad", "mode", None, None, None),
    )
    out_specs = (P(None, "circ", "rad", "mode"), P("mode", "circ"))
    return jax.shard_map(
        on_device, mesh=mesh, in_specs=in_specs, out_specs=out_specs, check_vma=False
    )
```

profile of v0, /device:TPU:8, one launch (start us, length us, event | category | flops | bytes accessed | tf_op | source)
XLA Modules:
  0.0 290.1 jit_solution(14557986491741561873)
XLA Ops:
  0.6 1.4 copy.75
  2.0 12.7 %all-to-all-start = ((s32[1,1,1,8,512]{4,2,1,0,3:T(1,128)}), s32[1,1,1,8,512]{4,2,1,0,3:T(1,128)S(1)}, u32[]{:S(2)}, u32[]{:S(2)}) async-start(s32[1,1,1,8,512]{4,2,1,0,3:T(1,128)} %copy.75), calls=%async_computation | async-start | bytes 32768 | tf_op jit(solution)/shard_map/all_to_all | solution.py:83
  14.7 1.6 fusion.190
  16.3 5.8 %add_bitcast_fusion = f32[1,4,8,256]{3,2,1,0:T(8,128)S(1)} fusion(s32[4,8,256]{2,1,0:T(8,128)} %param.61, f32[]{:T(128)} %bitcast.7, f32[]{:T(128)} %bitcast.6, f32[]{:T(128)} %bitcast.5, f32[]{:T(128)} %bitcast.4, f32[]{:T(128)} %bitcast.3, f32[]{:T(128)} %bitcast.2, f32[]{:T(128)} %bitcast.1, f32[]{:T(128)} %bitcast), kind=kLoop, calls=%fused_computation.404 | loop fusion | flops 188416 | bytes 65568 | tf_op jit(solution)/shard_map/broadcast_in_dim | solution.py:89
  22.1 0.8 pad_maximum_fusion.3
  22.9 4.9 %collective-permute-start.1 = (f32[4,1,8,256]{3,2,1,0:T(8,128)S(1)}, f32[4,1,8,256]{3,2,1,0:T(8,128)S(1)}, u32[]{:S(2)}, u32[]{:S(2)}) collective-permute-start(f32[4,1,8,256]{3,2,1,0:T(8,128)S(1)} %get-tuple-element.97), channel_id=1, source_target_pairs={{48,0},{96,48},{144,96},{192,144},{240,192},{288,240},{336,288},{3... | collective-permute-start | bytes 98312 | tf_op jit(solution)/shard_map/ppermute | solution.py:19
  27.8 1.9 collective-permute-start
  29.8 0.7 iota_compare_fusion
  30.5 1.5 copy_select_fusion
  32.0 5.5 %collective-permute-done = f32[4,1,8,256]{3,2,1,0:T(8,128)S(1)} collective-permute-done((f32[4,1,8,256]{3,2,1,0:T(8,128)S(1)}, f32[4,1,8,256]{3,2,1,0:T(8,128)S(1)}, u32[]{:S(2)}, u32[]{:S(2)}) %collective-permute-start) | collective-permute-done | bytes 32800 | tf_op jit(solution)/shard_map/ppermute | solution.py:17
  37.6 1.0 pad_maximum_fusion.7
  38.6 9.3 %collective-permute-start.3 = (f32[4,6,1,256]{3,2,1,0:T(1,128)S(1)}, f32[4,6,1,256]{3,2,1,0:T(1,128)S(1)}, u32[]{:S(2)}, u32[]{:S(2)}) collective-permute-start(f32[4,6,1,256]{3,2,1,0:T(1,128)S(1)} %get-tuple-element.59), channel_id=1, source_target_pairs={{8,0},{16,8},{24,16},{32,24},{40,32},{0,40},{9,1},{17,9},{25,17},{... | collective-permute-start | bytes 73736 | tf_op jit(solution)/shard_map/ppermute | solution.py:19
  47.9 1.9 collective-permute-start.2
  49.8 7.1 %collective-permute-done.2 = f32[4,6,1,256]{3,2,1,0:T(1,128)S(1)} collective-permute-done((f32[4,6,1,256]{3,2,1,0:T(1,128)S(1)}, f32[4,6,1,256]{3,2,1,0:T(1,128)S(1)}, u32[]{:S(2)}, u32[]{:S(2)}) %collective-permute-start.2) | collective-permute-done | bytes 24608 | tf_op jit(solution)/shard_map/ppermute | solution.py:17
  56.9 1.0 pad_maximum_fusion
  58.0 2.2 collective-permute-start.5
  60.2 3.6 %collective-permute-start.4 = (f32[4,6,10,1]{3,2,1,0:T(8,128)S(1)}, f32[4,6,10,1]{3,2,1,0:T(8,128)S(1)}, u32[]{:S(2)}, u32[]{:S(2)}) collective-permute-start(f32[4,6,10,1]{3,2,1,0:T(8,128)S(1)} %get-tuple-element.54), channel_id=1, source_target_pairs={{0,1},{1,2},{2,3},{3,4},{4,5},{5,6},{6,7},{7,0},{8,9},{9,10},{10,1... | collective-permute-start | bytes 2888 | tf_op jit(solution)/shard_map/ppermute | solution.py:17
  63.9 7.2 %all-to-all-start.1 = ((f32[1,1,1,8,3,512]{5,4,2,1,0,3:T(4,128)}), f32[1,1,1,8,3,512]{5,4,2,1,0,3:T(4,128)}, u32[]{:S(2)}, u32[]{:S(2)}) async-start(f32[1,1,1,8,3,512]{5,4,2,1,0,3:T(4,128)} %copy_select_fusion), calls=%async_computation.1 | async-start | bytes 131072 | tf_op jit(solution)/shard_map/all_to_all | solution.py:82
  71.7 1.3 fusion.2
  74.1 0.8 fusion.179
  74.9 0.8 broadcast_multiply_fusion.14
  75.7 0.6 fusion.87
  76.3 0.6 fusion.169
  76.9 0.6 fusion.94
  78.8 0.6 fusion.118
  80.7 0.6 fusion.138
  81.4 0.6 fusion.147
  82.6 0.6 fusion.160
  83.9 1.5 copy.77
  85.4 24.7 %scatter_custom_fusion = f32[3,8192]{0,1:T(8,128)} fusion(s32[4096]{0:T(1024)} %bitcast.146, f32[4096,3]{1,0:T(8,128)S(1)} %copy.77, f32[]{:T(128)} %constant.177.clone.1), kind=kCustom, calls=%fused_computation.2 | custom fusion | flops 12288 | bytes 98816 | tf_op jit(solution)/shard_map/scatter-add | solution.py:87
  110.5 3.0 %copy.78 = f32[3,4,8,256]{3,2,1,0:T(8,128)S(1)} copy(f32[3,4,8,256]{0,3,2,1:T(8,128)} %bitcast.142) | data formatting | bytes 196608 | tf_op jit(solution)/shard_map/reshape | solution.py:88
  113.8 2.0 divide_add_fusion.1
  115.8 3.2 %collective-permute-start.7 = (f32[3,1,8,256]{3,2,1,0:T(8,128)S(1)}, f32[3,1,8,256]{3,2,1,0:T(8,128)S(1)}, u32[]{:S(2)}, u32[]{:S(2)}) collective-permute-start(f32[3,1,8,256]{3,2,1,0:T(8,128)S(1)} %get-tuple-element.99), channel_id=1, source_target_pairs={{48,0},{96,48},{144,96},{192,144},{240,192},{288,240},{336,288},{3... | collective-permute-start | bytes 73736 | tf_op jit(solution)/shard_map/ppermute | solution.py:19
  119.0 2.7 collective-permute-start.6
  121.7 7.0 %collective-permute-done.6 = f32[3,1,8,256]{3,2,1,0:T(8,128)S(1)} collective-permute-done((f32[3,1,8,256]{3,2,1,0:T(8,128)S(1)}, f32[3,1,8,256]{3,2,1,0:T(8,128)S(1)}, u32[]{:S(2)}, u32[]{:S(2)}) %collective-permute-start.6) | collective-permute-done | bytes 24608 | tf_op jit(solution)/shard_map/ppermute | solution.py:17
  128.8 1.9 collective-permute-start.9
  130.7 2.4 collective-permute-start.8
  133.1 0.7 compare_select_fusion.1
  133.8 5.9 %collective-permute-done.8 = f32[3,6,1,256]{3,2,1,0:T(1,128)S(1)} collective-permute-done((f32[3,6,1,256]{3,2,1,0:T(1,128)S(1)}, f32[3,6,1,256]{3,2,1,0:T(1,128)S(1)}, u32[]{:S(2)}, u32[]{:S(2)}) %collective-permute-start.8) | collective-permute-done | bytes 18464 | tf_op jit(solution)/shard_map/ppermute | solution.py:17
  139.9 2.5 collective-permute-start.11
  142.3 3.5 %collective-permute-start.10 = (f32[3,6,10,1]{3,2,1,0:T(8,128)S(1)}, f32[3,6,10,1]{3,2,1,0:T(8,128)S(1)}, u32[]{:S(2)}, u32[]{:S(2)}) collective-permute-start(f32[3,6,10,1]{3,2,1,0:T(8,128)S(1)} %get-tuple-element.56), channel_id=1, source_target_pairs={{0,1},{1,2},{2,3},{3,4},{4,5},{5,6},{6,7},{7,0},{8,9},{9,10},{10,1... | collective-permute-start | bytes 2168 | tf_op jit(solution)/shard_map/ppermute | solution.py:17
  145.9 1.0 collective-permute-done.11
  146.9 3.1 %collective-permute-done.10 = f32[3,6,10,1]{3,2,1,0:T(8,128)S(1)} collective-permute-done((f32[3,6,10,1]{3,2,1,0:T(8,128)S(1)}, f32[3,6,10,1]{3,2,1,0:T(8,128)S(1)}, u32[]{:S(2)}, u32[]{:S(2)}) %collective-permute-start.10) | collective-permute-done | bytes 752 | tf_op jit(solution)/shard_map/ppermute | solution.py:17
  150.0 1.0 fusion.3
  152.9 1.0 divide_add_fusion
  154.0 2.7 copy.80
  156.7 3.2 %gather_fusion = f32[512,3]{1,0:T(8,128)S(1)} fusion(f32[3,8192]{0,1:T(8,128)} %bitcast.143, s32[1024]{0:T(1024)S(1)} %pad_clamp_fusion), kind=kCustom, calls=%fused_computation | custom fusion | bytes 14336 | tf_op jit(solution)/shard_map/gather | solution.py:96
  160.2 129.3 %psum.7 = f32[24]{0:T(128)S(1)} all-reduce(f32[24]{0:T(128)S(1)} %convolution_bitcast_fusion), channel_id=1, replica_groups=mesh['circ'=16,'rad'=6,'mode'=8] {'rad','mode'}, use_global_device_ids=true, to_apply=%region_1.2 | all-reduce | flops 24 | bytes 192 | tf_op jit(solution)/shard_map/psum | solution.py:101
  (207 shorter events, 8.0 us)
Async XLA Ops:
  0.6 159.4 %copy-start = (f32[1,1,1,24,3,512]{5,3,4,2,1,0:T(8,128)S(1)}, f32[1,1,1,24,3,512]{5,3,4,2,1,0:T(8,128)}, u32[]{:S(2)}) copy-start(f32[1,1,1,24,3,512]{5,3,4,2,1,0:T(8,128)} %param.67) | copy-start | bytes 442372
  2.0 61.9 %all-to-all-start = ((s32[1,1,1,8,512]{4,2,1,0,3:T(1,128)}), s32[1,1,1,8,512]{4,2,1,0,3:T(1,128)S(1)}, u32[]{:S(2)}, u32[]{:S(2)}) async-start(s32[1,1,1,8,512]{4,2,1,0,3:T(1,128)} %copy.75), calls=%async_computation | async-start | bytes 32768 | tf_op jit(solution)/shard_map/all_to_all | solution.py:83
  22.9 9.1 %collective-permute-start.1 = (f32[4,1,8,256]{3,2,1,0:T(8,128)S(1)}, f32[4,1,8,256]{3,2,1,0:T(8,128)S(1)}, u32[]{:S(2)}, u32[]{:S(2)}) collective-permute-start(f32[4,1,8,256]{3,2,1,0:T(8,128)S(1)} %get-tuple-element.97), channel_id=1, source_target_pairs={{48,0},{96,48},{144,96},{192,144},{240,192},{288,240},{336,288},{3... | collective-permute-start | bytes 98312 | tf_op jit(solution)/shard_map/ppermute | solution.py:19
  27.8 9.7 %collective-permute-start = (f32[4,1,8,256]{3,2,1,0:T(8,128)S(1)}, f32[4,1,8,256]{3,2,1,0:T(8,128)S(1)}, u32[]{:S(2)}, u32[]{:S(2)}) collective-permute-start(f32[4,1,8,256]{3,2,1,0:T(8,128)S(1)} %get-tuple-element.96), channel_id=1, source_target_pairs={{0,48},{48,96},{96,144},{144,192},{192,240},{240,288},{288,336},{3... | collective-permute-start | bytes 98312 | tf_op jit(solution)/shard_map/ppermute | solution.py:17
  32.0 42.1 %copy-start.40 = (f32[258]{0:T(512)}, f32[258]{0:T(512)S(1)}, u32[]{:S(2)}) copy-start(f32[258]{0:T(512)S(1)} %fusion.185) | copy-start | bytes 3100
  38.6 11.3 %collective-permute-start.3 = (f32[4,6,1,256]{3,2,1,0:T(1,128)S(1)}, f32[4,6,1,256]{3,2,1,0:T(1,128)S(1)}, u32[]{:S(2)}, u32[]{:S(2)}) collective-permute-start(f32[4,6,1,256]{3,2,1,0:T(1,128)S(1)} %get-tuple-element.59), channel_id=1, source_target_pairs={{8,0},{16,8},{24,16},{32,24},{40,32},{0,40},{9,1},{17,9},{25,17},{... | collective-permute-start | bytes 73736 | tf_op jit(solution)/shard_map/ppermute | solution.py:19
  47.9 9.1 %collective-permute-start.2 = (f32[4,6,1,256]{3,2,1,0:T(1,128)S(1)}, f32[4,6,1,256]{3,2,1,0:T(1,128)S(1)}, u32[]{:S(2)}, u32[]{:S(2)}) collective-permute-start(f32[4,6,1,256]{3,2,1,0:T(1,128)S(1)} %get-tuple-element.58), channel_id=1, source_target_pairs={{0,8},{8,16},{16,24},{24,32},{32,40},{40,0},{1,9},{9,17},{17,25},{... | collective-permute-start | bytes 73736 | tf_op jit(solution)/shard_map/ppermute | solution.py:17
  49.8 24.3 %copy-start.72 = (f32[10]{0:T(128)}, f32[10]{0:T(128)S(1)}, u32[]{:S(2)}) copy-start(f32[10]{0:T(128)S(1)} %or_select_fusion) | copy-start | bytes 124
  58.0 13.7 %collective-permute-start.5 = (f32[4,6,10,1]{3,2,1,0:T(8,128)S(1)}, f32[4,6,10,1]{3,2,1,0:T(8,128)S(1)}, u32[]{:S(2)}, u32[]{:S(2)}) collective-permute-start(f32[4,6,10,1]{3,2,1,0:T(8,128)S(1)} %get-tuple-element.55), channel_id=1, source_target_pairs={{1,0},{2,1},{3,2},{4,3},{5,4},{6,5},{7,6},{0,7},{9,8},{10,9},{11,1... | collective-permute-start | bytes 2888 | tf_op jit(solution)/shard_map/ppermute | solution.py:19
  60.2 11.5 %collective-permute-start.4 = (f32[4,6,10,1]{3,2,1,0:T(8,128)S(1)}, f32[4,6,10,1]{3,2,1,0:T(8,128)S(1)}, u32[]{:S(2)}, u32[]{:S(2)}) collective-permute-start(f32[4,6,10,1]{3,2,1,0:T(8,128)S(1)} %get-tuple-element.54), channel_id=1, source_target_pairs={{0,1},{1,2},{2,3},{3,4},{4,5},{5,6},{6,7},{7,0},{8,9},{9,10},{10,1... | collective-permute-start | bytes 2888 | tf_op jit(solution)/shard_map/ppermute | solution.py:17
  63.9 20.0 %all-to-all-start.1 = ((f32[1,1,1,8,3,512]{5,4,2,1,0,3:T(4,128)}), f32[1,1,1,8,3,512]{5,4,2,1,0,3:T(4,128)}, u32[]{:S(2)}, u32[]{:S(2)}) async-start(f32[1,1,1,8,3,512]{5,4,2,1,0,3:T(4,128)} %copy_select_fusion), calls=%async_computation.1 | async-start | bytes 131072 | tf_op jit(solution)/shard_map/all_to_all | solution.py:82
  110.1 3.3 %copy-start.6 = (f32[4,8,256]{2,1,0:T(8,128)S(1)}, f32[4,8,256]{2,1,0:T(8,128)}, u32[]{:S(2)}) copy-start(f32[4,8,256]{2,1,0:T(8,128)} %get-tuple-element.88) | copy-start | bytes 98308
  110.1 3.3 %copy-start.7 = (f32[4,8,256]{2,1,0:T(8,128)S(1)}, f32[4,8,256]{2,1,0:T(8,128)}, u32[]{:S(2)}) copy-start(f32[4,8,256]{2,1,0:T(8,128)} %get-tuple-element.89) | copy-start | bytes 98308
  110.1 3.3 %copy-start.8 = (f32[4,8,256]{2,1,0:T(8,128)S(1)}, f32[4,8,256]{2,1,0:T(8,128)}, u32[]{:S(2)}) copy-start(f32[4,8,256]{2,1,0:T(8,128)} %get-tuple-element.90) | copy-start | bytes 98308
  110.2 3.3 %copy-start.9 = (f32[4,8,256]{2,1,0:T(8,128)S(1)}, f32[4,8,256]{2,1,0:T(8,128)}, u32[]{:S(2)}) copy-start(f32[4,8,256]{2,1,0:T(8,128)} %get-tuple-element.91) | copy-start | bytes 98308
  110.2 3.3 %copy-start.10 = (f32[4,8,256]{2,1,0:T(8,128)S(1)}, f32[4,8,256]{2,1,0:T(8,128)}, u32[]{:S(2)}) copy-start(f32[4,8,256]{2,1,0:T(8,128)} %get-tuple-element.92) | copy-start | bytes 98308
  110.2 3.3 %copy-start.11 = (f32[4,8,256]{2,1,0:T(8,128)S(1)}, f32[4,8,256]{2,1,0:T(8,128)}, u32[]{:S(2)}) copy-start(f32[4,8,256]{2,1,0:T(8,128)} %get-tuple-element.93) | copy-start | bytes 98308
  110.2 3.3 %copy-start.12 = (f32[4,8,256]{2,1,0:T(8,128)S(1)}, f32[4,8,256]{2,1,0:T(8,128)}, u32[]{:S(2)}) copy-start(f32[4,8,256]{2,1,0:T(8,128)} %get-tuple-element.94) | copy-start | bytes 98308
  110.2 3.3 %copy-start.13 = (f32[4,8,256]{2,1,0:T(8,128)S(1)}, f32[4,8,256]{2,1,0:T(8,128)}, u32[]{:S(2)}) copy-start(f32[4,8,256]{2,1,0:T(8,128)} %get-tuple-element.95) | copy-start | bytes 98308
  110.2 3.3 %copy-start.14 = (f32[4,8,256]{2,1,0:T(8,128)S(1)}, f32[4,8,256]{2,1,0:T(8,128)}, u32[]{:S(2)}) copy-start(f32[4,8,256]{2,1,0:T(8,128)} %get-tuple-element.108) | copy-start | bytes 98308
  110.2 3.3 %copy-start.15 = (f32[4,8,256]{2,1,0:T(8,128)S(1)}, f32[4,8,256]{2,1,0:T(8,128)}, u32[]{:S(2)}) copy-start(f32[4,8,256]{2,1,0:T(8,128)} %get-tuple-element.109) | copy-start | bytes 98308
  110.2 3.3 %copy-start.16 = (f32[4,8,256]{2,1,0:T(8,128)S(1)}, f32[4,8,256]{2,1,0:T(8,128)}, u32[]{:S(2)}) copy-start(f32[4,8,256]{2,1,0:T(8,128)} %get-tuple-element.122) | copy-start | bytes 98308
  110.2 3.3 %copy-start.17 = (f32[4,8,256]{2,1,0:T(8,128)S(1)}, f32[4,8,256]{2,1,0:T(8,128)}, u32[]{:S(2)}) copy-start(f32[4,8,256]{2,1,0:T(8,128)} %get-tuple-element.123) | copy-start | bytes 98308
  110.2 3.3 %copy-start.18 = (f32[4,8,256]{2,1,0:T(8,128)S(1)}, f32[4,8,256]{2,1,0:T(8,128)}, u32[]{:S(2)}) copy-start(f32[4,8,256]{2,1,0:T(8,128)} %get-tuple-element.110) | copy-start | bytes 98308
  110.3 3.3 %copy-start.19 = (f32[4,8,256]{2,1,0:T(8,128)S(1)}, f32[4,8,256]{2,1,0:T(8,128)}, u32[]{:S(2)}) copy-start(f32[4,8,256]{2,1,0:T(8,128)} %get-tuple-element.111) | copy-start | bytes 98308
  110.3 3.3 %copy-start.20 = (f32[4,8,256]{2,1,0:T(8,128)S(1)}, f32[4,8,256]{2,1,0:T(8,128)}, u32[]{:S(2)}) copy-start(f32[4,8,256]{2,1,0:T(8,128)} %get-tuple-element.112) | copy-start | bytes 98308
  110.3 3.3 %copy-start.21 = (f32[4,8,256]{2,1,0:T(8,128)S(1)}, f32[4,8,256]{2,1,0:T(8,128)}, u32[]{:S(2)}) copy-start(f32[4,8,256]{2,1,0:T(8,128)} %get-tuple-element.113) | copy-start | bytes 98308
  110.3 3.3 %copy-start.22 = (f32[4,8,256]{2,1,0:T(8,128)S(1)}, f32[4,8,256]{2,1,0:T(8,128)}, u32[]{:S(2)}) copy-start(f32[4,8,256]{2,1,0:T(8,128)} %get-tuple-element.114) | copy-start | bytes 98308
  110.3 3.3 %copy-start.23 = (f32[4,8,256]{2,1,0:T(8,128)S(1)}, f32[4,8,256]{2,1,0:T(8,128)}, u32[]{:S(2)}) copy-start(f32[4,8,256]{2,1,0:T(8,128)} %get-tuple-element.115) | copy-start | bytes 98308
  110.3 3.3 %copy-start.24 = (f32[4,8,256]{2,1,0:T(8,128)S(1)}, f32[4,8,256]{2,1,0:T(8,128)}, u32[]{:S(2)}) copy-start(f32[4,8,256]{2,1,0:T(8,128)} %get-tuple-element.124) | copy-start | bytes 98308
  110.3 3.3 %copy-start.25 = (f32[4,8,256]{2,1,0:T(8,128)S(1)}, f32[4,8,256]{2,1,0:T(8,128)}, u32[]{:S(2)}) copy-start(f32[4,8,256]{2,1,0:T(8,128)} %get-tuple-element.125) | copy-start | bytes 98308
  110.3 3.3 %copy-start.26 = (f32[4,8,256]{2,1,0:T(8,128)S(1)}, f32[4,8,256]{2,1,0:T(8,128)}, u32[]{:S(2)}) copy-start(f32[4,8,256]{2,1,0:T(8,128)} %get-tuple-element.126) | copy-start | bytes 98308
  110.3 3.3 %copy-start.27 = (f32[4,8,256]{2,1,0:T(8,128)S(1)}, f32[4,8,256]{2,1,0:T(8,128)}, u32[]{:S(2)}) copy-start(f32[4,8,256]{2,1,0:T(8,128)} %get-tuple-element.127) | copy-start | bytes 98308
  110.3 3.3 %copy-start.28 = (f32[4,8,256]{2,1,0:T(8,128)S(1)}, f32[4,8,256]{2,1,0:T(8,128)}, u32[]{:S(2)}) copy-start(f32[4,8,256]{2,1,0:T(8,128)} %get-tuple-element.128) | copy-start | bytes 98308
  110.4 3.3 %copy-start.29 = (f32[4,8,256]{2,1,0:T(8,128)S(1)}, f32[4,8,256]{2,1,0:T(8,128)}, u32[]{:S(2)}) copy-start(f32[4,8,256]{2,1,0:T(8,128)} %get-tuple-element.129) | copy-start | bytes 98308
  110.4 3.3 %copy-start.30 = (f32[4,8,256]{2,1,0:T(8,128)S(1)}, f32[4,8,256]{2,1,0:T(8,128)}, u32[]{:S(2)}) copy-start(f32[4,8,256]{2,1,0:T(8,128)} %get-tuple-element.130) | copy-start | bytes 98308
  110.4 3.3 %copy-start.31 = (f32[4,8,256]{2,1,0:T(8,128)S(1)}, f32[4,8,256]{2,1,0:T(8,128)}, u32[]{:S(2)}) copy-start(f32[4,8,256]{2,1,0:T(8,128)} %get-tuple-element.131) | copy-start | bytes 98308
  110.4 3.3 %copy-start.32 = (f32[4,8,256]{2,1,0:T(8,128)S(1)}, f32[4,8,256]{2,1,0:T(8,128)}, u32[]{:S(2)}) copy-start(f32[4,8,256]{2,1,0:T(8,128)} %get-tuple-element.116) | copy-start | bytes 98308
  110.4 3.3 %copy-start.33 = (f32[4,8,256]{2,1,0:T(8,128)S(1)}, f32[4,8,256]{2,1,0:T(8,128)}, u32[]{:S(2)}) copy-start(f32[4,8,256]{2,1,0:T(8,128)} %get-tuple-element.117) | copy-start | bytes 98308
  110.4 3.3 %copy-start.34 = (f32[4,8,256]{2,1,0:T(8,128)S(1)}, f32[4,8,256]{2,1,0:T(8,128)}, u32[]{:S(2)}) copy-start(f32[4,8,256]{2,1,0:T(8,128)} %get-tuple-element.118) | copy-start | bytes 98308
  113.4 36.6 %copy-start.41 = (f32[258]{0:T(512)S(1)}, f32[258]{0:T(512)}, u32[]{:S(2)}) copy-start(f32[258]{0:T(512)} %copy-done.40) | copy-start | bytes 3100
  115.8 5.9 %collective-permute-start.7 = (f32[3,1,8,256]{3,2,1,0:T(8,128)S(1)}, f32[3,1,8,256]{3,2,1,0:T(8,128)S(1)}, u32[]{:S(2)}, u32[]{:S(2)}) collective-permute-start(f32[3,1,8,256]{3,2,1,0:T(8,128)S(1)} %get-tuple-element.99), channel_id=1, source_target_pairs={{48,0},{96,48},{144,96},{192,144},{240,192},{288,240},{336,288},{3... | collective-permute-start | bytes 73736 | tf_op jit(solution)/shard_map/ppermute | solution.py:19
  119.0 9.7 %collective-permute-start.6 = (f32[3,1,8,256]{3,2,1,0:T(8,128)S(1)}, f32[3,1,8,256]{3,2,1,0:T(8,128)S(1)}, u32[]{:S(2)}, u32[]{:S(2)}) collective-permute-start(f32[3,1,8,256]{3,2,1,0:T(8,128)S(1)} %get-tuple-element.98), channel_id=1, source_target_pairs={{0,48},{48,96},{96,144},{144,192},{192,240},{240,288},{288,336},{3... | collective-permute-start | bytes 73736 | tf_op jit(solution)/shard_map/ppermute | solution.py:17
  128.8 5.0 %collective-permute-start.9 = (f32[3,6,1,256]{3,2,1,0:T(1,128)S(1)}, f32[3,6,1,256]{3,2,1,0:T(1,128)S(1)}, u32[]{:S(2)}, u32[]{:S(2)}) collective-permute-start(f32[3,6,1,256]{3,2,1,0:T(1,128)S(1)} %get-tuple-element.61), channel_id=1, source_target_pairs={{8,0},{16,8},{24,16},{32,24},{40,32},{0,40},{9,1},{17,9},{25,17},{... | collective-permute-start | bytes 55304 | tf_op jit(solution)/shard_map/ppermute | solution.py:19
  130.7 9.0 %collective-permute-start.8 = (f32[3,6,1,256]{3,2,1,0:T(1,128)S(1)}, f32[3,6,1,256]{3,2,1,0:T(1,128)S(1)}, u32[]{:S(2)}, u32[]{:S(2)}) collective-permute-start(f32[3,6,1,256]{3,2,1,0:T(1,128)S(1)} %get-tuple-element.60), channel_id=1, source_target_pairs={{0,8},{8,16},{16,24},{24,32},{32,40},{40,0},{1,9},{9,17},{17,25},{... | collective-permute-start | bytes 55304 | tf_op jit(solution)/shard_map/ppermute | solution.py:17
  139.9 7.0 %collective-permute-start.11 = (f32[3,6,10,1]{3,2,1,0:T(8,128)S(1)}, f32[3,6,10,1]{3,2,1,0:T(8,128)S(1)}, u32[]{:S(2)}, u32[]{:S(2)}) collective-permute-start(f32[3,6,10,1]{3,2,1,0:T(8,128)S(1)} %get-tuple-element.57), channel_id=1, source_target_pairs={{1,0},{2,1},{3,2},{4,3},{5,4},{6,5},{7,6},{0,7},{9,8},{10,9},{11,1... | collective-permute-start | bytes 2168 | tf_op jit(solution)/shard_map/ppermute | solution.py:19
  142.3 7.7 %collective-permute-start.10 = (f32[3,6,10,1]{3,2,1,0:T(8,128)S(1)}, f32[3,6,10,1]{3,2,1,0:T(8,128)S(1)}, u32[]{:S(2)}, u32[]{:S(2)}) collective-permute-start(f32[3,6,10,1]{3,2,1,0:T(8,128)S(1)} %get-tuple-element.56), channel_id=1, source_target_pairs={{0,1},{1,2},{2,3},{3,4},{4,5},{5,6},{6,7},{7,0},{8,9},{9,10},{10,1... | collective-permute-start | bytes 2168 | tf_op jit(solution)/shard_map/ppermute | solution.py:17
  153.9 136.1 %copy-start.1 = (f32[3,4,8,256]{3,2,1,0:T(8,128)}, f32[3,4,8,256]{3,2,1,0:T(8,128)S(1)}, u32[]{:S(2)}) copy-start(f32[3,4,8,256]{3,2,1,0:T(8,128)S(1)} %divide_add_fusion) | copy-start | bytes 294916
  (39 other events, 76.7 us)
where the time goes:
time: 291 us; the launch traced here: 290 us
  blocking collectives  129 us (44%)
  starting transfers between devices  60 us (21%)
  other arithmetic  54 us (19%)
  waiting for transfers between devices  29.7 us (10%)
  local copies, waits for them, and re-layouts  14.6 us (5%)
    psum x1, blocking collectives, on_device(): summed = lax.psum(partial_force, ('rad', 'mode'))  129 us
    ppermute x6, waiting for transfers between devices, extended(): lax.ppermute(tail, axis, [(i, (i + 1) % count) for i in range(count)])  28.7 us
    scatter-add x1, other arithmetic, on_device(): rhs = jnp.zeros((3, cells), jnp.float32).at[:, flat_nodes].add(flat_values)  24.7 us
    ppermute x6, starting transfers between devices, extended(): lax.ppermute(head, axis, [((i + 1) % count, i) for i in range(count)])  24 us
    ppermute x6, starting transfers between devices, extended(): lax.ppermute(tail, axis, [(i, (i + 1) % count) for i in range(count)])  16.1 us
    all_to_all x1, starting transfers between devices, on_device(): lax.all_to_all(flow_nodes, 'mode', split_axis=3, concat_axis=3, tiled=True)  12.7 us
    mul x39, other arithmetic, relax(): action = action + link[None] * (diff + coupling * direction * along[None])  8.51 us
    all_to_all x1, starting transfers between devices, on_device(): lax.all_to_all(masked, 'mode', split_axis=3, concat_axis=3, tiled=True)  7.22 us
  transfers between devices with their start and end apart: 14, of which 6 were waited for; matrix products, arithmetic and copies ran while one was open for 9% of the time, Pallas kernels for 0%

commit v1 on v0

v1 whole, which is shorter than its diff:
```python
import functools

import jax
import jax.numpy as jnp
from jax import lax
from jax.experimental import pallas as pl
from jax.experimental.pallas import tpu as pltpu
from jax.sharding import PartitionSpec as P

coupling = 0.5
relaxation = 0.6

face_own, face_other = 0.5 * (1.0 + coupling), 0.5
edge_own, edge_other = 0.25 * (1.0 + 0.5 * coupling), 0.25
corner_own = (1.0 + coupling / 3.0) / 6.0
edge_cross = 0.25 * coupling / 2.0
corner_cross = coupling / 18.0
centre_weight = 2 * face_own + 4 * face_other + 8 * edge_own + 4 * edge_other + 8 * corner_own

F32 = jnp.float32
BF16 = jnp.bfloat16
NT = (((1,), (1,)), ((), ()))


def split(x):
    high = x.astype(BF16).astype(F32)
    return high, x - high


def pack_kernel(moduli, count, prev, cls, sens, nodes, send, e_out, values, hits):
    _, blocks, slots = sens.shape
    ncirc, nrad, naxial = cls.shape
    lines = ncirc * nrad
    k = lax.axis_index("mode")
    lane = lax.broadcasted_iota(jnp.int32, (nrad, 128), 1)
    to_low, to_high = [], []
    for c in range(ncirc):
        level = cls[c]
        e = jnp.zeros(level.shape, F32)
        for i in range(moduli.shape[0]):
            e = jnp.where(level == i, moduli[i], e)
        e_out[c] = e
        low = jnp.zeros((nrad, 128), F32)
        high = jnp.zeros((nrad, 128), F32)
        for f in range(4):
            field = prev[f, c] if f < 3 else e
            first = pltpu.roll(field[:, :128], 4 * f + 2, 1)
            last = pltpu.roll(field[:, naxial - 128 :], 4 * f + 2, 1)
            low = jnp.where((lane == 4 * f + 2) | (lane == 4 * f + 3), first, low)
            high = jnp.where((lane == 4 * f) | (lane == 4 * f + 1), last, high)
        to_low.append(low)
        to_high.append(high)

    values[...] = jnp.zeros(values.shape, BF16)
    slot = lax.broadcasted_iota(jnp.int32, (3, slots), 1)
    row = lax.broadcasted_iota(jnp.int32, (16, slots), 0)
    place = lax.broadcasted_iota(jnp.int32, (2 * lines, slots), 0)
    for d in range(blocks):
        vals = jnp.concatenate([sens[i, d : d + 1] for i in range(3)], axis=0)
        vals = jnp.where(slot < count[d], vals, 0.0)
        node = nodes[d : d + 1]
        for q in range(slots // 128):
            cut = slice(128 * q, 128 * (q + 1))
            send[d, 4 * q : 4 * q + 3, :] = vals[:, cut]
            send[d, 4 * q + 3 : 4 * q + 4, :] = node[:, cut].astype(F32)
        high, low = split(vals)
        tile = jnp.zeros((16, slots), F32)
        for i in range(3):
            tile = jnp.where(row == 2 * i, high[i : i + 1], tile)
            tile = jnp.where(row == 8 + 2 * i, low[i : i + 1], tile)
        values[16 * d : 16 * (d + 1), slots * d : slots * (d + 1)] = tile.astype(BF16)
        axial = node % naxial
        line = node // naxial
        key = jnp.where(axial == 0, line, jnp.where(axial == naxial - 1, line + lines, -1))
        hits[:, slots * d : slots * (d + 1)] = jnp.where(key == place, 1.0, 0.0).astype(BF16)

    planes = lax.dot_general(hits[...], values[...], NT, preferred_element_type=F32)
    planes = planes + pltpu.roll(planes, 120, 1)
    wide = lax.broadcasted_iota(jnp.int32, (lines, 128), 1)
    even = (wide == 16) | (wide == 18) | (wide == 20)
    odd = (wide == 17) | (wide == 19) | (wide == 21)
    for d in range(blocks):
        beside = jnp.zeros((lines, 128), F32)
        if d + 1 < blocks:
            moved = pltpu.roll(planes[:lines], (17 - 16 * (d + 1)) % 128, 1)
            beside = jnp.where(odd, moved, beside)
        if d > 0:
            moved = pltpu.roll(planes[lines:], (16 - 16 * (d - 1)) % 128, 1)
            beside = jnp.where(even, moved, beside)
        for c in range(ncirc):
            out = beside[nrad * c : nrad * (c + 1)]
            out = out + jnp.where(k == d + 1, to_low[c], 0.0) + jnp.where(k == d - 1, to_high[c], 0.0)
            send[d, 16 + nrad * c : 16 + nrad * (c + 1), :] = out


def scatter_kernel(got, prev, e, rhs, ends, first, second, left, right):
    blocks = got.shape[0]
    _, ncirc, nrad, naxial = prev.shape
    lines = ncirc * nrad
    row = lax.broadcasted_iota(jnp.int32, (lines, 128), 0)
    cell = lax.broadcasted_iota(jnp.int32, (naxial, 128), 0)
    for d in range(blocks):
        for q in range(4):
            cut = slice(128 * (4 * d + q), 128 * (4 * d + q + 1))
            node = got[d, 4 * q + 3 : 4 * q + 4, :].astype(jnp.int32)
            right[:, cut] = jnp.where(cell == node % naxial, 1.0, 0.0).astype(BF16)
            hit = row == node // naxial
            for i in range(3):
                for j, part in enumerate(split(got[d, 4 * q + i : 4 * q + i + 1, :])):
                    at = lines * (2 * i + j)
                    left[at : at + lines, cut] = jnp.where(hit, part, 0.0).astype(BF16)
    dense = lax.dot_general(left[...], right[...], NT, preferred_element_type=F32)
    for i in range(3):
        total = dense[2 * lines * i : 2 * lines * i + lines] + dense[2 * lines * i + lines : 2 * lines * (i + 1)]
        for c in range(ncirc):
            rhs[i, c] = total[nrad * c : nrad * (c + 1)]
    for c in range(ncirc):
        at = slice(16 + nrad * c, 16 + nrad * (c + 1))
        total = got[0, at, :]
        for d in range(1, blocks):
            total = total + got[d, at, :]
        ends[c] = total
    odd = lax.axis_index("circ") % 2
    for out, at_high in ((first, 1 - odd), (second, odd)):
        base = at_high * (ncirc - 2)
        edge = at_high * (ncirc - 1)
        for t in range(2):
            cut = slice(128 * t, 128 * (t + 1))
            for f in range(4):
                for j in range(2):
                    source = prev[f, base + j] if f < 3 else e[base + j]
                    out[4 * f + 2 * t + j] = source[:, cut]
            for i in range(3):
                out[16 + 2 * i + t] = rhs[i, edge][:, cut]
        for j in range(2):
            out[22 + j] = ends[base + j]


def turn_kernel(prev, e, rhs, ends, got_first, got_second, turned, first, second):
    _, ncirc, nrad, _ = prev.shape
    odd_circ = lax.axis_index("circ") % 2 == 1

    def put(index, c, plane):
        turned[index, pl.ds(c, nrad, stride=8), :] = plane

    for c in range(ncirc):
        for t in range(2):
            cut = slice(128 * t, 128 * (t + 1))
            for f in range(4):
                source = prev[f, c] if f < 3 else e[c]
                put(2 * f + t, c, source[:, cut])
            for i in range(3):
                put(8 + 2 * i + t, c, rhs[i, c][:, cut])
        put(14, c, ends[c])

    def sides(tile):
        a, b = got_first[tile], got_second[tile]
        return jnp.where(odd_circ, a, b), jnp.where(odd_circ, b, a)

    for index in range(8):
        for j in range(2):
            low, high = sides(2 * index + j)
            put(index, 6 + j, low)
            put(index, 4 + j, high)
    for index in range(6):
        low, high = sides(16 + index)
        put(8 + index, 7, low)
        put(8 + index, 4, high)
        put(8 + index, 6, low)
        put(8 + index, 5, high)
    for j in range(2):
        low, high = sides(22 + j)
        put(14, 6 + j, low)
        put(14, 4 + j, high)

    odd = lax.axis_index("rad") % 2
    for out, at_high in ((first, 1 - odd), (second, odd)):
        for index in range(15):
            for j in range(2):
                plane = at_high * (nrad - 2) + j
                at = 2 * index + j
                if 8 <= index < 14:
                    if j:
                        continue
                    plane = at_high * (nrad - 1)
                    at = 16 + index - 8
                elif index == 14:
                    at = 22 + j
                out[at] = turned[index, pl.ds(pl.multiple_of(8 * plane, 8), 8), :]


def sums(x):
    up = pltpu.roll(x, x.shape[1] - 1, 1)
    down = pltpu.roll(x, 1, 1)
    return up + down, up - down


def across(x):
    up = pltpu.roll(x, 7, 0)
    down = pltpu.roll(x, 1, 0)
    return up + down, up - down


def spread(x):
    sn, dn = sums(x)
    sm, dm = across(x)
    smsn, dmsn = across(sn)
    smdn, dmdn = across(dn)
    return sn, dn, sm, dm, smsn, dmsn, smdn, dmdn


def leading_terms(x, s):
    sn, _, sm, _, both = s[0], s[1], s[2], s[3], s[4]
    near = sm + sn
    return face_other * near + edge_other * both, face_own * x + edge_own * near + corner_own * both


def plane_terms(x, own, other, both):
    centre = face_own * own + face_other * other + edge_own * both
    side = face_other * x + edge_own * own + edge_other * other + corner_own * both
    return centre, side


def cross_terms(s):
    _, dn, _, dm, _, dmsn, smdn, dmdn = s
    return edge_cross * dm + corner_cross * dmsn, edge_cross * dn + corner_cross * smdn, dmdn


def vector_terms(v):
    s0, s1, s2 = spread(v[0]), spread(v[1]), spread(v[2])
    p0, q0 = plane_terms(v[0], s0[2], s0[0], s0[4])
    p1, q1 = leading_terms(v[1], s1)
    p2, q2 = plane_terms(v[2], s2[0], s2[2], s2[4])
    rm0, _, w0 = cross_terms(s0)
    rm1, rn1, _ = cross_terms(s1)
    _, rn2, w2 = cross_terms(s2)
    p0 = p0 + edge_cross * w2
    q0 = q0 + corner_cross * w2
    p2 = p2 + edge_cross * w0
    q2 = q2 + corner_cross * w0
    d0, d1, d2 = rm1, rm0 + rn2, rn1
    return (p0, p1, p2), (q0 + d0, q1 + d1, q2 + d2), (q0 - d0, q1 - d1, q2 - d2)


def scalar_terms(e):
    s = spread(e)
    p0, q0 = plane_terms(e, s[2], s[0], s[4])
    p1, q1 = leading_terms(e, s)
    p2, q2 = plane_terms(e, s[0], s[2], s[4])
    rm, rn, w = cross_terms(s)
    return (p0, p1, p2), (q0, q1, q2), rm, rn, w


def stiffness(e, below, here, above):
    diag = [
        centre_weight * e + here[0][i] + below[1][i] + above[1][i] for i in range(3)
    ]
    c01 = above[2] - below[2]
    c12 = above[3] - below[3]
    c02 = edge_cross * here[4] + corner_cross * (above[4] + below[4])
    return diag, c01, c02, c12


def residual(v, e, rhs, stiff, below, here, above, below_e, here_e, above_e):
    (d0, d1, d2), c01, c02, c12 = stiff
    own = (
        d0 * v[0] + c01 * v[1] + c02 * v[2],
        c01 * v[0] + d1 * v[1] + c12 * v[2],
        c02 * v[0] + c12 * v[1] + d2 * v[2],
    )
    out = []
    for i in range(3):
        plain = here[0][i] + above[1][i] + below[2][i]
        scaled = here_e[0][i] + above_e[1][i] + below_e[2][i]
        out.append(rhs[i] - own[i] + e * plain + scaled)
    return out


def sweep_kernel(
    devices, turned, got_first, got_second, shapes, ids, adjoint, force, keep, sums_of
):
    nrad = turned.shape[1] // 8
    ncirc = adjoint.shape[1]
    rad, mode = lax.axis_index("rad"), lax.axis_index("mode")
    odd = rad % 2 == 1

    def from_low(tile):
        return jnp.where(odd, got_first[tile], got_second[tile])

    def from_high(tile):
        return jnp.where(odd, got_second[tile], got_first[tile])

    def tile_at(index, plane):
        if 0 <= plane < nrad:
            return turned[index, 8 * plane : 8 * (plane + 1), :]
        low = plane < 0
        j = plane + 2 if low else plane - nrad
        if index == 14:
            at = 22 + j
        elif index >= 8:
            at = 16 + index - 8
        else:
            at = 2 * index + j
        return from_low(at) if low else from_high(at)

    def field_at(f, plane, ends):
        shift = 4 * f + 2 if f < 4 else 17 + 2 * (f - 4)
        return jnp.concatenate(
            [tile_at(2 * f, plane), tile_at(2 * f + 1, plane), pltpu.roll(ends, 128 - shift, 1)], axis=1
        )

    lane = lax.broadcasted_iota(jnp.int32, (8, 384), 1)
    outside = ((lane == 383) & (mode == 0)) | ((lane == 256) & (mode == lax.axis_size("mode") - 1))
    fields, terms, e_terms, scaled_terms = {}, {}, {}, {}
    middle, stiff, inverse = {}, {}, {}
    for plane in range(-2, nrad + 2):
        ends = tile_at(14, plane)
        v = [field_at(f, plane, ends) for f in range(3)]
        e = field_at(3, plane, ends)
        fields[plane] = (v, e, ends)
        terms[plane] = vector_terms(v)
        scaled_terms[plane] = vector_terms([e * x for x in v])
        e_terms[plane] = scalar_terms(e)
        at = plane - 1
        if at < -1:
            continue
        v, e, ends = fields[at]
        stiff[at] = stiffness(e, e_terms[at - 1], e_terms[at], e_terms[at + 1])
        inverse[at] = [relaxation / x for x in stiff[at][0]]
        rhs = [field_at(4 + i, at, ends) for i in range(3)]
        rest = residual(
            v, e, rhs, stiff[at],
            terms[at - 1], terms[at], terms[at + 1],
            scaled_terms[at - 1], scaled_terms[at], scaled_terms[at + 1],
        )
        drop = outside
        if at == -1:
            drop = drop | (rad == 0)
        if at == nrad:
            drop = drop | (rad == lax.axis_size("rad") - 1)
        middle[at] = [jnp.where(drop, 0.0, v[i] + inverse[at][i] * rest[i]) for i in range(3)]

    terms, scaled_terms = {}, {}
    for plane in range(-1, nrad + 1):
        v, e = middle[plane], fields[plane][1]
        terms[plane] = vector_terms(v)
        scaled_terms[plane] = vector_terms([e * x for x in v])
        at = plane - 1
        if at < 0:
            continue
        v, e = middle[at], fields[at][1]
        rhs = [field_at(4 + i, at, fields[at][2]) for i in range(3)]
        rest = residual(
            v, e, rhs, stiff[at],
            terms[at - 1], terms[at], terms[at + 1],
            scaled_terms[at - 1], scaled_terms[at], scaled_terms[at + 1],
        )
        for i in range(3):
            final = v[i] + inverse[at][i] * rest[i]
            for t in range(2):
                keep[2 * i + t, 8 * at : 8 * (at + 1), :] = final[:, 128 * t : 128 * (t + 1)]

    parts = []
    for i in range(3):
        for c in range(ncirc):
            both = [keep[2 * i + t, pl.ds(c, nrad, stride=8), :] for t in range(2)]
            plane = jnp.concatenate(both, axis=1)
            adjoint[i, c] = plane
            parts.append(plane)
    lines = ncirc * nrad
    flat = jnp.concatenate(parts, axis=0)
    high, low = split(flat)
    table = jnp.concatenate([high, low], axis=0).astype(BF16)
    node = ids[...]
    cell = lax.broadcasted_iota(jnp.int32, (256, node.shape[1]), 0)
    pick = jnp.where(cell == node % 256, 1.0, 0.0).astype(BF16)
    rows = jnp.dot(table, pick, preferred_element_type=F32)
    rows = rows[: 3 * lines] + rows[3 * lines :]
    line = lax.broadcasted_iota(jnp.int32, (lines, node.shape[1]), 0)
    hit = line == node // 256
    picked = [
        jnp.sum(jnp.where(hit, rows[lines * i : lines * (i + 1)], 0.0), axis=0, keepdims=True)
        for i in range(3)
    ]
    weighted = sum(shapes[i] * picked[i] for i in range(3))
    sums_of[...] = jnp.broadcast_to(jnp.sum(weighted, axis=1, keepdims=True), sums_of.shape)
    owned = sums_of.shape[0] // devices
    lane = lax.broadcasted_iota(jnp.int32, (devices, 128), 1)
    out = jnp.zeros((devices, 128), F32)
    for j in range(owned):
        out = jnp.where(lane == j, sums_of[pl.ds(j, devices, stride=owned), :], out)
    for r in range(force.shape[0] // devices):
        force[devices * r : devices * (r + 1), 0, :] = out


def swaps(axis, start, wrap):
    count = lax.axis_size(axis)
    pairs = []
    for i in range(start, count, 2):
        j = (i + 1) % count
        if j > i or wrap:
            pairs += [(i, j), (j, i)]
    return pairs


def call(kernel, outs, scratch=(), smem=0, ins=0):
    spec = [pl.BlockSpec(memory_space=pltpu.SMEM)] * smem + [pl.BlockSpec(memory_space=pltpu.VMEM)] * ins
    return pl.pallas_call(
        kernel,
        out_shape=[jax.ShapeDtypeStruct(o, F32) for o in outs],
        in_specs=spec,
        out_specs=[pl.BlockSpec(memory_space=pltpu.VMEM)] * len(outs),
        scratch_shapes=list(scratch),
        compiler_params=pltpu.CompilerParams(vmem_limit_bytes=48 * 1024 * 1024),
    )


def on_device(
    adjoint_prev, cell_class, class_moduli, flow_sens, flow_nodes, flow_count, surf_ids, mode_shapes
):
    _, ncirc, nrad, naxial = adjoint_prev.shape
    n_mode, n_rad = lax.axis_size("mode"), lax.axis_size("rad")
    slots = flow_nodes.shape[-1]
    lines = ncirc * nrad
    cells = (ncirc, nrad, naxial)
    message = (24, 8, 128)
    send, e = call(
        pack_kernel,
        [(n_mode, 48, 128), cells],
        [pltpu.VMEM((128, n_mode * slots), BF16), pltpu.VMEM((2 * lines, n_mode * slots), BF16)],
        2, 4,
    )(class_moduli, flow_count[0, 0, 0], adjoint_prev, cell_class, jnp.swapaxes(flow_sens[0, 0, 0], 0, 1), flow_nodes[0, 0, 0])
    got = lax.all_to_all(send, "mode", split_axis=0, concat_axis=0, tiled=True)
    rhs, ends, first, second = call(
        scatter_kernel,
        [(3,) + cells, (ncirc, nrad, 128), message, message],
        [pltpu.VMEM((6 * lines, n_mode * slots), BF16), pltpu.VMEM((naxial, n_mode * slots), BF16)],
        0, 3,
    )(got, adjoint_prev, e)
    first = lax.ppermute(first, "circ", swaps("circ", 0, True))
    second = lax.ppermute(second, "circ", swaps("circ", 1, True))
    turned, first, second = call(turn_kernel, [(15, 8 * nrad, 128), message, message], (), 0, 6)(
        adjoint_prev, e, rhs, ends, first, second
    )
    first = lax.ppermute(first, "rad", swaps("rad", 0, False))
    second = lax.ppermute(second, "rad", swaps("rad", 1, False))
    modes = mode_shapes.shape[3]
    owned = modes // n_mode
    final, force = call(
        functools.partial(sweep_kernel, n_mode),
        [adjoint_prev.shape, (n_rad * n_mode, 1, 128)],
        [pltpu.VMEM((6, 8 * nrad, 128), F32), pltpu.VMEM((modes, 128), F32)],
        0, 5,
    )(turned, first, second, jnp.swapaxes(mode_shapes[0, 0, 0], 0, 1), surf_ids[0, 0])
    parts = lax.all_to_all(force, ("rad", "mode"), split_axis=0, concat_axis=0, tiled=True)
    own_force = jnp.sum(parts[:, 0, :owned], axis=0)
    return (final, own_force.reshape(owned, 1))


def solution(mesh):
    in_specs = (
        P(None, "circ", "rad", "mode"),
        P("circ", "rad", "mode"),
        P(),
        P("circ", "rad", "mode", None, None, None),
        P("circ", "rad", "mode", None, None),
        P("circ", "rad", "mode", None),
        P("circ", "rad", "mode", None),
        P("circ", "rad", "mode", None, None, None),
    )
    out_specs = (P(None, "circ", "rad", "mode"), P("mode", "circ"))
    return jax.shard_map(
        on_device, mesh=mesh, in_specs=in_specs, out_specs=out_specs, check_vma=False
    )
```

time: 291 us -> 84.1 us (0.29)
  the two profiles are of different devices: /device:TPU:8 before, /device:TPU:1 now
where the time goes in v1:
time: 84.1 us; the launch traced here: 83.6 us
  blocking collectives  37.2 us (44%)
  starting transfers between devices  27.8 us (33%)
  waiting for transfers between devices  6.56 us (8%)
  Pallas kernels  6.15 us (7%)
  local copies, waits for them, and re-layouts  4.51 us (5%)
    all_to_all x1, blocking collectives, on_device(): lax.all_to_all(force, ('rad', 'mode'), split_axis=0, concat_axis=0, tiled...  21 us
    all_to_all x1, blocking collectives, on_device(): got = lax.all_to_all(send, 'mode', split_axis=0, concat_axis=0, tiled=True)  16.2 us
    ppermute x1, starting transfers between devices, on_device(): second = lax.ppermute(second, 'rad', swaps('rad', 1, False))  9.12 us
    ppermute x1, starting transfers between devices, on_device(): second = lax.ppermute(second, 'circ', swaps('circ', 1, True))  7.72 us
    ppermute x1, starting transfers between devices, on_device(): first = lax.ppermute(first, 'rad', swaps('rad', 0, False))  6.79 us
    unnamed x18, local copies, waits for them, and re-layouts  4.51 us
    ppermute x1, waiting for transfers between devices, on_device(): second = lax.ppermute(second, 'rad', swaps('rad', 1, False))  4.36 us
    ppermute x1, starting transfers between devices, on_device(): first = lax.ppermute(first, 'circ', swaps('circ', 0, True))  4.19 us
  transfers between devices with their start and end apart: 4, of which 2 were waited for; matrix products, arithmetic and copies ran while one was open for 0% of the time, Pallas kernels for 0%

profile of v1, /device:TPU:1, one launch (start us, length us, event | category | flops | bytes accessed | tf_op | source)
XLA Modules:
  0.0 83.6 jit_solution(2863986205653189417)
XLA Ops:
  0.6 0.0 copy-start.7
  0.6 0.0 copy-start.8
  0.7 0.6 copy-done.7
  1.3 0.0 copy-done.8
  1.3 0.0 copy-start
  1.3 0.9 %copy-done = f32[3,4,8,256]{3,2,1,0:T(8,128)S(1)} copy-done((f32[3,4,8,256]{3,2,1,0:T(8,128)S(1)}, f32[3,4,8,256]{3,2,1,0:T(8,128)}, u32[]{:S(2)}) %copy-start) | copy-done | bytes 98328
  2.2 0.0 copy-start.3
  2.2 0.8 copy-done.3
  3.0 0.0 copy-start.4
  3.0 0.8 copy-done.4
  3.8 0.0 copy-start.5
  3.8 0.7 copy-done.5
  4.5 1.2 %shard_map.95 = (f32[8,48,128]{2,1,0:T(8,128)S(1)}, f32[4,8,256]{2,1,0:T(8,128)S(1)}) custom-call(f32[8]{0:T(128)S(1)} %copy-done.7, s32[8]{0:T(128)S(1)} %bitcast.14, f32[3,4,8,256]{3,2,1,0:T(8,128)S(1)} %copy-done, s32[4,8,256]{2,1,0:T(8,128)S(1)} %copy-done.4, f32[3,8,512]{2,1,0:T(8,128)S(1)} %bitcast.11, s32[8,512]{1,0:T(8,128)S(1)} %bitcast.12), custom_call_target="tpu_custom_call" | custom-call | tf_op jit(solution)/shard_map/pallas_call | solution.py:427
  5.6 0.0 copy-start.1
  5.6 16.2 %all_to_all.10.got = f32[8,48,128]{2,1,0:T(8,128)S(1)} all-to-all(f32[8,48,128]{2,1,0:T(8,128)S(1)} %get-tuple-element.14), channel_id=1, replica_groups=mesh['circ'=16,'rad'=6,'mode'=8] {'mode'}, dimensions={0} | all-to-all | bytes 393216 | tf_op jit(solution)/shard_map/all_to_all | solution.py:433
  21.9 0.0 copy-done.1
  21.9 1.6 %shard_map.96 = (f32[3,4,8,256]{3,2,1,0:T(8,128)S(1)}, f32[4,8,128]{2,1,0:T(8,128)S(1)}, f32[24,8,128]{2,1,0:T(8,128)S(1)}, f32[24,8,128]{2,1,0:T(8,128)S(1)}) custom-call(f32[8,48,128]{2,1,0:T(8,128)S(1)} %all_to_all.10.got, f32[3,4,8,256]{3,2,1,0:T(8,128)S(1)} %copy-done.1, f32[4,8,256]{2,1,0:T(8,128)S(1)} %get-tuple-element.13.e), custom_call_target="tpu_custom_call" | custom-call | tf_op jit(solution)/shard_map/pallas_call | solution.py:434
  23.5 4.2 %collective-permute-start = (f32[24,8,128]{2,1,0:T(8,128)S(1)}, f32[24,8,128]{2,1,0:T(8,128)S(1)}, u32[]{:S(2)}, u32[]{:S(2)}) collective-permute-start(f32[24,8,128]{2,1,0:T(8,128)S(1)} %get-tuple-element.17), channel_id=1, source_target_pairs={{0,48},{48,0},{96,144},{144,96},{192,240},{240,192},{288,336},{336... | collective-permute-start | bytes 294920 | tf_op jit(solution)/shard_map/ppermute | solution.py:440
  27.7 7.7 %collective-permute-start.1 = (f32[24,8,128]{2,1,0:T(8,128)S(1)}, f32[24,8,128]{2,1,0:T(8,128)S(1)}, u32[]{:S(2)}, u32[]{:S(2)}) collective-permute-start(f32[24,8,128]{2,1,0:T(8,128)S(1)} %get-tuple-element.18), channel_id=1, source_target_pairs={{48,96},{96,48},{144,192},{192,144},{240,288},{288,240},{336,384},... | collective-permute-start | bytes 294920 | tf_op jit(solution)/shard_map/ppermute | solution.py:441
  35.4 0.0 collective-permute-done.got_first
  35.4 2.2 %collective-permute-done.1.got_second = f32[24,8,128]{2,1,0:T(8,128)S(1)} collective-permute-done((f32[24,8,128]{2,1,0:T(8,128)S(1)}, f32[24,8,128]{2,1,0:T(8,128)S(1)}, u32[]{:S(2)}, u32[]{:S(2)}) %collective-permute-start.1) | collective-permute-done | bytes 98336 | tf_op jit(solution)/shard_map/ppermute | solution.py:441
  37.6 0.0 copy-start.2
  37.6 0.1 shard_map.97
  37.7 6.8 %collective-permute-start.2 = (f32[24,8,128]{2,1,0:T(8,128)S(1)}, f32[24,8,128]{2,1,0:T(8,128)S(1)}, u32[]{:S(2)}, u32[]{:S(2)}) collective-permute-start(f32[24,8,128]{2,1,0:T(8,128)S(1)} %get-tuple-element.20), channel_id=1, source_target_pairs={{0,8},{8,0},{16,24},{24,16},{32,40},{40,32},{1,9},{9,1},{17,25},{2... | collective-permute-start | bytes 294920 | tf_op jit(solution)/shard_map/ppermute | solution.py:445
  44.5 9.1 %collective-permute-start.3 = (f32[24,8,128]{2,1,0:T(8,128)S(1)}, f32[24,8,128]{2,1,0:T(8,128)S(1)}, u32[]{:S(2)}, u32[]{:S(2)}) collective-permute-start(f32[24,8,128]{2,1,0:T(8,128)S(1)} %get-tuple-element.21), channel_id=1, source_target_pairs={{8,16},{16,8},{24,32},{32,24},{9,17},{17,9},{25,33},{33,25},{10,18... | collective-permute-start | bytes 294920 | tf_op jit(solution)/shard_map/ppermute | solution.py:446
  53.7 0.0 collective-permute-done.2.got_first
  53.7 4.4 %collective-permute-done.3.got_second = f32[24,8,128]{2,1,0:T(8,128)S(1)} collective-permute-done((f32[24,8,128]{2,1,0:T(8,128)S(1)}, f32[24,8,128]{2,1,0:T(8,128)S(1)}, u32[]{:S(2)}, u32[]{:S(2)}) %collective-permute-start.3) | collective-permute-done | bytes 98336 | tf_op jit(solution)/shard_map/ppermute | solution.py:446
  58.0 0.0 copy-start.6
  58.0 0.0 copy-done.2
  58.0 0.7 copy-done.6
  58.7 3.3 %shard_map.98 = (f32[3,4,8,256]{3,2,1,0:T(8,128)}, f32[48,1,128]{2,1,0:T(1,128)S(1)}) custom-call(f32[15,64,128]{2,1,0:T(8,128)S(1)} %get-tuple-element.19.turned, f32[24,8,128]{2,1,0:T(8,128)S(1)} %collective-permute-done.2.got_first, f32[24,8,128]{2,1,0:T(8,128)S(1)} %collective-permute-done.3.got_second, f32[3,24,512]{2,1,0:T(8,128)S(1)} %bitcast.10, ...), custom_call_target="tpu_custom_call" | custom-call | tf_op jit(solution)/shard_map/pallas_call | solution.py:449
  62.0 21.0 %all_to_all.11 = f32[48,1,128]{2,1,0:T(1,128)S(1)} all-to-all(f32[48,1,128]{2,1,0:T(1,128)S(1)} %get-tuple-element.23), channel_id=1, replica_groups=mesh['circ'=16,'rad'=6,'mode'=8] {'rad','mode'}, dimensions={0} | all-to-all | bytes 49152 | tf_op jit(solution)/shard_map/all_to_all | solution.py:455
  83.0 0.6 slice_reduce_fusion
Async XLA Ops:
  0.6 0.7 copy-start.7
  0.6 0.7 copy-start.8
  1.3 0.9 %copy-start = (f32[3,4,8,256]{3,2,1,0:T(8,128)S(1)}, f32[3,4,8,256]{3,2,1,0:T(8,128)}, u32[]{:S(2)}) copy-start(f32[3,4,8,256]{3,2,1,0:T(8,128)} %prev.5) | copy-start | bytes 294916
  2.2 0.8 copy-start.3
  3.0 0.8 copy-start.4
  3.8 0.7 copy-start.5
  5.6 16.2 %copy-start.1 = (f32[3,4,8,256]{3,2,1,0:T(8,128)S(1)}, f32[3,4,8,256]{3,2,1,0:T(8,128)}, u32[]{:S(2)}) copy-start(f32[3,4,8,256]{3,2,1,0:T(8,128)} %prev.5) | copy-start | bytes 294916
  23.5 11.9 %collective-permute-start = (f32[24,8,128]{2,1,0:T(8,128)S(1)}, f32[24,8,128]{2,1,0:T(8,128)S(1)}, u32[]{:S(2)}, u32[]{:S(2)}) collective-permute-start(f32[24,8,128]{2,1,0:T(8,128)S(1)} %get-tuple-element.17), channel_id=1, source_target_pairs={{0,48},{48,0},{96,144},{144,96},{192,240},{240,192},{288,336},{336... | collective-permute-start | bytes 294920 | tf_op jit(solution)/shard_map/ppermute | solution.py:440
  27.7 9.9 %collective-permute-start.1 = (f32[24,8,128]{2,1,0:T(8,128)S(1)}, f32[24,8,128]{2,1,0:T(8,128)S(1)}, u32[]{:S(2)}, u32[]{:S(2)}) collective-permute-start(f32[24,8,128]{2,1,0:T(8,128)S(1)} %get-tuple-element.18), channel_id=1, source_target_pairs={{48,96},{96,48},{144,192},{192,144},{240,288},{288,240},{336,384},... | collective-permute-start | bytes 294920 | tf_op jit(solution)/shard_map/ppermute | solution.py:441
  37.6 20.4 %copy-start.2 = (f32[1,1,1,24,3,512]{5,3,4,2,1,0:T(8,128)S(1)}, f32[1,1,1,24,3,512]{5,3,4,2,1,0:T(8,128)}, u32[]{:S(2)}) copy-start(f32[1,1,1,24,3,512]{5,3,4,2,1,0:T(8,128)} %param.15) | copy-start | bytes 442372
  37.7 15.9 %collective-permute-start.2 = (f32[24,8,128]{2,1,0:T(8,128)S(1)}, f32[24,8,128]{2,1,0:T(8,128)S(1)}, u32[]{:S(2)}, u32[]{:S(2)}) collective-permute-start(f32[24,8,128]{2,1,0:T(8,128)S(1)} %get-tuple-element.20), channel_id=1, source_target_pairs={{0,8},{8,0},{16,24},{24,16},{32,40},{40,32},{1,9},{9,1},{17,25},{2... | collective-permute-start | bytes 294920 | tf_op jit(solution)/shard_map/ppermute | solution.py:445
  44.5 13.5 %collective-permute-start.3 = (f32[24,8,128]{2,1,0:T(8,128)S(1)}, f32[24,8,128]{2,1,0:T(8,128)S(1)}, u32[]{:S(2)}, u32[]{:S(2)}) collective-permute-start(f32[24,8,128]{2,1,0:T(8,128)S(1)} %get-tuple-element.21), channel_id=1, source_target_pairs={{8,16},{16,8},{24,32},{32,24},{9,17},{17,9},{25,33},{33,25},{10,18... | collective-permute-start | bytes 294920 | tf_op jit(solution)/shard_map/ppermute | solution.py:446
  58.0 0.7 copy-start.6

commit v2 on v1

--- a/solution.py
+++ b/solution.py
@@ -27,7 +27,24 @@
     return high, x - high
 
 
-def pack_kernel(moduli, count, prev, cls, sens, nodes, send, e_out, values, hits):
+def pack_kernel(
+    moduli_in, count_in, prev_in, cls_in, sens_in, nodes_in, send, e_out,
+    values, hits, moduli, count, prev, cls, sens, nodes, sems,
+):
+    copies = [
+        pltpu.make_async_copy(source, target, sems.at[i])
+        for i, (source, target) in enumerate(
+            (
+                (sens_in, sens), (nodes_in, nodes), (prev_in, prev), (cls_in, cls),
+                (count_in, count), (moduli_in, moduli),
+            )
+        )
+    ]
+    for copy in copies:
+        copy.start()
+    values[...] = jnp.zeros(values.shape, BF16)
+    for copy in copies:
+        copy.wait()
     _, blocks, slots = sens.shape
     ncirc, nrad, naxial = cls.shape
     lines = ncirc * nrad
@@ -51,7 +68,6 @@
         to_low.append(low)
         to_high.append(high)
 
-    values[...] = jnp.zeros(values.shape, BF16)
     slot = lax.broadcasted_iota(jnp.int32, (3, slots), 1)
     row = lax.broadcasted_iota(jnp.int32, (16, slots), 0)
     place = lax.broadcasted_iota(jnp.int32, (2 * lines, slots), 0)
@@ -136,7 +152,7 @@
             out[22 + j] = ends[base + j]
 
 
-def turn_kernel(prev, e, rhs, ends, got_first, got_second, turned, first, second):
+def turn_kernel(prev, e, rhs, ends, got_second, got_first, turned, first, second):
     _, ncirc, nrad, _ = prev.shape
     odd_circ = lax.axis_index("circ") % 2 == 1
 
@@ -251,115 +267,200 @@
     return (p0, p1, p2), (q0, q1, q2), rm, rn, w
 
 
-def stiffness(e, below, here, above):
-    diag = [
-        centre_weight * e + here[0][i] + below[1][i] + above[1][i] for i in range(3)
+def moved(v, e):
+    plain, scaled = vector_terms(v), vector_terms([e * x for x in v])
+    return [list(plain[j]) + list(scaled[j]) for j in range(3)]
+
+
+def weighed(e):
+    p, q, rm, rn, w = scalar_terms(e)
+    zero = jnp.zeros_like(w)
+    side = corner_cross * w
+    return [
+        list(p) + [zero, zero, edge_cross * w],
+        list(q) + [rm, rn, side],
+        list(q) + [-rm, -rn, side],
     ]
-    c01 = above[2] - below[2]
-    c12 = above[3] - below[3]
-    c02 = edge_cross * here[4] + corner_cross * (above[4] + below[4])
-    return diag, c01, c02, c12
-
-
-def residual(v, e, rhs, stiff, below, here, above, below_e, here_e, above_e):
-    (d0, d1, d2), c01, c02, c12 = stiff
+
+
+def plus(*parts):
+    return [functools.reduce(lambda a, b: a + b, column) for column in zip(*parts)]
+
+
+def stiffness(e, part):
+    diag = [centre_weight * e + x for x in part[:3]]
+    return diag, [relaxation / x for x in diag], part[3], part[4], part[5]
+
+
+def remainder(v, e, rhs, stiff, part):
+    (d0, d1, d2), _, c01, c12, c02 = stiff
     own = (
         d0 * v[0] + c01 * v[1] + c02 * v[2],
         c01 * v[0] + d1 * v[1] + c12 * v[2],
         c02 * v[0] + c12 * v[1] + d2 * v[2],
     )
-    out = []
+    return [rhs[i] - own[i] + e * part[i] + part[3 + i] for i in range(3)]
+
+
+def relaxed(v, stiff, rest):
+    return [v[i] + stiff[1][i] * rest[i] for i in range(3)]
+
+
+def outside_mask():
+    lane = lax.broadcasted_iota(jnp.int32, (8, 384), 1)
+    mode = lax.axis_index("mode")
+    return ((lane == 383) & (mode == 0)) | ((lane == 256) & (mode == lax.axis_size("mode") - 1))
+
+
+def own_tile(turned, index, plane):
+    return turned[index, 8 * plane : 8 * (plane + 1), :]
+
+
+def field_of(tile, f, ends):
+    shift = 4 * f + 2 if f < 4 else 17 + 2 * (f - 4)
+    return jnp.concatenate([tile(2 * f), tile(2 * f + 1), pltpu.roll(ends, 128 - shift, 1)], axis=1)
+
+
+def cells_of(turned, plane, first, last):
+    tile = lambda index: own_tile(turned, index, plane)
+    ends = tile(14)
+    return [field_of(tile, f, ends) for f in range(first, last)]
+
+
+def put_final(keep, plane, final):
     for i in range(3):
-        plain = here[0][i] + above[1][i] + below[2][i]
-        scaled = here_e[0][i] + above_e[1][i] + below_e[2][i]
-        out.append(rhs[i] - own[i] + e * plain + scaled)
-    return out
+        for t in range(2):
+            keep[2 * i + t, 8 * plane : 8 * (plane + 1), :] = final[i][:, 128 * t : 128 * (t + 1)]
+
+
+BEYOND, EDGE, CARRY, REST, HELD, SCALE, COUNT = 0, 12, 24, 30, 33, 36, 39
+OWN, DOWN, UP = 0, 1, 2
+
+
+def inner_kernel(turned, ids, left, keep, pick, nodes, sem):
+    nrad = turned.shape[1] // 8
+    copy = pltpu.make_async_copy(ids, nodes, sem)
+    copy.start()
+    outside = outside_mask()
+    last = nrad - 1
+    adds, middle, stiff = {}, {}, {}
+
+    def leave(side, at, arrays):
+        for j, x in enumerate(arrays):
+            left[side, at + j] = x
+
+    for plane in range(nrad):
+        v, e = cells_of(turned, plane, 0, 3), cells_of(turned, plane, 3, 4)[0]
+        adds[plane] = [a + b for a, b in zip(moved(v, e), weighed(e))]
+        if plane == 0:
+            leave(0, BEYOND, adds[0][DOWN])
+        if plane == 1:
+            leave(0, EDGE, plus(adds[0][OWN], adds[1][DOWN]))
+        if plane == last:
+            leave(1, EDGE, plus(adds[last][OWN], adds[last - 1][UP]))
+            leave(1, BEYOND, adds[last][UP])
+        at = plane - 1
+        if at < 1:
+            continue
+        v, e = cells_of(turned, at, 0, 3), cells_of(turned, at, 3, 4)[0]
+        part = plus(adds[at - 1][UP], adds[at][OWN], adds[at + 1][DOWN])
+        stiff[at] = stiffness(e, part[6:])
+        rest = remainder(v, e, cells_of(turned, at, 4, 7), stiff[at], part)
+        middle[at] = [jnp.where(outside, 0.0, x) for x in relaxed(v, stiff[at], rest)]
+
+    adds = {}
+    for plane in range(1, last):
+        e = cells_of(turned, plane, 3, 4)[0]
+        adds[plane] = moved(middle[plane], e)
+        if plane == 1:
+            leave(0, CARRY, adds[1][DOWN])
+        if plane == last - 1:
+            leave(1, CARRY, adds[last - 1][UP])
+        for at in (plane - 1, plane):
+            if at < 1 or (at == plane and plane < last - 1):
+                continue
+            beside = []
+            if at - 1 in adds:
+                beside.append(adds[at - 1][UP])
+            if at + 1 in adds:
+                beside.append(adds[at + 1][DOWN])
+            part = plus(adds[at][OWN], *beside)
+            v, e = middle[at], cells_of(turned, at, 3, 4)[0]
+            rest = remainder(v, e, cells_of(turned, at, 4, 7), stiff[at], part)
+            if len(beside) == 2:
+                put_final(keep, at, relaxed(v, stiff[at], rest))
+            else:
+                side = 0 if at == 1 else 1
+                leave(side, REST, rest)
+                leave(side, HELD, v)
+                leave(side, SCALE, stiff[at][1])
+    copy.wait()
+    cell = lax.broadcasted_iota(jnp.int32, pick.shape, 0)
+    pick[...] = jnp.where(cell == nodes[...] % 256, 1.0, 0.0).astype(BF16)
 
 
 def sweep_kernel(
-    devices, turned, got_first, got_second, shapes, ids, adjoint, force, keep, sums_of
+    devices, turned, got_second, got_first, left, kept, pick, ids, shapes_in,
+    adjoint, force, keep, sums_of, shapes, sem,
 ):
+    copy = pltpu.make_async_copy(shapes_in, shapes, sem)
+    copy.start()
     nrad = turned.shape[1] // 8
     ncirc = adjoint.shape[1]
-    rad, mode = lax.axis_index("rad"), lax.axis_index("mode")
+    rad = lax.axis_index("rad")
     odd = rad % 2 == 1
-
-    def from_low(tile):
-        return jnp.where(odd, got_first[tile], got_second[tile])
-
-    def from_high(tile):
-        return jnp.where(odd, got_second[tile], got_first[tile])
-
-    def tile_at(index, plane):
-        if 0 <= plane < nrad:
-            return turned[index, 8 * plane : 8 * (plane + 1), :]
-        low = plane < 0
-        j = plane + 2 if low else plane - nrad
-        if index == 14:
-            at = 22 + j
-        elif index >= 8:
-            at = 16 + index - 8
-        else:
-            at = 2 * index + j
-        return from_low(at) if low else from_high(at)
-
-    def field_at(f, plane, ends):
-        shift = 4 * f + 2 if f < 4 else 17 + 2 * (f - 4)
-        return jnp.concatenate(
-            [tile_at(2 * f, plane), tile_at(2 * f + 1, plane), pltpu.roll(ends, 128 - shift, 1)], axis=1
+    outside = outside_mask()
+
+    def halo(side, j, first, last):
+        def tile(index):
+            if index == 14:
+                at = 22 + j
+            elif index >= 8:
+                at = 16 + index - 8
+            else:
+                at = 2 * index + j
+            a, b = got_first[at], got_second[at]
+            return jnp.where(odd, b, a) if side else jnp.where(odd, a, b)
+
+        ends = tile(14)
+        return [field_of(tile, f, ends) for f in range(first, last)]
+
+    def handed(side, at, count):
+        return [left[side, at + j] for j in range(count)]
+
+    for side in range(2):
+        inward = DOWN if side else UP
+        near, far = (0, 1) if side else (1, 0)
+        edge, next_in = (nrad - 1, nrad - 2) if side else (0, 1)
+        v, e = halo(side, far, 0, 3), halo(side, far, 3, 4)[0]
+        beyond = moved(v, e)[inward] + weighed(e)[inward]
+        v, e = halo(side, near, 0, 3), halo(side, near, 3, 4)[0]
+        here = [a + b for a, b in zip(moved(v, e), weighed(e))]
+        part = plus(handed(side, BEYOND, 12), here[OWN], beyond)
+        stiff = stiffness(e, part[6:])
+        rest = remainder(v, e, halo(side, near, 4, 7), stiff, part)
+        drop = outside | (rad == (lax.axis_size("rad") - 1 if side else 0))
+        beside = moved([jnp.where(drop, 0.0, x) for x in relaxed(v, stiff, rest)], e)
+
+        v, e = cells_of(turned, edge, 0, 3), cells_of(turned, edge, 3, 4)[0]
+        rhs = cells_of(turned, edge, 4, 7)
+        part = plus(handed(side, EDGE, 12), here[inward])
+        stiff = stiffness(e, part[6:])
+        v = [jnp.where(outside, 0.0, x) for x in relaxed(v, stiff, remainder(v, e, rhs, stiff, part))]
+        here = moved(v, e)
+        part = plus(handed(side, CARRY, 6), here[OWN], beside[inward])
+        put_final(keep, edge, relaxed(v, stiff, remainder(v, e, rhs, stiff, part)))
+
+        e = cells_of(turned, next_in, 3, 4)[0]
+        add, rest = here[inward], handed(side, REST, 3)
+        v, scale = handed(side, HELD, 3), handed(side, SCALE, 3)
+        put_final(
+            keep, next_in, [v[i] + scale[i] * (rest[i] + e * add[i] + add[3 + i]) for i in range(3)]
         )
 
-    lane = lax.broadcasted_iota(jnp.int32, (8, 384), 1)
-    outside = ((lane == 383) & (mode == 0)) | ((lane == 256) & (mode == lax.axis_size("mode") - 1))
-    fields, terms, e_terms, scaled_terms = {}, {}, {}, {}
-    middle, stiff, inverse = {}, {}, {}
-    for plane in range(-2, nrad + 2):
-        ends = tile_at(14, plane)
-        v = [field_at(f, plane, ends) for f in range(3)]
-        e = field_at(3, plane, ends)
-        fields[plane] = (v, e, ends)
-        terms[plane] = vector_terms(v)
-        scaled_terms[plane] = vector_terms([e * x for x in v])
-        e_terms[plane] = scalar_terms(e)
-        at = plane - 1
-        if at < -1:
-            continue
-        v, e, ends = fields[at]
-        stiff[at] = stiffness(e, e_terms[at - 1], e_terms[at], e_terms[at + 1])
-        inverse[at] = [relaxation / x for x in stiff[at][0]]
-        rhs = [field_at(4 + i, at, ends) for i in range(3)]
-        rest = residual(
-            v, e, rhs, stiff[at],
-            terms[at - 1], terms[at], terms[at + 1],
-            scaled_terms[at - 1], scaled_terms[at], scaled_terms[at + 1],
-        )
-        drop = outside
-        if at == -1:
-            drop = drop | (rad == 0)
-        if at == nrad:
-            drop = drop | (rad == lax.axis_size("rad") - 1)
-        middle[at] = [jnp.where(drop, 0.0, v[i] + inverse[at][i] * rest[i]) for i in range(3)]
-
-    terms, scaled_terms = {}, {}
-    for plane in range(-1, nrad + 1):
-        v, e = middle[plane], fields[plane][1]
-        terms[plane] = vector_terms(v)
-        scaled_terms[plane] = vector_terms([e * x for x in v])
-        at = plane - 1
-        if at < 0:
-            continue
-        v, e = middle[at], fields[at][1]
-        rhs = [field_at(4 + i, at, fields[at][2]) for i in range(3)]
-        rest = residual(
-            v, e, rhs, stiff[at],
-            terms[at - 1], terms[at], terms[at + 1],
-            scaled_terms[at - 1], scaled_terms[at], scaled_terms[at + 1],
-        )
-        for i in range(3):
-            final = v[i] + inverse[at][i] * rest[i]
-            for t in range(2):
-                keep[2 * i + t, 8 * at : 8 * (at + 1), :] = final[:, 128 * t : 128 * (t + 1)]
-
+    inside = slice(16, 8 * (nrad - 2))
+    for index in range(6):
+        keep[index, inside, :] = kept[index, inside, :]
     parts = []
     for i in range(3):
         for c in range(ncirc):
@@ -372,9 +473,7 @@
     high, low = split(flat)
     table = jnp.concatenate([high, low], axis=0).astype(BF16)
     node = ids[...]
-    cell = lax.broadcasted_iota(jnp.int32, (256, node.shape[1]), 0)
-    pick = jnp.where(cell == node % 256, 1.0, 0.0).astype(BF16)
-    rows = jnp.dot(table, pick, preferred_element_type=F32)
+    rows = jnp.dot(table, pick[...], preferred_element_type=F32)
     rows = rows[: 3 * lines] + rows[3 * lines :]
     line = lax.broadcasted_iota(jnp.int32, (lines, node.shape[1]), 0)
     hit = line == node // 256
@@ -382,6 +481,7 @@
         jnp.sum(jnp.where(hit, rows[lines * i : lines * (i + 1)], 0.0), axis=0, keepdims=True)
         for i in range(3)
     ]
+    copy.wait()
     weighted = sum(shapes[i] * picked[i] for i in range(3))
     sums_of[...] = jnp.broadcast_to(jnp.sum(weighted, axis=1, keepdims=True), sums_of.shape)
     owned = sums_of.shape[0] // devices
@@ -403,15 +503,20 @@
     return pairs
 
 
-def call(kernel, outs, scratch=(), smem=0, ins=0):
-    spec = [pl.BlockSpec(memory_space=pltpu.SMEM)] * smem + [pl.BlockSpec(memory_space=pltpu.VMEM)] * ins
+VMEM = pl.BlockSpec(memory_space=pltpu.VMEM)
+HBM = pl.BlockSpec(memory_space=pltpu.HBM)
+
+
+def call(kernel, ins, outs, scratch=(), flops=1_000_000, limit=40 * 1024 * 1024):
+    outs = [o if isinstance(o, jax.ShapeDtypeStruct) else jax.ShapeDtypeStruct(o, F32) for o in outs]
     return pl.pallas_call(
         kernel,
-        out_shape=[jax.ShapeDtypeStruct(o, F32) for o in outs],
-        in_specs=spec,
-        out_specs=[pl.BlockSpec(memory_space=pltpu.VMEM)] * len(outs),
+        out_shape=outs,
+        in_specs=ins,
+        out_specs=[VMEM] * len(outs),
         scratch_shapes=list(scratch),
-        compiler_params=pltpu.CompilerParams(vmem_limit_bytes=48 * 1024 * 1024),
+        compiler_params=pltpu.CompilerParams(vmem_limit_bytes=limit),
+        cost_estimate=pl.CostEstimate(flops=flops, bytes_accessed=1_000_000, transcendentals=0),
     )
 
 
@@ -424,34 +529,55 @@
     lines = ncirc * nrad
     cells = (ncirc, nrad, naxial)
     message = (24, 8, 128)
+    args = (
+        class_moduli, flow_count[0, 0, 0], adjoint_prev, cell_class,
+        jnp.swapaxes(flow_sens[0, 0, 0], 0, 1), flow_nodes[0, 0, 0],
+    )
     send, e = call(
         pack_kernel,
+        [HBM] * 6,
         [(n_mode, 48, 128), cells],
-        [pltpu.VMEM((128, n_mode * slots), BF16), pltpu.VMEM((2 * lines, n_mode * slots), BF16)],
-        2, 4,
-    )(class_moduli, flow_count[0, 0, 0], adjoint_prev, cell_class, jnp.swapaxes(flow_sens[0, 0, 0], 0, 1), flow_nodes[0, 0, 0])
+        [pltpu.VMEM((128, n_mode * slots), BF16), pltpu.VMEM((2 * lines, n_mode * slots), BF16)]
+        + [pltpu.SMEM(x.shape, x.dtype) for x in args[:2]]
+        + [pltpu.VMEM(x.shape, x.dtype) for x in args[2:]]
+        + [pltpu.SemaphoreType.DMA((6,))],
+        limit=63 * 1024 * 1024 + 512 * 1024,
+    )(*args)
     got = lax.all_to_all(send, "mode", split_axis=0, concat_axis=0, tiled=True)
     rhs, ends, first, second = call(
         scatter_kernel,
+        [VMEM] * 3,
         [(3,) + cells, (ncirc, nrad, 128), message, message],
         [pltpu.VMEM((6 * lines, n_mode * slots), BF16), pltpu.VMEM((naxial, n_mode * slots), BF16)],
-        0, 3,
     )(got, adjoint_prev, e)
+    second = lax.ppermute(second, "circ", swaps("circ", 1, True))
     first = lax.ppermute(first, "circ", swaps("circ", 0, True))
-    second = lax.ppermute(second, "circ", swaps("circ", 1, True))
-    turned, first, second = call(turn_kernel, [(15, 8 * nrad, 128), message, message], (), 0, 6)(
-        adjoint_prev, e, rhs, ends, first, second
+    turned, first, second = call(turn_kernel, [VMEM] * 6, [(15, 8 * nrad, 128), message, message])(
+        adjoint_prev, e, rhs, ends, second, first
     )
+    second = lax.ppermute(second, "rad", swaps("rad", 1, False))
     first = lax.ppermute(first, "rad", swaps("rad", 0, False))
-    second = lax.ppermute(second, "rad", swaps("rad", 1, False))
     modes = mode_shapes.shape[3]
     owned = modes // n_mode
+    ids = surf_ids[0, 0]
+    shapes = jnp.swapaxes(mode_shapes[0, 0, 0], 0, 1)
+    kept = (6, 8 * nrad, 128)
+    left, keep, pick = call(
+        inner_kernel,
+        [VMEM, HBM],
+        [(2, COUNT, 8, 384), kept, jax.ShapeDtypeStruct((naxial, ids.shape[1]), BF16)],
+        [pltpu.VMEM(ids.shape, ids.dtype), pltpu.SemaphoreType.DMA],
+        flops=10_000_000,
+    )(turned, ids)
     final, force = call(
         functools.partial(sweep_kernel, n_mode),
+        [VMEM] * 7 + [HBM],
         [adjoint_prev.shape, (n_rad * n_mode, 1, 128)],
-        [pltpu.VMEM((6, 8 * nrad, 128), F32), pltpu.VMEM((modes, 128), F32)],
-        0, 5,
-    )(turned, first, second, jnp.swapaxes(mode_shapes[0, 0, 0], 0, 1), surf_ids[0, 0])
+        [
+            pltpu.VMEM(kept, F32), pltpu.VMEM((modes, 128), F32),
+            pltpu.VMEM(shapes.shape, F32), pltpu.SemaphoreType.DMA,
+        ],
+    )(turned, second, first, left, keep, pick, ids, shapes)
     parts = lax.all_to_all(force, ("rad", "mode"), split_axis=0, concat_axis=0, tiled=True)
     own_force = jnp.sum(parts[:, 0, :owned], axis=0)
     return (final, own_force.reshape(owned, 1))

time: 84.1 us -> 77.4 us (0.920)
  local copies, waits for them, and re-layouts: 4.51 us -> 0.03 us
  waiting for transfers between devices: 6.56 us -> 3.73 us
  Pallas kernels: 6.15 us -> 7.96 us
  blocking collectives: 37.2 us -> 36.1 us
    ppermute x1, starting transfers between devices: 6.79 us -> 1.92 us  [on_device(): first = lax.ppermute(first, 'rad', swaps('rad', 0, False))]
    ppermute x1, starting transfers between devices: 9.12 us -> 14 us  [on_device(): second = lax.ppermute(second, 'rad', swaps('rad', 1, False))]
    unnamed x18 -> x8, local copies, waits for them, and re-layouts: 4.51 us -> 0.03 us
    ppermute x1, waiting for transfers between devices: 4.36 us -> 0.01 us  [on_device(): second = lax.ppermute(second, 'rad', swaps('rad', 1, False))]
    ppermute x1, waiting for transfers between devices: 0.01 us -> 3.66 us  [on_device(): first = lax.ppermute(first, 'circ', swaps('circ', 0, True))]
    ppermute x1, starting transfers between devices: 7.72 us -> 10 us  [on_device(): second = lax.ppermute(second, 'circ', swaps('circ', 1, True))]
    ppermute x1, starting transfers between devices: 4.19 us -> 1.92 us  [on_device(): first = lax.ppermute(first, 'circ', swaps('circ', 0, True))]
    ppermute x1, waiting for transfers between devices: 2.19 us -> 0.07 us  [on_device(): second = lax.ppermute(second, 'circ', swaps('circ', 1, True))]
  transfers between devices with their start and end apart: 4 -> 4, of which waited for: 2 -> 2; matrix products, arithmetic and copies ran while one was open for 0% -> 0% of each run, Pallas kernels for 0% -> 3%
where the time goes in v2:
time: 77.4 us; the launch traced here: 77 us
  blocking collectives  36.1 us (47%)
  starting transfers between devices  27.8 us (36%)
  Pallas kernels  7.96 us (10%)
  waiting for transfers between devices  3.73 us (5%)
    all_to_all x1, blocking collectives, on_device(): lax.all_to_all(force, ('rad', 'mode'), split_axis=0, concat_axis=0, tiled...  19.7 us
    all_to_all x1, blocking collectives, on_device(): got = lax.all_to_all(send, 'mode', split_axis=0, concat_axis=0, tiled=True)  16.4 us
    ppermute x1, starting transfers between devices, on_device(): second = lax.ppermute(second, 'rad', swaps('rad', 1, False))  14 us
    ppermute x1, starting transfers between devices, on_device(): second = lax.ppermute(second, 'circ', swaps('circ', 1, True))  10 us
    ppermute x1, waiting for transfers between devices, on_device(): first = lax.ppermute(first, 'circ', swaps('circ', 0, True))  3.66 us
    pallas_call x1, Pallas kernels, on_device(): call(pack_kernel, [HBM] * 6, [(n_mode, 48, 128), cells], [pltpu.VMEM((128...  2.3 us
    pallas_call x1, Pallas kernels, on_device(): call(functools.partial(sweep_kernel, n_mode), [VMEM] * 7 + [HBM], [adjoin...  1.97 us
    pallas_call x1, Pallas kernels, on_device(): call(inner_kernel, [VMEM, HBM], [(2, COUNT, 8, 384), kept, jax.ShapeDtype...  1.94 us
  transfers between devices with their start and end apart: 4, of which 2 were waited for; matrix products, arithmetic and copies ran while one was open for 0% of the time, Pallas kernels for 3%

profile of v2, /device:TPU:1, one launch (start us, length us, event | category | flops | bytes accessed | tf_op | source)
XLA Modules:
  0.0 77.0 jit_solution(5855032466948814159)
XLA Ops:
  0.6 2.3 %shard_map.95 = (f32[8,48,128]{2,1,0:T(8,128)}, f32[4,8,256]{2,1,0:T(8,128)}) custom-call(f32[8]{0:T(128)} %moduli_in.1, s32[8]{0:T(128)} %bitcast.15, f32[3,4,8,256]{3,2,1,0:T(8,128)} %prev.3, s32[4,8,256]{2,1,0:T(8,128)} %cls_in.1, f32[3,8,512]{2,1,0:T(8,128)} %bitcast.13, s32[8,512]{1,0:T(8,128)} %bitcast.14), custom_call_target="tpu_custom_call" | custom-call | flops 1000000 | bytes 1000000 | tf_op jit(solution)/shard_map/pallas_call | solution.py:536
  2.9 0.0 copy-start
  3.0 0.0 copy-start.2
  3.0 16.4 %all_to_all.10.got = f32[8,48,128]{2,1,0:T(8,128)S(1)} all-to-all(f32[8,48,128]{2,1,0:T(8,128)} %get-tuple-element.17), channel_id=1, replica_groups=mesh['circ'=16,'rad'=6,'mode'=8] {'mode'}, dimensions={0} | all-to-all | bytes 393216 | tf_op jit(solution)/shard_map/all_to_all | solution.py:546
  19.4 0.0 copy-done
  19.4 0.0 copy-done.2
  19.4 1.6 %shard_map.96 = (f32[3,4,8,256]{3,2,1,0:T(8,128)S(1)}, f32[4,8,128]{2,1,0:T(8,128)S(1)}, f32[24,8,128]{2,1,0:T(8,128)S(1)}, f32[24,8,128]{2,1,0:T(8,128)S(1)}) custom-call(f32[8,48,128]{2,1,0:T(8,128)S(1)} %all_to_all.10.got, f32[3,4,8,256]{3,2,1,0:T(8,128)S(1)} %copy-done, f32[4,8,256]{2,1,0:T(8,128)S(1)} %copy-done.2), custom_call_target="tpu_custom_call" | custom-call | flops 1000000 | bytes 1000000 | tf_op jit(solution)/shard_map/pallas_call | solution.py:547
  21.0 10.0 %collective-permute-start = (f32[24,8,128]{2,1,0:T(8,128)S(1)}, f32[24,8,128]{2,1,0:T(8,128)S(1)}, u32[]{:S(2)}, u32[]{:S(2)}) collective-permute-start(f32[24,8,128]{2,1,0:T(8,128)S(1)} %get-tuple-element.20), channel_id=1, source_target_pairs={{48,96},{96,48},{144,192},{192,144},{240,288},{288,240},{336,384},... | collective-permute-start | bytes 294920 | tf_op jit(solution)/shard_map/ppermute | solution.py:553
  31.0 1.9 %collective-permute-start.1 = (f32[24,8,128]{2,1,0:T(8,128)S(1)}, f32[24,8,128]{2,1,0:T(8,128)S(1)}, u32[]{:S(2)}, u32[]{:S(2)}) collective-permute-start(f32[24,8,128]{2,1,0:T(8,128)S(1)} %get-tuple-element.21), channel_id=1, source_target_pairs={{0,48},{48,0},{96,144},{144,96},{192,240},{240,192},{288,336},{336... | collective-permute-start | bytes 294920 | tf_op jit(solution)/shard_map/ppermute | solution.py:554
  33.0 0.1 collective-permute-done.got_second
  33.0 3.7 %collective-permute-done.1.got_first = f32[24,8,128]{2,1,0:T(8,128)S(1)} collective-permute-done((f32[24,8,128]{2,1,0:T(8,128)S(1)}, f32[24,8,128]{2,1,0:T(8,128)S(1)}, u32[]{:S(2)}, u32[]{:S(2)}) %collective-permute-start.1) | collective-permute-done | bytes 98336 | tf_op jit(solution)/shard_map/ppermute | solution.py:554
  36.7 0.1 shard_map.97
  36.8 14.0 %collective-permute-start.2 = (f32[24,8,128]{2,1,0:T(8,128)S(1)}, f32[24,8,128]{2,1,0:T(8,128)S(1)}, u32[]{:S(2)}, u32[]{:S(2)}) collective-permute-start(f32[24,8,128]{2,1,0:T(8,128)S(1)} %get-tuple-element.23), channel_id=1, source_target_pairs={{8,16},{16,8},{24,32},{32,24},{9,17},{17,9},{25,33},{33,25},{10,18... | collective-permute-start | bytes 294920 | tf_op jit(solution)/shard_map/ppermute | solution.py:558
  50.8 0.0 copy-start.3
  50.8 1.9 %collective-permute-start.3 = (f32[24,8,128]{2,1,0:T(8,128)S(1)}, f32[24,8,128]{2,1,0:T(8,128)S(1)}, u32[]{:S(2)}, u32[]{:S(2)}) collective-permute-start(f32[24,8,128]{2,1,0:T(8,128)S(1)} %get-tuple-element.24), channel_id=1, source_target_pairs={{0,8},{8,0},{16,24},{24,16},{32,40},{40,32},{1,9},{9,1},{17,25},{2... | collective-permute-start | bytes 294920 | tf_op jit(solution)/shard_map/ppermute | solution.py:559
  52.7 0.0 copy-done.3
  52.8 0.0 copy-start.1
  52.8 1.9 %shard_map.98 = (f32[2,39,8,384]{3,2,1,0:T(8,128)S(1)}, f32[6,64,128]{2,1,0:T(8,128)S(1)}, bf16[256,512]{1,0:T(8,128)(2,1)S(1)}) custom-call(f32[15,64,128]{2,1,0:T(8,128)S(1)} %get-tuple-element.22.turned, s32[1,512]{1,0:T(1,128)S(1)} %bitcast.11), custom_call_target="tpu_custom_call" | custom-call | flops 10000000 | bytes 1000000 | tf_op jit(solution)/shard_map/pallas_call | solution.py:565
  54.7 0.0 collective-permute-done.2.got_second
  54.7 0.0 collective-permute-done.3.got_first
  54.7 0.0 copy-done.1
  54.7 2.0 %shard_map.99 = (f32[3,4,8,256]{3,2,1,0:T(8,128)}, f32[48,1,128]{2,1,0:T(1,128)S(1)}) custom-call(f32[15,64,128]{2,1,0:T(8,128)S(1)} %get-tuple-element.22.turned, f32[24,8,128]{2,1,0:T(8,128)S(1)} %collective-permute-done.2.got_second, f32[24,8,128]{2,1,0:T(8,128)S(1)} %collective-permute-done.3.got_first, f32[2,39,8,384]{3,2,1,0:T(8,128)S(1)} %get-tuple-element.25.left, ...), custom_call_target="tpu_custom_call" | custom-call | flops 1000000 | bytes 1000000 | tf_op jit(solution)/shard_map/pallas_call | solution.py:572
  56.7 19.7 %all_to_all.11 = f32[48,1,128]{2,1,0:T(1,128)S(1)} all-to-all(f32[48,1,128]{2,1,0:T(1,128)S(1)} %get-tuple-element.29), channel_id=1, replica_groups=mesh['circ'=16,'rad'=6,'mode'=8] {'rad','mode'}, dimensions={0} | all-to-all | bytes 49152 | tf_op jit(solution)/shard_map/all_to_all | solution.py:581
  76.4 0.6 slice_reduce_fusion
Async XLA Ops:
  2.9 16.4 %copy-start = (f32[3,4,8,256]{3,2,1,0:T(8,128)S(1)}, f32[3,4,8,256]{3,2,1,0:T(8,128)}, u32[]{:S(2)}) copy-start(f32[3,4,8,256]{3,2,1,0:T(8,128)} %prev.3) | copy-start | bytes 294916
  3.0 16.4 %copy-start.2 = (f32[4,8,256]{2,1,0:T(8,128)S(1)}, f32[4,8,256]{2,1,0:T(8,128)}, u32[]{:S(2)}) copy-start(f32[4,8,256]{2,1,0:T(8,128)} %get-tuple-element.16.e) | copy-start | bytes 98308
  21.0 12.0 %collective-permute-start = (f32[24,8,128]{2,1,0:T(8,128)S(1)}, f32[24,8,128]{2,1,0:T(8,128)S(1)}, u32[]{:S(2)}, u32[]{:S(2)}) collective-permute-start(f32[24,8,128]{2,1,0:T(8,128)S(1)} %get-tuple-element.20), channel_id=1, source_target_pairs={{48,96},{96,48},{144,192},{192,144},{240,288},{288,240},{336,384},... | collective-permute-start | bytes 294920 | tf_op jit(solution)/shard_map/ppermute | solution.py:553
  31.0 5.7 %collective-permute-start.1 = (f32[24,8,128]{2,1,0:T(8,128)S(1)}, f32[24,8,128]{2,1,0:T(8,128)S(1)}, u32[]{:S(2)}, u32[]{:S(2)}) collective-permute-start(f32[24,8,128]{2,1,0:T(8,128)S(1)} %get-tuple-element.21), channel_id=1, source_target_pairs={{0,48},{48,0},{96,144},{144,96},{192,240},{240,192},{288,336},{336... | collective-permute-start | bytes 294920 | tf_op jit(solution)/shard_map/ppermute | solution.py:554
  36.8 17.9 %collective-permute-start.2 = (f32[24,8,128]{2,1,0:T(8,128)S(1)}, f32[24,8,128]{2,1,0:T(8,128)S(1)}, u32[]{:S(2)}, u32[]{:S(2)}) collective-permute-start(f32[24,8,128]{2,1,0:T(8,128)S(1)} %get-tuple-element.23), channel_id=1, source_target_pairs={{8,16},{16,8},{24,32},{32,24},{9,17},{17,9},{25,33},{33,25},{10,18... | collective-permute-start | bytes 294920 | tf_op jit(solution)/shard_map/ppermute | solution.py:558
  50.8 1.9 %copy-start.3 = (s32[1,1,1,512]{3,2,1,0:T(1,128)S(1)}, s32[1,1,1,512]{3,2,1,0:T(1,128)}, u32[]{:S(2)}) copy-start(s32[1,1,1,512]{3,2,1,0:T(1,128)} %param.14) | copy-start | bytes 6148
  50.8 3.9 %collective-permute-start.3 = (f32[24,8,128]{2,1,0:T(8,128)S(1)}, f32[24,8,128]{2,1,0:T(8,128)S(1)}, u32[]{:S(2)}, u32[]{:S(2)}) collective-permute-start(f32[24,8,128]{2,1,0:T(8,128)S(1)} %get-tuple-element.24), channel_id=1, source_target_pairs={{0,8},{8,0},{16,24},{24,16},{32,40},{40,32},{1,9},{9,1},{17,25},{2... | collective-permute-start | bytes 294920 | tf_op jit(solution)/shard_map/ppermute | solution.py:559
  52.8 2.0 %copy-start.1 = (f32[1,1,1,24,3,512]{5,3,4,2,1,0:T(8,128)S(1)}, f32[1,1,1,24,3,512]{5,3,4,2,1,0:T(8,128)}, u32[]{:S(2)}) copy-start(f32[1,1,1,24,3,512]{5,3,4,2,1,0:T(8,128)} %param.15) | copy-start | bytes 442372

commit v3 on v2

--- a/solution.py
+++ b/solution.py
@@ -29,7 +29,7 @@
 
 def pack_kernel(
     moduli_in, count_in, prev_in, cls_in, sens_in, nodes_in, send, e_out,
-    values, hits, moduli, count, prev, cls, sens, nodes, sems,
+    moduli, count, prev, cls, sens, nodes, sems,
 ):
     copies = [
         pltpu.make_async_copy(source, target, sems.at[i])
@@ -42,7 +42,6 @@
     ]
     for copy in copies:
         copy.start()
-    values[...] = jnp.zeros(values.shape, BF16)
     for copy in copies:
         copy.wait()
     _, blocks, slots = sens.shape
@@ -50,92 +49,100 @@
     lines = ncirc * nrad
     k = lax.axis_index("mode")
     lane = lax.broadcasted_iota(jnp.int32, (nrad, 128), 1)
-    to_low, to_high = [], []
+    columns = []
     for c in range(ncirc):
         level = cls[c]
         e = jnp.zeros(level.shape, F32)
         for i in range(moduli.shape[0]):
             e = jnp.where(level == i, moduli[i], e)
         e_out[c] = e
-        low = jnp.zeros((nrad, 128), F32)
-        high = jnp.zeros((nrad, 128), F32)
+        ends = jnp.zeros((nrad, 128), F32)
         for f in range(4):
             field = prev[f, c] if f < 3 else e
             first = pltpu.roll(field[:, :128], 4 * f + 2, 1)
             last = pltpu.roll(field[:, naxial - 128 :], 4 * f + 2, 1)
-            low = jnp.where((lane == 4 * f + 2) | (lane == 4 * f + 3), first, low)
-            high = jnp.where((lane == 4 * f) | (lane == 4 * f + 1), last, high)
-        to_low.append(low)
-        to_high.append(high)
-
-    slot = lax.broadcasted_iota(jnp.int32, (3, slots), 1)
-    row = lax.broadcasted_iota(jnp.int32, (16, slots), 0)
-    place = lax.broadcasted_iota(jnp.int32, (2 * lines, slots), 0)
+            ends = jnp.where((lane == 4 * f + 2) | (lane == 4 * f + 3), first, ends)
+            ends = jnp.where((lane == 4 * f) | (lane == 4 * f + 1), last, ends)
+        columns.append(ends)
+    columns.append(jnp.zeros((128 - lines, 128), F32))
+    items = jnp.concatenate(columns, axis=0).T
+    halo = items[:8] + pltpu.roll(items[8:16], 32, 1)
+    tall = lax.broadcasted_iota(jnp.int32, (8, 128), 0)
+    to_high = jnp.where(tall % 4 < 2, halo, 0.0)
+    to_low = halo - to_high
+
+    node = nodes[...]
+    axial, line = node % naxial, node // naxial
+    key = jnp.where(axial == 0, line, jnp.where(axial == naxial - 1, line + lines, -1))
+    key = key.astype(F32).astype(BF16)
+    place = lax.broadcasted_iota(jnp.int32, (2 * lines, slots), 0).astype(F32).astype(BF16)
+    slot = lax.broadcasted_iota(jnp.int32, (1, slots), 1)
+    row = lax.broadcasted_iota(jnp.int32, (16, slots), 0) // 2
+    zero, one = BF16(0.0), BF16(1.0)
+    planes = []
     for d in range(blocks):
-        vals = jnp.concatenate([sens[i, d : d + 1] for i in range(3)], axis=0)
-        vals = jnp.where(slot < count[d], vals, 0.0)
-        node = nodes[d : d + 1]
-        for q in range(slots // 128):
-            cut = slice(128 * q, 128 * (q + 1))
-            send[d, 4 * q : 4 * q + 3, :] = vals[:, cut]
-            send[d, 4 * q + 3 : 4 * q + 4, :] = node[:, cut].astype(F32)
-        high, low = split(vals)
+        live = slot < count[d]
         tile = jnp.zeros((16, slots), F32)
         for i in range(3):
-            tile = jnp.where(row == 2 * i, high[i : i + 1], tile)
-            tile = jnp.where(row == 8 + 2 * i, low[i : i + 1], tile)
-        values[16 * d : 16 * (d + 1), slots * d : slots * (d + 1)] = tile.astype(BF16)
-        axial = node % naxial
-        line = node // naxial
-        key = jnp.where(axial == 0, line, jnp.where(axial == naxial - 1, line + lines, -1))
-        hits[:, slots * d : slots * (d + 1)] = jnp.where(key == place, 1.0, 0.0).astype(BF16)
-
-    planes = lax.dot_general(hits[...], values[...], NT, preferred_element_type=F32)
-    planes = planes + pltpu.roll(planes, 120, 1)
-    wide = lax.broadcasted_iota(jnp.int32, (lines, 128), 1)
-    even = (wide == 16) | (wide == 18) | (wide == 20)
-    odd = (wide == 17) | (wide == 19) | (wide == 21)
+            value = jnp.where(live, sens[i, d : d + 1], 0.0)
+            for q in range(slots // 128):
+                send[d, 4 * (i + 1) + q : 4 * (i + 1) + q + 1, :] = value[:, 128 * q : 128 * (q + 1)]
+            high, low = split(value)
+            tile = jnp.where(row == i, high, jnp.where(row == 4 + i, low, tile))
+        for q in range(slots // 128):
+            send[d, q : q + 1, :] = node[d : d + 1, 128 * q : 128 * (q + 1)].astype(F32)
+        hits = jnp.where(place == jnp.broadcast_to(key[d : d + 1], place.shape), one, zero)
+        plane = lax.dot_general(tile.astype(BF16), hits, NT, preferred_element_type=F32)
+        plane = jnp.concatenate([plane[:8] + plane[8:], jnp.zeros((8, 128 - 2 * lines), F32)], axis=1)
+        planes.append(plane)
+    group = lax.broadcasted_iota(jnp.int32, (8, 128), 1) // lines == 2
+    even, odd = group & (tall % 2 == 0), group & (tall % 2 == 1)
     for d in range(blocks):
-        beside = jnp.zeros((lines, 128), F32)
+        out = jnp.where(k == d + 1, to_low, 0.0) + jnp.where(k == d - 1, to_high, 0.0)
         if d + 1 < blocks:
-            moved = pltpu.roll(planes[:lines], (17 - 16 * (d + 1)) % 128, 1)
-            beside = jnp.where(odd, moved, beside)
+            out = jnp.where(odd, pltpu.roll(planes[d + 1], 2 * lines, 1), out)
         if d > 0:
-            moved = pltpu.roll(planes[lines:], (16 - 16 * (d - 1)) % 128, 1)
-            beside = jnp.where(even, moved, beside)
-        for c in range(ncirc):
-            out = beside[nrad * c : nrad * (c + 1)]
-            out = out + jnp.where(k == d + 1, to_low[c], 0.0) + jnp.where(k == d - 1, to_high[c], 0.0)
-            send[d, 16 + nrad * c : 16 + nrad * (c + 1), :] = out
-
-
-def scatter_kernel(got, prev, e, rhs, ends, first, second, left, right):
+            out = jnp.where(even, pltpu.roll(planes[d - 1], lines, 1), out)
+        send[d, 16:24, :] = out
+
+
+def scatter_kernel(got, prev, e, rhs, ends, first, second):
     blocks = got.shape[0]
     _, ncirc, nrad, naxial = prev.shape
     lines = ncirc * nrad
-    row = lax.broadcasted_iota(jnp.int32, (lines, 128), 0)
-    cell = lax.broadcasted_iota(jnp.int32, (naxial, 128), 0)
+    row = lax.broadcasted_iota(jnp.int32, (lines, 128), 0).astype(F32).astype(BF16)
+    cell = lax.broadcasted_iota(jnp.int32, (128, naxial), 1).astype(F32).astype(BF16)
+    nodes = jnp.concatenate([got[d, :4, :] for d in range(blocks)], axis=0).astype(jnp.int32)
+    line = (nodes // naxial).astype(F32).astype(BF16)
+    tall = jnp.concatenate([nodes % naxial, jnp.zeros((128 - 4 * blocks, 128), jnp.int32)], axis=0)
+    tall = tall.astype(F32).T.astype(BF16)
+    zero, one = BF16(0.0), BF16(1.0)
+    dense = jnp.zeros((6 * lines, naxial), F32)
     for d in range(blocks):
+        left, right = [], []
         for q in range(4):
-            cut = slice(128 * (4 * d + q), 128 * (4 * d + q + 1))
-            node = got[d, 4 * q + 3 : 4 * q + 4, :].astype(jnp.int32)
-            right[:, cut] = jnp.where(cell == node % naxial, 1.0, 0.0).astype(BF16)
-            hit = row == node // naxial
+            g = 4 * d + q
+            at = jnp.broadcast_to(tall[:, g : g + 1], cell.shape)
+            right.append(jnp.where(cell == at, one, zero))
+            hit = row == jnp.broadcast_to(line[g : g + 1], row.shape)
+            column = []
             for i in range(3):
-                for j, part in enumerate(split(got[d, 4 * q + i : 4 * q + i + 1, :])):
-                    at = lines * (2 * i + j)
-                    left[at : at + lines, cut] = jnp.where(hit, part, 0.0).astype(BF16)
-    dense = lax.dot_general(left[...], right[...], NT, preferred_element_type=F32)
+                for part in split(got[d, 4 * (i + 1) + q : 4 * (i + 1) + q + 1, :]):
+                    column.append(jnp.where(hit, jnp.broadcast_to(part.astype(BF16), row.shape), zero))
+            left.append(jnp.concatenate(column, axis=0))
+        left, right = jnp.concatenate(left, axis=1), jnp.concatenate(right, axis=0)
+        dense = dense + jnp.dot(left, right, preferred_element_type=F32)
     for i in range(3):
         total = dense[2 * lines * i : 2 * lines * i + lines] + dense[2 * lines * i + lines : 2 * lines * (i + 1)]
         for c in range(ncirc):
             rhs[i, c] = total[nrad * c : nrad * (c + 1)]
+    total = got[0, 16:24, :]
+    for d in range(1, blocks):
+        total = total + got[d, 16:24, :]
+    groups = [total, pltpu.roll(total, 128 - lines, 1), pltpu.roll(total, 128 - 2 * lines, 1)]
+    columns = jnp.concatenate(groups + [jnp.zeros((104, 128), F32)], axis=0).T
     for c in range(ncirc):
-        at = slice(16 + nrad * c, 16 + nrad * (c + 1))
-        total = got[0, at, :]
-        for d in range(1, blocks):
-            total = total + got[d, at, :]
-        ends[c] = total
+        ends[c] = columns[nrad * c : nrad * (c + 1)]
     odd = lax.axis_index("circ") % 2
     for out, at_high in ((first, 1 - odd), (second, odd)):
         base = at_high * (ncirc - 2)
@@ -152,7 +159,7 @@
             out[22 + j] = ends[base + j]
 
 
-def turn_kernel(prev, e, rhs, ends, got_second, got_first, turned, first, second):
+def turn_kernel(prev, e, rhs, ends, got_first, got_second, turned, first, second):
     _, ncirc, nrad, _ = prev.shape
     odd_circ = lax.axis_index("circ") % 2 == 1
 
@@ -400,13 +407,11 @@
 
 
 def sweep_kernel(
-    devices, turned, got_second, got_first, left, kept, pick, ids, shapes_in,
-    adjoint, force, keep, sums_of, shapes, sem,
+    devices, turned, got_second, got_first, left, kept, pick, ids, shapes,
+    adjoint, force, keep, sums_of, result, sem,
 ):
-    copy = pltpu.make_async_copy(shapes_in, shapes, sem)
-    copy.start()
     nrad = turned.shape[1] // 8
-    ncirc = adjoint.shape[1]
+    ncirc = result.shape[1]
     rad = lax.axis_index("rad")
     odd = rad % 2 == 1
     outside = outside_mask()
@@ -466,8 +471,10 @@
         for c in range(ncirc):
             both = [keep[2 * i + t, pl.ds(c, nrad, stride=8), :] for t in range(2)]
             plane = jnp.concatenate(both, axis=1)
-            adjoint[i, c] = plane
+            result[i, c] = plane
             parts.append(plane)
+    copy = pltpu.make_async_copy(result, adjoint, sem)
+    copy.start()
     lines = ncirc * nrad
     flat = jnp.concatenate(parts, axis=0)
     high, low = split(flat)
@@ -481,7 +488,6 @@
         jnp.sum(jnp.where(hit, rows[lines * i : lines * (i + 1)], 0.0), axis=0, keepdims=True)
         for i in range(3)
     ]
-    copy.wait()
     weighted = sum(shapes[i] * picked[i] for i in range(3))
     sums_of[...] = jnp.broadcast_to(jnp.sum(weighted, axis=1, keepdims=True), sums_of.shape)
     owned = sums_of.shape[0] // devices
@@ -491,6 +497,7 @@
         out = jnp.where(lane == j, sums_of[pl.ds(j, devices, stride=owned), :], out)
     for r in range(force.shape[0] // devices):
         force[devices * r : devices * (r + 1), 0, :] = out
+    copy.wait()
 
 
 def swaps(axis, start, wrap):
@@ -507,13 +514,13 @@
 HBM = pl.BlockSpec(memory_space=pltpu.HBM)
 
 
-def call(kernel, ins, outs, scratch=(), flops=1_000_000, limit=40 * 1024 * 1024):
+def call(kernel, ins, outs, scratch=(), flops=1_000_000, limit=40 * 1024 * 1024, out_specs=None):
     outs = [o if isinstance(o, jax.ShapeDtypeStruct) else jax.ShapeDtypeStruct(o, F32) for o in outs]
     return pl.pallas_call(
         kernel,
         out_shape=outs,
         in_specs=ins,
-        out_specs=[VMEM] * len(outs),
+        out_specs=out_specs or [VMEM] * len(outs),
         scratch_shapes=list(scratch),
         compiler_params=pltpu.CompilerParams(vmem_limit_bytes=limit),
         cost_estimate=pl.CostEstimate(flops=flops, bytes_accessed=1_000_000, transcendentals=0),
@@ -536,9 +543,8 @@
     send, e = call(
         pack_kernel,
         [HBM] * 6,
-        [(n_mode, 48, 128), cells],
-        [pltpu.VMEM((128, n_mode * slots), BF16), pltpu.VMEM((2 * lines, n_mode * slots), BF16)]
-        + [pltpu.SMEM(x.shape, x.dtype) for x in args[:2]]
+        [(n_mode, 24, 128), cells],
+        [pltpu.SMEM(x.shape, x.dtype) for x in args[:2]]
         + [pltpu.VMEM(x.shape, x.dtype) for x in args[2:]]
         + [pltpu.SemaphoreType.DMA((6,))],
         limit=63 * 1024 * 1024 + 512 * 1024,
@@ -548,12 +554,11 @@
         scatter_kernel,
         [VMEM] * 3,
         [(3,) + cells, (ncirc, nrad, 128), message, message],
-        [pltpu.VMEM((6 * lines, n_mode * slots), BF16), pltpu.VMEM((naxial, n_mode * slots), BF16)],
     )(got, adjoint_prev, e)
+    first = lax.ppermute(first, "circ", swaps("circ", 0, True))
     second = lax.ppermute(second, "circ", swaps("circ", 1, True))
-    first = lax.ppermute(first, "circ", swaps("circ", 0, True))
     turned, first, second = call(turn_kernel, [VMEM] * 6, [(15, 8 * nrad, 128), message, message])(
-        adjoint_prev, e, rhs, ends, second, first
+        adjoint_prev, e, rhs, ends, first, second
     )
     second = lax.ppermute(second, "rad", swaps("rad", 1, False))
     first = lax.ppermute(first, "rad", swaps("rad", 0, False))
@@ -571,12 +576,13 @@
     )(turned, ids)
     final, force = call(
         functools.partial(sweep_kernel, n_mode),
-        [VMEM] * 7 + [HBM],
+        [VMEM] * 8,
         [adjoint_prev.shape, (n_rad * n_mode, 1, 128)],
         [
             pltpu.VMEM(kept, F32), pltpu.VMEM((modes, 128), F32),
-            pltpu.VMEM(shapes.shape, F32), pltpu.SemaphoreType.DMA,
+            pltpu.VMEM(adjoint_prev.shape, F32), pltpu.SemaphoreType.DMA,
         ],
+        out_specs=[HBM, VMEM],
     )(turned, second, first, left, keep, pick, ids, shapes)
     parts = lax.all_to_all(force, ("rad", "mode"), split_axis=0, concat_axis=0, tiled=True)
     own_force = jnp.sum(parts[:, 0, :owned], axis=0)

time: 77.4 us -> 73.5 us (0.950)
  Pallas kernels: 7.96 us -> 6.68 us
  starting transfers between devices: 27.8 us -> 26.6 us
  waiting for transfers between devices: 3.73 us -> 2.78 us
    ppermute x1, waiting for transfers between devices: 3.66 us -> 0.01 us  [on_device(): first = lax.ppermute(first, 'circ', swaps('circ', 0, True))]
    ppermute x1, waiting for transfers between devices: 0.07 us -> 2.71 us  [on_device(): second = lax.ppermute(second, 'circ', swaps('circ', 1, True))]
    ppermute x1, starting transfers between devices: 10 us -> 7.73 us  [on_device(): second = lax.ppermute(second, 'circ', swaps('circ', 1, True))]
    ppermute x1, starting transfers between devices: 1.92 us -> 4.04 us  [on_device(): first = lax.ppermute(first, 'circ', swaps('circ', 0, True))]
    ppermute x1, starting transfers between devices: 14 us -> 12.9 us  [on_device(): second = lax.ppermute(second, 'rad', swaps('rad', 1, False))]
    all_to_all x1, blocking collectives: 16.4 us -> 15.4 us  [on_device(): got = lax.all_to_all(send, 'mode', split_axis=0, concat_axis=0, tiled=True)]
    pallas_call x1, Pallas kernels: 1.62 us -> 0.79 us  [on_device(): call(scatter_kernel, [VMEM] * 3, [(3,) + cells, (ncirc, nrad, 128), messa...]
where the time goes in v3:
time: 73.5 us; the launch traced here: 72.9 us
  blocking collectives  35.5 us (48%)
  starting transfers between devices  26.6 us (36%)
  Pallas kernels  6.68 us (9%)
  waiting for transfers between devices  2.78 us (4%)
  between operations  0.75 us (1%)
    all_to_all x1, blocking collectives, on_device(): lax.all_to_all(force, ('rad', 'mode'), split_axis=0, concat_axis=0, tiled...  20.1 us
    all_to_all x1, blocking collectives, on_device(): got = lax.all_to_all(send, 'mode', split_axis=0, concat_axis=0, tiled=True)  15.4 us
    ppermute x1, starting transfers between devices, on_device(): second = lax.ppermute(second, 'rad', swaps('rad', 1, False))  12.9 us
    ppermute x1, starting transfers between devices, on_device(): second = lax.ppermute(second, 'circ', swaps('circ', 1, True))  7.73 us
    ppermute x1, starting transfers between devices, on_device(): first = lax.ppermute(first, 'circ', swaps('circ', 0, True))  4.04 us
    ppermute x1, waiting for transfers between devices, on_device(): second = lax.ppermute(second, 'circ', swaps('circ', 1, True))  2.71 us
    pallas_call x1, Pallas kernels, on_device(): call(pack_kernel, [HBM] * 6, [(n_mode, 24, 128), cells], [pltpu.SMEM(x.sh...  2.06 us
    pallas_call x1, Pallas kernels, on_device(): call(inner_kernel, [VMEM, HBM], [(2, COUNT, 8, 384), kept, jax.ShapeDtype...  1.94 us
  transfers between devices with their start and end apart: 4, of which 2 were waited for; matrix products, arithmetic and copies ran while one was open for 0% of the time, Pallas kernels for 3%

profile of v3, /device:TPU:1, one launch (start us, length us, event | category | flops | bytes accessed | tf_op | source)
XLA Modules:
  0.0 72.9 jit_solution(11143275981757372579)
XLA Ops:
  0.6 2.1 %shard_map.95 = (f32[8,24,128]{2,1,0:T(8,128)}, f32[4,8,256]{2,1,0:T(8,128)}) custom-call(f32[8]{0:T(128)} %moduli_in.1, s32[8]{0:T(128)} %bitcast.15, f32[3,4,8,256]{3,2,1,0:T(8,128)} %prev.3, s32[4,8,256]{2,1,0:T(8,128)} %cls_in.1, f32[3,8,512]{2,1,0:T(8,128)} %bitcast.13, s32[8,512]{1,0:T(8,128)} %bitcast.14), custom_call_target="tpu_custom_call" | custom-call | flops 1000000 | bytes 1000000 | tf_op jit(solution)/shard_map/pallas_call | solution.py:543
  2.7 0.0 copy-start
  2.7 0.0 copy-start.2
  2.7 15.4 %all_to_all.10.got = f32[8,24,128]{2,1,0:T(8,128)S(1)} all-to-all(f32[8,24,128]{2,1,0:T(8,128)} %get-tuple-element.17), channel_id=1, replica_groups=mesh['circ'=16,'rad'=6,'mode'=8] {'mode'}, dimensions={0} | all-to-all | bytes 196608 | tf_op jit(solution)/shard_map/all_to_all | solution.py:552
  18.1 0.0 copy-done
  18.1 0.0 copy-done.2
  18.1 0.8 %shard_map.96 = (f32[3,4,8,256]{3,2,1,0:T(8,128)S(1)}, f32[4,8,128]{2,1,0:T(8,128)S(1)}, f32[24,8,128]{2,1,0:T(8,128)S(1)}, f32[24,8,128]{2,1,0:T(8,128)S(1)}) custom-call(f32[8,24,128]{2,1,0:T(8,128)S(1)} %all_to_all.10.got, f32[3,4,8,256]{3,2,1,0:T(8,128)S(1)} %copy-done, f32[4,8,256]{2,1,0:T(8,128)S(1)} %copy-done.2), custom_call_target="tpu_custom_call" | custom-call | flops 1000000 | bytes 1000000 | tf_op jit(solution)/shard_map/pallas_call | solution.py:553
  18.9 4.0 %collective-permute-start = (f32[24,8,128]{2,1,0:T(8,128)S(1)}, f32[24,8,128]{2,1,0:T(8,128)S(1)}, u32[]{:S(2)}, u32[]{:S(2)}) collective-permute-start(f32[24,8,128]{2,1,0:T(8,128)S(1)} %get-tuple-element.20), channel_id=1, source_target_pairs={{0,48},{48,0},{96,144},{144,96},{192,240},{240,192},{288,336},{336... | collective-permute-start | bytes 294920 | tf_op jit(solution)/shard_map/ppermute | solution.py:558
  22.9 7.7 %collective-permute-start.1 = (f32[24,8,128]{2,1,0:T(8,128)S(1)}, f32[24,8,128]{2,1,0:T(8,128)S(1)}, u32[]{:S(2)}, u32[]{:S(2)}) collective-permute-start(f32[24,8,128]{2,1,0:T(8,128)S(1)} %get-tuple-element.21), channel_id=1, source_target_pairs={{48,96},{96,48},{144,192},{192,144},{240,288},{288,240},{336,384},... | collective-permute-start | bytes 294920 | tf_op jit(solution)/shard_map/ppermute | solution.py:559
  30.7 0.0 collective-permute-done.got_first
  30.7 2.7 %collective-permute-done.1.got_second = f32[24,8,128]{2,1,0:T(8,128)S(1)} collective-permute-done((f32[24,8,128]{2,1,0:T(8,128)S(1)}, f32[24,8,128]{2,1,0:T(8,128)S(1)}, u32[]{:S(2)}, u32[]{:S(2)}) %collective-permute-start.1) | collective-permute-done | bytes 98336 | tf_op jit(solution)/shard_map/ppermute | solution.py:559
  33.4 0.1 shard_map.97
  33.5 12.9 %collective-permute-start.2 = (f32[24,8,128]{2,1,0:T(8,128)S(1)}, f32[24,8,128]{2,1,0:T(8,128)S(1)}, u32[]{:S(2)}, u32[]{:S(2)}) collective-permute-start(f32[24,8,128]{2,1,0:T(8,128)S(1)} %get-tuple-element.23), channel_id=1, source_target_pairs={{8,16},{16,8},{24,32},{32,24},{9,17},{17,9},{25,33},{33,25},{10,18... | collective-permute-start | bytes 294920 | tf_op jit(solution)/shard_map/ppermute | solution.py:563
  46.4 0.0 copy-start.3
  46.5 1.9 %collective-permute-start.3 = (f32[24,8,128]{2,1,0:T(8,128)S(1)}, f32[24,8,128]{2,1,0:T(8,128)S(1)}, u32[]{:S(2)}, u32[]{:S(2)}) collective-permute-start(f32[24,8,128]{2,1,0:T(8,128)S(1)} %get-tuple-element.24), channel_id=1, source_target_pairs={{0,8},{8,0},{16,24},{24,16},{32,40},{40,32},{1,9},{9,1},{17,25},{2... | collective-permute-start | bytes 294920 | tf_op jit(solution)/shard_map/ppermute | solution.py:564
  48.4 0.0 copy-done.3
  48.4 0.0 copy-start.1
  48.4 1.9 %shard_map.98 = (f32[2,39,8,384]{3,2,1,0:T(8,128)S(1)}, f32[6,64,128]{2,1,0:T(8,128)S(1)}, bf16[256,512]{1,0:T(8,128)(2,1)S(1)}) custom-call(f32[15,64,128]{2,1,0:T(8,128)S(1)} %get-tuple-element.22.turned, s32[1,512]{1,0:T(1,128)S(1)} %bitcast.11), custom_call_target="tpu_custom_call" | custom-call | flops 10000000 | bytes 1000000 | tf_op jit(solution)/shard_map/pallas_call | solution.py:570
  50.4 0.1 collective-permute-done.2.got_second
  50.4 0.0 collective-permute-done.3.got_first
  50.4 0.0 copy-done.1
  50.4 1.8 %shard_map.99 = (f32[3,4,8,256]{3,2,1,0:T(8,128)}, f32[48,1,128]{2,1,0:T(1,128)S(1)}) custom-call(f32[15,64,128]{2,1,0:T(8,128)S(1)} %get-tuple-element.22.turned, f32[24,8,128]{2,1,0:T(8,128)S(1)} %collective-permute-done.2.got_second, f32[24,8,128]{2,1,0:T(8,128)S(1)} %collective-permute-done.3.got_first, f32[2,39,8,384]{3,2,1,0:T(8,128)S(1)} %get-tuple-element.25.left, ...), custom_call_target="tpu_custom_call" | custom-call | flops 1000000 | bytes 1000000 | tf_op jit(solution)/shard_map/pallas_call | solution.py:577
  52.2 20.1 %all_to_all.11 = f32[48,1,128]{2,1,0:T(1,128)S(1)} all-to-all(f32[48,1,128]{2,1,0:T(1,128)S(1)} %get-tuple-element.29), channel_id=1, replica_groups=mesh['circ'=16,'rad'=6,'mode'=8] {'rad','mode'}, dimensions={0} | all-to-all | bytes 49152 | tf_op jit(solution)/shard_map/all_to_all | solution.py:587
  72.3 0.6 slice_reduce_fusion
Async XLA Ops:
  2.7 15.4 %copy-start = (f32[3,4,8,256]{3,2,1,0:T(8,128)S(1)}, f32[3,4,8,256]{3,2,1,0:T(8,128)}, u32[]{:S(2)}) copy-start(f32[3,4,8,256]{3,2,1,0:T(8,128)} %prev.3) | copy-start | bytes 294916
  2.7 15.4 %copy-start.2 = (f32[4,8,256]{2,1,0:T(8,128)S(1)}, f32[4,8,256]{2,1,0:T(8,128)}, u32[]{:S(2)}) copy-start(f32[4,8,256]{2,1,0:T(8,128)} %get-tuple-element.16.e) | copy-start | bytes 98308
  18.9 11.8 %collective-permute-start = (f32[24,8,128]{2,1,0:T(8,128)S(1)}, f32[24,8,128]{2,1,0:T(8,128)S(1)}, u32[]{:S(2)}, u32[]{:S(2)}) collective-permute-start(f32[24,8,128]{2,1,0:T(8,128)S(1)} %get-tuple-element.20), channel_id=1, source_target_pairs={{0,48},{48,0},{96,144},{144,96},{192,240},{240,192},{288,336},{336... | collective-permute-start | bytes 294920 | tf_op jit(solution)/shard_map/ppermute | solution.py:558
  22.9 10.5 %collective-permute-start.1 = (f32[24,8,128]{2,1,0:T(8,128)S(1)}, f32[24,8,128]{2,1,0:T(8,128)S(1)}, u32[]{:S(2)}, u32[]{:S(2)}) collective-permute-start(f32[24,8,128]{2,1,0:T(8,128)S(1)} %get-tuple-element.21), channel_id=1, source_target_pairs={{48,96},{96,48},{144,192},{192,144},{240,288},{288,240},{336,384},... | collective-permute-start | bytes 294920 | tf_op jit(solution)/shard_map/ppermute | solution.py:559
  33.5 16.9 %collective-permute-start.2 = (f32[24,8,128]{2,1,0:T(8,128)S(1)}, f32[24,8,128]{2,1,0:T(8,128)S(1)}, u32[]{:S(2)}, u32[]{:S(2)}) collective-permute-start(f32[24,8,128]{2,1,0:T(8,128)S(1)} %get-tuple-element.23), channel_id=1, source_target_pairs={{8,16},{16,8},{24,32},{32,24},{9,17},{17,9},{25,33},{33,25},{10,18... | collective-permute-start | bytes 294920 | tf_op jit(solution)/shard_map/ppermute | solution.py:563
  46.4 1.9 %copy-start.3 = (s32[1,1,1,512]{3,2,1,0:T(1,128)S(1)}, s32[1,1,1,512]{3,2,1,0:T(1,128)}, u32[]{:S(2)}) copy-start(s32[1,1,1,512]{3,2,1,0:T(1,128)} %param.14) | copy-start | bytes 6148
  46.5 4.0 %collective-permute-start.3 = (f32[24,8,128]{2,1,0:T(8,128)S(1)}, f32[24,8,128]{2,1,0:T(8,128)S(1)}, u32[]{:S(2)}, u32[]{:S(2)}) collective-permute-start(f32[24,8,128]{2,1,0:T(8,128)S(1)} %get-tuple-element.24), channel_id=1, source_target_pairs={{0,8},{8,0},{16,24},{24,16},{32,40},{40,32},{1,9},{9,1},{17,25},{2... | collective-permute-start | bytes 294920 | tf_op jit(solution)/shard_map/ppermute | solution.py:564
  48.4 2.0 %copy-start.1 = (f32[1,1,1,24,3,512]{5,3,4,2,1,0:T(8,128)S(1)}, f32[1,1,1,24,3,512]{5,3,4,2,1,0:T(8,128)}, u32[]{:S(2)}) copy-start(f32[1,1,1,24,3,512]{5,3,4,2,1,0:T(8,128)} %param.15) | copy-start | bytes 442372

commit v4 on v3

--- a/solution.py
+++ b/solution.py
@@ -143,10 +143,7 @@
     columns = jnp.concatenate(groups + [jnp.zeros((104, 128), F32)], axis=0).T
     for c in range(ncirc):
         ends[c] = columns[nrad * c : nrad * (c + 1)]
-    odd = lax.axis_index("circ") % 2
-    for out, at_high in ((first, 1 - odd), (second, odd)):
-        base = at_high * (ncirc - 2)
-        edge = at_high * (ncirc - 1)
+    for out, base, edge in ((first, ncirc - 2, ncirc - 1), (second, 0, 0)):
         for t in range(2):
             cut = slice(128 * t, 128 * (t + 1))
             for f in range(4):
@@ -161,8 +158,6 @@
 
 def turn_kernel(prev, e, rhs, ends, got_first, got_second, turned, first, second):
     _, ncirc, nrad, _ = prev.shape
-    odd_circ = lax.axis_index("circ") % 2 == 1
-
     def put(index, c, plane):
         turned[index, pl.ds(c, nrad, stride=8), :] = plane
 
@@ -177,8 +172,7 @@
         put(14, c, ends[c])
 
     def sides(tile):
-        a, b = got_first[tile], got_second[tile]
-        return jnp.where(odd_circ, a, b), jnp.where(odd_circ, b, a)
+        return got_first[tile], got_second[tile]
 
     for index in range(8):
         for j in range(2):
@@ -555,8 +549,9 @@
         [VMEM] * 3,
         [(3,) + cells, (ncirc, nrad, 128), message, message],
     )(got, adjoint_prev, e)
-    first = lax.ppermute(first, "circ", swaps("circ", 0, True))
-    second = lax.ppermute(second, "circ", swaps("circ", 1, True))
+    n_circ = lax.axis_size("circ")
+    first = lax.ppermute(first, "circ", [(i, (i + 1) % n_circ) for i in range(n_circ)])
+    second = lax.ppermute(second, "circ", [((i + 1) % n_circ, i) for i in range(n_circ)])
     turned, first, second = call(turn_kernel, [VMEM] * 6, [(15, 8 * nrad, 128), message, message])(
         adjoint_prev, e, rhs, ends, first, second
     )

time: 73.5 us -> 72.6 us (0.988)
  waiting for transfers between devices: 2.78 us -> 1.62 us
    ppermute x2, waiting for transfers between devices: 2.71 us -> 1.62 us  [the longest x1 1.48 us: on_device(): lax.ppermute(second, 'circ', [((i + 1) % n_circ, i) for i in range(n_circ)])]
where the time goes in v4:
time: 72.6 us; the launch traced here: 71.9 us
  blocking collectives  35.4 us (49%)
  starting transfers between devices  26.8 us (37%)
  Pallas kernels  6.67 us (9%)
  waiting for transfers between devices  1.62 us (2%)
  between operations  0.77 us (1%)
    all_to_all x1, blocking collectives, on_device(): lax.all_to_all(force, ('rad', 'mode'), split_axis=0, concat_axis=0, tiled...  20 us
    all_to_all x1, blocking collectives, on_device(): got = lax.all_to_all(send, 'mode', split_axis=0, concat_axis=0, tiled=True)  15.4 us
    ppermute x1, starting transfers between devices, on_device(): second = lax.ppermute(second, 'rad', swaps('rad', 1, False))  13.2 us
    ppermute x1, starting transfers between devices, on_device(): lax.ppermute(second, 'circ', [((i + 1) % n_circ, i) for i in range(n_circ)])  7.73 us
    ppermute x1, starting transfers between devices, on_device(): lax.ppermute(first, 'circ', [(i, (i + 1) % n_circ) for i in range(n_circ)])  4.04 us
    pallas_call x1, Pallas kernels, on_device(): call(pack_kernel, [HBM] * 6, [(n_mode, 24, 128), cells], [pltpu.SMEM(x.sh...  2.06 us
    pallas_call x1, Pallas kernels, on_device(): call(inner_kernel, [VMEM, HBM], [(2, COUNT, 8, 384), kept, jax.ShapeDtype...  1.94 us
    ppermute x1, starting transfers between devices, on_device(): first = lax.ppermute(first, 'rad', swaps('rad', 0, False))  1.92 us
  transfers between devices with their start and end apart: 4, of which 2 were waited for; matrix products, arithmetic and copies ran while one was open for 0% of the time, Pallas kernels for 3%

profile of v4, /device:TPU:1, one launch (start us, length us, event | category | flops | bytes accessed | tf_op | source)
XLA Modules:
  0.0 71.9 jit_solution(4978217389192922101)
XLA Ops:
  0.6 2.1 %shard_map.95 = (f32[8,24,128]{2,1,0:T(8,128)}, f32[4,8,256]{2,1,0:T(8,128)}) custom-call(f32[8]{0:T(128)} %moduli_in.1, s32[8]{0:T(128)} %bitcast.15, f32[3,4,8,256]{3,2,1,0:T(8,128)} %prev.3, s32[4,8,256]{2,1,0:T(8,128)} %cls_in.1, f32[3,8,512]{2,1,0:T(8,128)} %bitcast.13, s32[8,512]{1,0:T(8,128)} %bitcast.14), custom_call_target="tpu_custom_call" | custom-call | flops 1000000 | bytes 1000000 | tf_op jit(solution)/shard_map/pallas_call | solution.py:537
  2.7 0.0 copy-start
  2.7 0.0 copy-start.2
  2.7 15.4 %all_to_all.10.got = f32[8,24,128]{2,1,0:T(8,128)S(1)} all-to-all(f32[8,24,128]{2,1,0:T(8,128)} %get-tuple-element.17), channel_id=1, replica_groups=mesh['circ'=16,'rad'=6,'mode'=8] {'mode'}, dimensions={0} | all-to-all | bytes 196608 | tf_op jit(solution)/shard_map/all_to_all | solution.py:546
  18.1 0.0 copy-done
  18.1 0.0 copy-done.2
  18.1 0.8 %shard_map.96 = (f32[3,4,8,256]{3,2,1,0:T(8,128)S(1)}, f32[4,8,128]{2,1,0:T(8,128)S(1)}, f32[24,8,128]{2,1,0:T(8,128)S(1)}, f32[24,8,128]{2,1,0:T(8,128)S(1)}) custom-call(f32[8,24,128]{2,1,0:T(8,128)S(1)} %all_to_all.10.got, f32[3,4,8,256]{3,2,1,0:T(8,128)S(1)} %copy-done, f32[4,8,256]{2,1,0:T(8,128)S(1)} %copy-done.2), custom_call_target="tpu_custom_call" | custom-call | flops 1000000 | bytes 1000000 | tf_op jit(solution)/shard_map/pallas_call | solution.py:547
  18.9 4.0 %collective-permute-start = (f32[24,8,128]{2,1,0:T(8,128)S(1)}, f32[24,8,128]{2,1,0:T(8,128)S(1)}, u32[]{:S(2)}, u32[]{:S(2)}) collective-permute-start(f32[24,8,128]{2,1,0:T(8,128)S(1)} %get-tuple-element.20), channel_id=1, source_target_pairs={{0,48},{48,96},{96,144},{144,192},{192,240},{240,288},{288,336},{3... | collective-permute-start | bytes 294920 | tf_op jit(solution)/shard_map/ppermute | solution.py:553
  22.9 7.7 %collective-permute-start.1 = (f32[24,8,128]{2,1,0:T(8,128)S(1)}, f32[24,8,128]{2,1,0:T(8,128)S(1)}, u32[]{:S(2)}, u32[]{:S(2)}) collective-permute-start(f32[24,8,128]{2,1,0:T(8,128)S(1)} %get-tuple-element.21), channel_id=1, source_target_pairs={{48,0},{96,48},{144,96},{192,144},{240,192},{288,240},{336,288},{3... | collective-permute-start | bytes 294920 | tf_op jit(solution)/shard_map/ppermute | solution.py:554
  30.7 0.1 collective-permute-done.got_first
  30.8 1.5 %collective-permute-done.1.got_second = f32[24,8,128]{2,1,0:T(8,128)S(1)} collective-permute-done((f32[24,8,128]{2,1,0:T(8,128)S(1)}, f32[24,8,128]{2,1,0:T(8,128)S(1)}, u32[]{:S(2)}, u32[]{:S(2)}) %collective-permute-start.1) | collective-permute-done | bytes 98336 | tf_op jit(solution)/shard_map/ppermute | solution.py:554
  32.3 0.1 shard_map.97
  32.4 13.2 %collective-permute-start.2 = (f32[24,8,128]{2,1,0:T(8,128)S(1)}, f32[24,8,128]{2,1,0:T(8,128)S(1)}, u32[]{:S(2)}, u32[]{:S(2)}) collective-permute-start(f32[24,8,128]{2,1,0:T(8,128)S(1)} %get-tuple-element.23), channel_id=1, source_target_pairs={{8,16},{16,8},{24,32},{32,24},{9,17},{17,9},{25,33},{33,25},{10,18... | collective-permute-start | bytes 294920 | tf_op jit(solution)/shard_map/ppermute | solution.py:558
  45.6 0.0 copy-start.3
  45.6 1.9 %collective-permute-start.3 = (f32[24,8,128]{2,1,0:T(8,128)S(1)}, f32[24,8,128]{2,1,0:T(8,128)S(1)}, u32[]{:S(2)}, u32[]{:S(2)}) collective-permute-start(f32[24,8,128]{2,1,0:T(8,128)S(1)} %get-tuple-element.24), channel_id=1, source_target_pairs={{0,8},{8,0},{16,24},{24,16},{32,40},{40,32},{1,9},{9,1},{17,25},{2... | collective-permute-start | bytes 294920 | tf_op jit(solution)/shard_map/ppermute | solution.py:559
  47.5 0.0 copy-done.3
  47.5 0.0 copy-start.1
  47.5 1.9 %shard_map.98 = (f32[2,39,8,384]{3,2,1,0:T(8,128)S(1)}, f32[6,64,128]{2,1,0:T(8,128)S(1)}, bf16[256,512]{1,0:T(8,128)(2,1)S(1)}) custom-call(f32[15,64,128]{2,1,0:T(8,128)S(1)} %get-tuple-element.22.turned, s32[1,512]{1,0:T(1,128)S(1)} %bitcast.11), custom_call_target="tpu_custom_call" | custom-call | flops 10000000 | bytes 1000000 | tf_op jit(solution)/shard_map/pallas_call | solution.py:565
  49.5 0.0 collective-permute-done.2.got_second
  49.5 0.0 collective-permute-done.3.got_first
  49.5 0.0 copy-done.1
  49.5 1.8 %shard_map.99 = (f32[3,4,8,256]{3,2,1,0:T(8,128)}, f32[48,1,128]{2,1,0:T(1,128)S(1)}) custom-call(f32[15,64,128]{2,1,0:T(8,128)S(1)} %get-tuple-element.22.turned, f32[24,8,128]{2,1,0:T(8,128)S(1)} %collective-permute-done.2.got_second, f32[24,8,128]{2,1,0:T(8,128)S(1)} %collective-permute-done.3.got_first, f32[2,39,8,384]{3,2,1,0:T(8,128)S(1)} %get-tuple-element.25.left, ...), custom_call_target="tpu_custom_call" | custom-call | flops 1000000 | bytes 1000000 | tf_op jit(solution)/shard_map/pallas_call | solution.py:572
  51.3 20.0 %all_to_all.11 = f32[48,1,128]{2,1,0:T(1,128)S(1)} all-to-all(f32[48,1,128]{2,1,0:T(1,128)S(1)} %get-tuple-element.29), channel_id=1, replica_groups=mesh['circ'=16,'rad'=6,'mode'=8] {'rad','mode'}, dimensions={0} | all-to-all | bytes 49152 | tf_op jit(solution)/shard_map/all_to_all | solution.py:582
  71.3 0.6 slice_reduce_fusion
Async XLA Ops:
  2.7 15.4 %copy-start = (f32[3,4,8,256]{3,2,1,0:T(8,128)S(1)}, f32[3,4,8,256]{3,2,1,0:T(8,128)}, u32[]{:S(2)}) copy-start(f32[3,4,8,256]{3,2,1,0:T(8,128)} %prev.3) | copy-start | bytes 294916
  2.7 15.4 %copy-start.2 = (f32[4,8,256]{2,1,0:T(8,128)S(1)}, f32[4,8,256]{2,1,0:T(8,128)}, u32[]{:S(2)}) copy-start(f32[4,8,256]{2,1,0:T(8,128)} %get-tuple-element.16.e) | copy-start | bytes 98308
  18.9 11.9 %collective-permute-start = (f32[24,8,128]{2,1,0:T(8,128)S(1)}, f32[24,8,128]{2,1,0:T(8,128)S(1)}, u32[]{:S(2)}, u32[]{:S(2)}) collective-permute-start(f32[24,8,128]{2,1,0:T(8,128)S(1)} %get-tuple-element.20), channel_id=1, source_target_pairs={{0,48},{48,96},{96,144},{144,192},{192,240},{240,288},{288,336},{3... | collective-permute-start | bytes 294920 | tf_op jit(solution)/shard_map/ppermute | solution.py:553
  22.9 9.4 %collective-permute-start.1 = (f32[24,8,128]{2,1,0:T(8,128)S(1)}, f32[24,8,128]{2,1,0:T(8,128)S(1)}, u32[]{:S(2)}, u32[]{:S(2)}) collective-permute-start(f32[24,8,128]{2,1,0:T(8,128)S(1)} %get-tuple-element.21), channel_id=1, source_target_pairs={{48,0},{96,48},{144,96},{192,144},{240,192},{288,240},{336,288},{3... | collective-permute-start | bytes 294920 | tf_op jit(solution)/shard_map/ppermute | solution.py:554
  32.4 17.1 %collective-permute-start.2 = (f32[24,8,128]{2,1,0:T(8,128)S(1)}, f32[24,8,128]{2,1,0:T(8,128)S(1)}, u32[]{:S(2)}, u32[]{:S(2)}) collective-permute-start(f32[24,8,128]{2,1,0:T(8,128)S(1)} %get-tuple-element.23), channel_id=1, source_target_pairs={{8,16},{16,8},{24,32},{32,24},{9,17},{17,9},{25,33},{33,25},{10,18... | collective-permute-start | bytes 294920 | tf_op jit(solution)/shard_map/ppermute | solution.py:558
  45.6 1.9 %copy-start.3 = (s32[1,1,1,512]{3,2,1,0:T(1,128)S(1)}, s32[1,1,1,512]{3,2,1,0:T(1,128)}, u32[]{:S(2)}) copy-start(s32[1,1,1,512]{3,2,1,0:T(1,128)} %param.14) | copy-start | bytes 6148
  45.6 3.9 %collective-permute-start.3 = (f32[24,8,128]{2,1,0:T(8,128)S(1)}, f32[24,8,128]{2,1,0:T(8,128)S(1)}, u32[]{:S(2)}, u32[]{:S(2)}) collective-permute-start(f32[24,8,128]{2,1,0:T(8,128)S(1)} %get-tuple-element.24), channel_id=1, source_target_pairs={{0,8},{8,0},{16,24},{24,16},{32,40},{40,32},{1,9},{9,1},{17,25},{2... | collective-permute-start | bytes 294920 | tf_op jit(solution)/shard_map/ppermute | solution.py:559
  47.5 2.0 %copy-start.1 = (f32[1,1,1,24,3,512]{5,3,4,2,1,0:T(8,128)S(1)}, f32[1,1,1,24,3,512]{5,3,4,2,1,0:T(8,128)}, u32[]{:S(2)}) copy-start(f32[1,1,1,24,3,512]{5,3,4,2,1,0:T(8,128)} %param.15) | copy-start | bytes 442372

commit v5 on v4

--- a/solution.py
+++ b/solution.py
@@ -156,7 +156,7 @@
             out[22 + j] = ends[base + j]
 
 
-def turn_kernel(prev, e, rhs, ends, got_first, got_second, turned, first, second):
+def turn_kernel(prev, e, rhs, ends, got_first, got_second, turned, first, second, left, keep):
     _, ncirc, nrad, _ = prev.shape
     def put(index, c, plane):
         turned[index, pl.ds(c, nrad, stride=8), :] = plane
@@ -205,6 +205,10 @@
                     at = 22 + j
                 out[at] = turned[index, pl.ds(pl.multiple_of(8 * plane, 8), 8), :]
 
+    @pl.when(works_ahead())
+    def _():
+        inner_work(turned, left, keep)
+
 
 def sums(x):
     up = pltpu.roll(x, x.shape[1] - 1, 1)
@@ -338,10 +342,12 @@
 OWN, DOWN, UP = 0, 1, 2
 
 
-def inner_kernel(turned, ids, left, keep, pick, nodes, sem):
+def works_ahead():
+    return lax.axis_index("circ") % 4 != 0
+
+
+def inner_work(turned, left, keep):
     nrad = turned.shape[1] // 8
-    copy = pltpu.make_async_copy(ids, nodes, sem)
-    copy.start()
     outside = outside_mask()
     last = nrad - 1
     adds, middle, stiff = {}, {}, {}
@@ -395,17 +401,31 @@
                 leave(side, REST, rest)
                 leave(side, HELD, v)
                 leave(side, SCALE, stiff[at][1])
+
+
+def inner_kernel(turned, left_in, keep_in, ids, left, keep, pick, nodes, sem):
+    copy = pltpu.make_async_copy(ids, nodes, sem)
+    copy.start()
+    ahead = works_ahead()
+
+    @pl.when(ahead)
+    def _():
+        left[...] = left_in[...]
+        keep[...] = keep_in[...]
+
+    @pl.when(jnp.logical_not(ahead))
+    def _():
+        inner_work(turned, left, keep)
+
     copy.wait()
     cell = lax.broadcasted_iota(jnp.int32, pick.shape, 0)
     pick[...] = jnp.where(cell == nodes[...] % 256, 1.0, 0.0).astype(BF16)
 
 
 def sweep_kernel(
-    devices, turned, got_second, got_first, left, kept, pick, ids, shapes,
-    adjoint, force, keep, sums_of, result, sem,
+    turned, got_second, got_first, left, kept, keep
 ):
     nrad = turned.shape[1] // 8
-    ncirc = result.shape[1]
     rad = lax.axis_index("rad")
     odd = rad % 2 == 1
     outside = outside_mask()
@@ -460,17 +480,34 @@
     inside = slice(16, 8 * (nrad - 2))
     for index in range(6):
         keep[index, inside, :] = kept[index, inside, :]
-    parts = []
+
+def plane_of(keep, i, c, nrad):
+    both = [keep[2 * i + t, pl.ds(c, nrad, stride=8), :] for t in range(2)]
+    return jnp.concatenate(both, axis=1)
+
+
+def emit_kernel(keep, adjoint):
+    _, ncirc, nrad, _ = adjoint.shape
     for i in range(3):
         for c in range(ncirc):
-            both = [keep[2 * i + t, pl.ds(c, nrad, stride=8), :] for t in range(2)]
-            plane = jnp.concatenate(both, axis=1)
-            result[i, c] = plane
-            parts.append(plane)
-    copy = pltpu.make_async_copy(result, adjoint, sem)
-    copy.start()
+            adjoint[i, c] = plane_of(keep, i, c, nrad)
+
+
+def finish_kernel(keep, parts, adjoint, own, result, total, sems):
+    emit_kernel(keep, result)
+    first = pltpu.make_async_copy(result, adjoint, sems.at[0])
+    first.start()
+    total[...] = jnp.sum(parts[...], axis=0)[:, : total.shape[1]]
+    second = pltpu.make_async_copy(total, own, sems.at[1])
+    second.start()
+    first.wait()
+    second.wait()
+
+
+def force_kernel(devices, ncirc, keep, pick, ids, shapes, force, sums_of):
+    nrad = keep.shape[1] // 8
     lines = ncirc * nrad
-    flat = jnp.concatenate(parts, axis=0)
+    flat = jnp.concatenate([plane_of(keep, i, c, nrad) for i in range(3) for c in range(ncirc)], axis=0)
     high, low = split(flat)
     table = jnp.concatenate([high, low], axis=0).astype(BF16)
     node = ids[...]
@@ -491,7 +528,6 @@
         out = jnp.where(lane == j, sums_of[pl.ds(j, devices, stride=owned), :], out)
     for r in range(force.shape[0] // devices):
         force[devices * r : devices * (r + 1), 0, :] = out
-    copy.wait()
 
 
 def swaps(axis, start, wrap):
@@ -552,7 +588,11 @@
     n_circ = lax.axis_size("circ")
     first = lax.ppermute(first, "circ", [(i, (i + 1) % n_circ) for i in range(n_circ)])
     second = lax.ppermute(second, "circ", [((i + 1) % n_circ, i) for i in range(n_circ)])
-    turned, first, second = call(turn_kernel, [VMEM] * 6, [(15, 8 * nrad, 128), message, message])(
+    kept = (6, 8 * nrad, 128)
+    left = (2, COUNT, 8, 384)
+    turned, first, second, left, keep = call(
+        turn_kernel, [VMEM] * 6, [(15, 8 * nrad, 128), message, message, left, kept]
+    )(
         adjoint_prev, e, rhs, ends, first, second
     )
     second = lax.ppermute(second, "rad", swaps("rad", 1, False))
@@ -561,26 +601,31 @@
     owned = modes // n_mode
     ids = surf_ids[0, 0]
     shapes = jnp.swapaxes(mode_shapes[0, 0, 0], 0, 1)
-    kept = (6, 8 * nrad, 128)
     left, keep, pick = call(
         inner_kernel,
-        [VMEM, HBM],
-        [(2, COUNT, 8, 384), kept, jax.ShapeDtypeStruct((naxial, ids.shape[1]), BF16)],
+        [VMEM] * 3 + [HBM],
+        [left.shape, kept, jax.ShapeDtypeStruct((naxial, ids.shape[1]), BF16)],
         [pltpu.VMEM(ids.shape, ids.dtype), pltpu.SemaphoreType.DMA],
         flops=10_000_000,
-    )(turned, ids)
-    final, force = call(
-        functools.partial(sweep_kernel, n_mode),
-        [VMEM] * 8,
-        [adjoint_prev.shape, (n_rad * n_mode, 1, 128)],
+    )(turned, left, keep, ids)
+    (keep,) = call(sweep_kernel, [VMEM] * 5, [kept])(turned, second, first, left, keep)
+    (force,) = call(
+        functools.partial(force_kernel, n_mode, ncirc),
+        [VMEM] * 4,
+        [(n_rad * n_mode, 1, 128)],
+        [pltpu.VMEM((modes, 128), F32)],
+    )(keep, pick, ids, shapes)
+    parts = lax.all_to_all(force, ("rad", "mode"), split_axis=0, concat_axis=0, tiled=True)
+    final, own_force = call(
+        finish_kernel,
+        [VMEM] * 2,
+        [adjoint_prev.shape, (1, owned)],
         [
-            pltpu.VMEM(kept, F32), pltpu.VMEM((modes, 128), F32),
-            pltpu.VMEM(adjoint_prev.shape, F32), pltpu.SemaphoreType.DMA,
+            pltpu.VMEM(adjoint_prev.shape, F32), pltpu.VMEM((1, owned), F32),
+            pltpu.SemaphoreType.DMA((2,)),
         ],
-        out_specs=[HBM, VMEM],
-    )(turned, second, first, left, keep, pick, ids, shapes)
-    parts = lax.all_to_all(force, ("rad", "mode"), split_axis=0, concat_axis=0, tiled=True)
-    own_force = jnp.sum(parts[:, 0, :owned], axis=0)
+        out_specs=[HBM, HBM],
+    )(keep, parts)
     return (final, own_force.reshape(owned, 1))
 
 

time: 72.6 us -> 71.6 us (0.986)
  blocking collectives: 35.4 us -> 34.4 us
    all_to_all x1, blocking collectives: 20 us -> 19 us  [on_device(): lax.all_to_all(force, ('rad', 'mode'), split_axis=0, concat_axis=0, tiled...]
    pallas_call x3 -> x5, Pallas kernels: 3.83 us -> 4.08 us  [the longest x1 1.94 us: on_device(): call(inner_kernel, [VMEM] * 3 + [HBM], [left.shape, kept, jax.ShapeDtypeS...]
where the time goes in v5:
time: 71.6 us; the launch traced here: 71.2 us
  blocking collectives  34.4 us (48%)
  starting transfers between devices  26.8 us (37%)
  Pallas kernels  6.92 us (10%)
  waiting for transfers between devices  1.62 us (2%)
  between operations  0.77 us (1%)
    all_to_all x1, blocking collectives, on_device(): lax.all_to_all(force, ('rad', 'mode'), split_axis=0, concat_axis=0, tiled...  19 us
    all_to_all x1, blocking collectives, on_device(): got = lax.all_to_all(send, 'mode', split_axis=0, concat_axis=0, tiled=True)  15.4 us
    ppermute x1, starting transfers between devices, on_device(): second = lax.ppermute(second, 'rad', swaps('rad', 1, False))  13.2 us
    ppermute x1, starting transfers between devices, on_device(): lax.ppermute(second, 'circ', [((i + 1) % n_circ, i) for i in range(n_circ)])  7.73 us
    ppermute x1, starting transfers between devices, on_device(): lax.ppermute(first, 'circ', [(i, (i + 1) % n_circ) for i in range(n_circ)])  4.04 us
    pallas_call x1, Pallas kernels, on_device(): call(pack_kernel, [HBM] * 6, [(n_mode, 24, 128), cells], [pltpu.SMEM(x.sh...  2.06 us
    pallas_call x1, Pallas kernels, on_device(): call(inner_kernel, [VMEM] * 3 + [HBM], [left.shape, kept, jax.ShapeDtypeS...  1.94 us
    ppermute x1, starting transfers between devices, on_device(): first = lax.ppermute(first, 'rad', swaps('rad', 0, False))  1.92 us
  transfers between devices with their start and end apart: 4, of which 2 were waited for; matrix products, arithmetic and copies ran while one was open for 0% of the time, Pallas kernels for 3%

profile of v5, /device:TPU:1, one launch (start us, length us, event | category | flops | bytes accessed | tf_op | source)
XLA Modules:
  0.0 71.2 jit_solution(17075238239472278124)
XLA Ops:
  0.6 2.1 %shard_map.95 = (f32[8,24,128]{2,1,0:T(8,128)}, f32[4,8,256]{2,1,0:T(8,128)}) custom-call(f32[8]{0:T(128)} %moduli_in.1, s32[8]{0:T(128)} %bitcast.15, f32[3,4,8,256]{3,2,1,0:T(8,128)} %prev.3, s32[4,8,256]{2,1,0:T(8,128)} %cls_in.1, f32[3,8,512]{2,1,0:T(8,128)} %bitcast.13, s32[8,512]{1,0:T(8,128)} %bitcast.14), custom_call_target="tpu_custom_call" | custom-call | flops 1000000 | bytes 1000000 | tf_op jit(solution)/shard_map/pallas_call | solution.py:573
  2.7 0.0 copy-start
  2.7 0.0 copy-start.2
  2.7 15.4 %all_to_all.10.got = f32[8,24,128]{2,1,0:T(8,128)S(1)} all-to-all(f32[8,24,128]{2,1,0:T(8,128)} %get-tuple-element.19), channel_id=1, replica_groups=mesh['circ'=16,'rad'=6,'mode'=8] {'mode'}, dimensions={0} | all-to-all | bytes 196608 | tf_op jit(solution)/shard_map/all_to_all | solution.py:582
  18.1 0.0 copy-done
  18.1 0.0 copy-done.2
  18.1 0.8 %shard_map.96 = (f32[3,4,8,256]{3,2,1,0:T(8,128)S(1)}, f32[4,8,128]{2,1,0:T(8,128)S(1)}, f32[24,8,128]{2,1,0:T(8,128)S(1)}, f32[24,8,128]{2,1,0:T(8,128)S(1)}) custom-call(f32[8,24,128]{2,1,0:T(8,128)S(1)} %all_to_all.10.got, f32[3,4,8,256]{3,2,1,0:T(8,128)S(1)} %copy-done, f32[4,8,256]{2,1,0:T(8,128)S(1)} %copy-done.2), custom_call_target="tpu_custom_call" | custom-call | flops 1000000 | bytes 1000000 | tf_op jit(solution)/shard_map/pallas_call | solution.py:583
  18.9 4.0 %collective-permute-start = (f32[24,8,128]{2,1,0:T(8,128)S(1)}, f32[24,8,128]{2,1,0:T(8,128)S(1)}, u32[]{:S(2)}, u32[]{:S(2)}) collective-permute-start(f32[24,8,128]{2,1,0:T(8,128)S(1)} %get-tuple-element.22), channel_id=1, source_target_pairs={{0,48},{48,96},{96,144},{144,192},{192,240},{240,288},{288,336},{3... | collective-permute-start | bytes 294920 | tf_op jit(solution)/shard_map/ppermute | solution.py:589
  22.9 7.7 %collective-permute-start.1 = (f32[24,8,128]{2,1,0:T(8,128)S(1)}, f32[24,8,128]{2,1,0:T(8,128)S(1)}, u32[]{:S(2)}, u32[]{:S(2)}) collective-permute-start(f32[24,8,128]{2,1,0:T(8,128)S(1)} %get-tuple-element.23), channel_id=1, source_target_pairs={{48,0},{96,48},{144,96},{192,144},{240,192},{288,240},{336,288},{3... | collective-permute-start | bytes 294920 | tf_op jit(solution)/shard_map/ppermute | solution.py:590
  30.7 0.1 collective-permute-done.got_first
  30.8 1.5 %collective-permute-done.1.got_second = f32[24,8,128]{2,1,0:T(8,128)S(1)} collective-permute-done((f32[24,8,128]{2,1,0:T(8,128)S(1)}, f32[24,8,128]{2,1,0:T(8,128)S(1)}, u32[]{:S(2)}, u32[]{:S(2)}) %collective-permute-start.1) | collective-permute-done | bytes 98336 | tf_op jit(solution)/shard_map/ppermute | solution.py:590
  32.3 0.1 shard_map.97
  32.4 13.2 %collective-permute-start.2 = (f32[24,8,128]{2,1,0:T(8,128)S(1)}, f32[24,8,128]{2,1,0:T(8,128)S(1)}, u32[]{:S(2)}, u32[]{:S(2)}) collective-permute-start(f32[24,8,128]{2,1,0:T(8,128)S(1)} %get-tuple-element.25), channel_id=1, source_target_pairs={{8,16},{16,8},{24,32},{32,24},{9,17},{17,9},{25,33},{33,25},{10,18... | collective-permute-start | bytes 294920 | tf_op jit(solution)/shard_map/ppermute | solution.py:598
  45.6 1.9 %collective-permute-start.3 = (f32[24,8,128]{2,1,0:T(8,128)S(1)}, f32[24,8,128]{2,1,0:T(8,128)S(1)}, u32[]{:S(2)}, u32[]{:S(2)}) collective-permute-start(f32[24,8,128]{2,1,0:T(8,128)S(1)} %get-tuple-element.26), channel_id=1, source_target_pairs={{0,8},{8,0},{16,24},{24,16},{32,40},{40,32},{1,9},{9,1},{17,25},{2... | collective-permute-start | bytes 294920 | tf_op jit(solution)/shard_map/ppermute | solution.py:599
  47.5 0.0 copy-start.3
  47.5 0.7 copy-done.3
  48.2 1.9 %shard_map.98 = (f32[2,39,8,384]{3,2,1,0:T(8,128)S(1)}, f32[6,64,128]{2,1,0:T(8,128)S(1)}, bf16[256,512]{1,0:T(8,128)(2,1)S(1)}) custom-call(f32[15,64,128]{2,1,0:T(8,128)S(1)} %get-tuple-element.24.turned, f32[2,39,8,384]{3,2,1,0:T(8,128)S(1)} %get-tuple-element.27.left_in, f32[6,64,128]{2,1,0:T(8,128)S(1)} %get-tuple-element.28.keep_in, s32[1,512]{1,0:T(1,128)S(1)} %bitcast.11), custom_call_target="tpu_custom_call" | custom-call | flops 10000000 | bytes 1000000 | tf_op jit(solution)/shard_map/pallas_call | solution.py:604
  50.1 0.0 collective-permute-done.2.got_second
  50.1 0.0 collective-permute-done.3.got_first
  50.2 0.0 copy-start.1
  50.2 1.0 %shard_map.99.keep = f32[6,64,128]{2,1,0:T(8,128)S(1)} custom-call(f32[15,64,128]{2,1,0:T(8,128)S(1)} %get-tuple-element.24.turned, f32[24,8,128]{2,1,0:T(8,128)S(1)} %collective-permute-done.2.got_second, f32[24,8,128]{2,1,0:T(8,128)S(1)} %collective-permute-done.3.got_first, f32[2,39,8,384]{3,2,1,0:T(8,128)S(1)} %get-tuple-element.29.left, ...), custom_call_target="tpu_custom_call" | custom-call | flops 1000000 | bytes 1000000 | tf_op jit(solution)/shard_map/pallas_call | solution.py:611
  51.2 0.0 copy-done.1
  51.2 0.3 shard_map.100
  51.5 19.0 %all_to_all.11.parts = f32[48,1,128]{2,1,0:T(1,128)S(1)} all-to-all(f32[48,1,128]{2,1,0:T(1,128)S(1)} %shard_map.100), channel_id=1, replica_groups=mesh['circ'=16,'rad'=6,'mode'=8] {'rad','mode'}, dimensions={0} | all-to-all | bytes 49152 | tf_op jit(solution)/shard_map/all_to_all | solution.py:618
  70.5 0.7 shard_map.101
Async XLA Ops:
  2.7 15.4 %copy-start = (f32[3,4,8,256]{3,2,1,0:T(8,128)S(1)}, f32[3,4,8,256]{3,2,1,0:T(8,128)}, u32[]{:S(2)}) copy-start(f32[3,4,8,256]{3,2,1,0:T(8,128)} %prev.3) | copy-start | bytes 294916
  2.7 15.4 %copy-start.2 = (f32[4,8,256]{2,1,0:T(8,128)S(1)}, f32[4,8,256]{2,1,0:T(8,128)}, u32[]{:S(2)}) copy-start(f32[4,8,256]{2,1,0:T(8,128)} %get-tuple-element.18.e) | copy-start | bytes 98308
  18.9 11.9 %collective-permute-start = (f32[24,8,128]{2,1,0:T(8,128)S(1)}, f32[24,8,128]{2,1,0:T(8,128)S(1)}, u32[]{:S(2)}, u32[]{:S(2)}) collective-permute-start(f32[24,8,128]{2,1,0:T(8,128)S(1)} %get-tuple-element.22), channel_id=1, source_target_pairs={{0,48},{48,96},{96,144},{144,192},{192,240},{240,288},{288,336},{3... | collective-permute-start | bytes 294920 | tf_op jit(solution)/shard_map/ppermute | solution.py:589
  22.9 9.4 %collective-permute-start.1 = (f32[24,8,128]{2,1,0:T(8,128)S(1)}, f32[24,8,128]{2,1,0:T(8,128)S(1)}, u32[]{:S(2)}, u32[]{:S(2)}) collective-permute-start(f32[24,8,128]{2,1,0:T(8,128)S(1)} %get-tuple-element.23), channel_id=1, source_target_pairs={{48,0},{96,48},{144,96},{192,144},{240,192},{288,240},{336,288},{3... | collective-permute-start | bytes 294920 | tf_op jit(solution)/shard_map/ppermute | solution.py:590
  32.4 17.7 %collective-permute-start.2 = (f32[24,8,128]{2,1,0:T(8,128)S(1)}, f32[24,8,128]{2,1,0:T(8,128)S(1)}, u32[]{:S(2)}, u32[]{:S(2)}) collective-permute-start(f32[24,8,128]{2,1,0:T(8,128)S(1)} %get-tuple-element.25), channel_id=1, source_target_pairs={{8,16},{16,8},{24,32},{32,24},{9,17},{17,9},{25,33},{33,25},{10,18... | collective-permute-start | bytes 294920 | tf_op jit(solution)/shard_map/ppermute | solution.py:598
  45.6 4.6 %collective-permute-start.3 = (f32[24,8,128]{2,1,0:T(8,128)S(1)}, f32[24,8,128]{2,1,0:T(8,128)S(1)}, u32[]{:S(2)}, u32[]{:S(2)}) collective-permute-start(f32[24,8,128]{2,1,0:T(8,128)S(1)} %get-tuple-element.26), channel_id=1, source_target_pairs={{0,8},{8,0},{16,24},{24,16},{32,40},{40,32},{1,9},{9,1},{17,25},{2... | collective-permute-start | bytes 294920 | tf_op jit(solution)/shard_map/ppermute | solution.py:599
  47.5 0.7 copy-start.3
  50.2 1.0 %copy-start.1 = (f32[1,1,1,24,3,512]{5,3,4,2,1,0:T(8,128)S(1)}, f32[1,1,1,24,3,512]{5,3,4,2,1,0:T(8,128)}, u32[]{:S(2)}) copy-start(f32[1,1,1,24,3,512]{5,3,4,2,1,0:T(8,128)} %param.15) | copy-start | bytes 442372

commit v6 on v5

--- a/solution.py
+++ b/solution.py
@@ -423,7 +423,7 @@
 
 
 def sweep_kernel(
-    turned, got_second, got_first, left, kept, keep
+    devices, ncirc, turned, got_second, got_first, left, kept, pick, ids, shapes, keep, force, sums_of
 ):
     nrad = turned.shape[1] // 8
     rad = lax.axis_index("rad")
@@ -480,6 +480,7 @@
     inside = slice(16, 8 * (nrad - 2))
     for index in range(6):
         keep[index, inside, :] = kept[index, inside, :]
+    force_of(devices, ncirc, keep, pick, ids, shapes, force, sums_of)
 
 def plane_of(keep, i, c, nrad):
     both = [keep[2 * i + t, pl.ds(c, nrad, stride=8), :] for t in range(2)]
@@ -504,7 +505,7 @@
     second.wait()
 
 
-def force_kernel(devices, ncirc, keep, pick, ids, shapes, force, sums_of):
+def force_of(devices, ncirc, keep, pick, ids, shapes, force, sums_of):
     nrad = keep.shape[1] // 8
     lines = ncirc * nrad
     flat = jnp.concatenate([plane_of(keep, i, c, nrad) for i in range(3) for c in range(ncirc)], axis=0)
@@ -608,13 +609,12 @@
         [pltpu.VMEM(ids.shape, ids.dtype), pltpu.SemaphoreType.DMA],
         flops=10_000_000,
     )(turned, left, keep, ids)
-    (keep,) = call(sweep_kernel, [VMEM] * 5, [kept])(turned, second, first, left, keep)
-    (force,) = call(
-        functools.partial(force_kernel, n_mode, ncirc),
-        [VMEM] * 4,
-        [(n_rad * n_mode, 1, 128)],
+    keep, force = call(
+        functools.partial(sweep_kernel, n_mode, ncirc),
+        [VMEM] * 8,
+        [kept, (n_rad * n_mode, 1, 128)],
         [pltpu.VMEM((modes, 128), F32)],
-    )(keep, pick, ids, shapes)
+    )(turned, second, first, left, keep, pick, ids, shapes)
     parts = lax.all_to_all(force, ("rad", "mode"), split_axis=0, concat_axis=0, tiled=True)
     final, own_force = call(
         finish_kernel,

time: 71.6 us -> 71.5 us (level)
  no operation moved by 1% of the time
where the time goes in v6:
time: 71.5 us; the launch traced here: 71.1 us
  blocking collectives  34.4 us (48%)
  starting transfers between devices  26.8 us (37%)
  Pallas kernels  6.8 us (10%)
  waiting for transfers between devices  1.62 us (2%)
  between operations  0.75 us (1%)
    all_to_all x1, blocking collectives, on_device(): lax.all_to_all(force, ('rad', 'mode'), split_axis=0, concat_axis=0, tiled...  19 us
    all_to_all x1, blocking collectives, on_device(): got = lax.all_to_all(send, 'mode', split_axis=0, concat_axis=0, tiled=True)  15.4 us
    ppermute x1, starting transfers between devices, on_device(): second = lax.ppermute(second, 'rad', swaps('rad', 1, False))  13.2 us
    ppermute x1, starting transfers between devices, on_device(): lax.ppermute(second, 'circ', [((i + 1) % n_circ, i) for i in range(n_circ)])  7.73 us
    ppermute x1, starting transfers between devices, on_device(): lax.ppermute(first, 'circ', [(i, (i + 1) % n_circ) for i in range(n_circ)])  4.04 us
    pallas_call x1, Pallas kernels, on_device(): call(pack_kernel, [HBM] * 6, [(n_mode, 24, 128), cells], [pltpu.SMEM(x.sh...  2.06 us
    pallas_call x1, Pallas kernels, on_device(): call(inner_kernel, [VMEM] * 3 + [HBM], [left.shape, kept, jax.ShapeDtypeS...  1.94 us
    ppermute x1, starting transfers between devices, on_device(): first = lax.ppermute(first, 'rad', swaps('rad', 0, False))  1.92 us
  transfers between devices with their start and end apart: 4, of which 2 were waited for; matrix products, arithmetic and copies ran while one was open for 0% of the time, Pallas kernels for 3%

profile of v6, /device:TPU:1, one launch (start us, length us, event | category | flops | bytes accessed | tf_op | source)
XLA Modules:
  0.0 71.1 jit_solution(2060990210116005848)
XLA Ops:
  0.6 2.1 %shard_map.95 = (f32[8,24,128]{2,1,0:T(8,128)}, f32[4,8,256]{2,1,0:T(8,128)}) custom-call(f32[8]{0:T(128)} %moduli_in.1, s32[8]{0:T(128)} %bitcast.15, f32[3,4,8,256]{3,2,1,0:T(8,128)} %prev.3, s32[4,8,256]{2,1,0:T(8,128)} %cls_in.1, f32[3,8,512]{2,1,0:T(8,128)} %bitcast.13, s32[8,512]{1,0:T(8,128)} %bitcast.14), custom_call_target="tpu_custom_call" | custom-call | flops 1000000 | bytes 1000000 | tf_op jit(solution)/shard_map/pallas_call | solution.py:574
  2.7 0.0 copy-start
  2.7 0.0 copy-start.2
  2.7 15.4 %all_to_all.10.got = f32[8,24,128]{2,1,0:T(8,128)S(1)} all-to-all(f32[8,24,128]{2,1,0:T(8,128)} %get-tuple-element.21), channel_id=1, replica_groups=mesh['circ'=16,'rad'=6,'mode'=8] {'mode'}, dimensions={0} | all-to-all | bytes 196608 | tf_op jit(solution)/shard_map/all_to_all | solution.py:583
  18.1 0.0 copy-done
  18.1 0.0 copy-done.2
  18.1 0.8 %shard_map.96 = (f32[3,4,8,256]{3,2,1,0:T(8,128)S(1)}, f32[4,8,128]{2,1,0:T(8,128)S(1)}, f32[24,8,128]{2,1,0:T(8,128)S(1)}, f32[24,8,128]{2,1,0:T(8,128)S(1)}) custom-call(f32[8,24,128]{2,1,0:T(8,128)S(1)} %all_to_all.10.got, f32[3,4,8,256]{3,2,1,0:T(8,128)S(1)} %copy-done, f32[4,8,256]{2,1,0:T(8,128)S(1)} %copy-done.2), custom_call_target="tpu_custom_call" | custom-call | flops 1000000 | bytes 1000000 | tf_op jit(solution)/shard_map/pallas_call | solution.py:584
  18.9 4.0 %collective-permute-start = (f32[24,8,128]{2,1,0:T(8,128)S(1)}, f32[24,8,128]{2,1,0:T(8,128)S(1)}, u32[]{:S(2)}, u32[]{:S(2)}) collective-permute-start(f32[24,8,128]{2,1,0:T(8,128)S(1)} %get-tuple-element.24), channel_id=1, source_target_pairs={{0,48},{48,96},{96,144},{144,192},{192,240},{240,288},{288,336},{3... | collective-permute-start | bytes 294920 | tf_op jit(solution)/shard_map/ppermute | solution.py:590
  22.9 7.7 %collective-permute-start.1 = (f32[24,8,128]{2,1,0:T(8,128)S(1)}, f32[24,8,128]{2,1,0:T(8,128)S(1)}, u32[]{:S(2)}, u32[]{:S(2)}) collective-permute-start(f32[24,8,128]{2,1,0:T(8,128)S(1)} %get-tuple-element.25), channel_id=1, source_target_pairs={{48,0},{96,48},{144,96},{192,144},{240,192},{288,240},{336,288},{3... | collective-permute-start | bytes 294920 | tf_op jit(solution)/shard_map/ppermute | solution.py:591
  30.7 0.1 collective-permute-done.got_first
  30.8 1.5 %collective-permute-done.1.got_second = f32[24,8,128]{2,1,0:T(8,128)S(1)} collective-permute-done((f32[24,8,128]{2,1,0:T(8,128)S(1)}, f32[24,8,128]{2,1,0:T(8,128)S(1)}, u32[]{:S(2)}, u32[]{:S(2)}) %collective-permute-start.1) | collective-permute-done | bytes 98336 | tf_op jit(solution)/shard_map/ppermute | solution.py:591
  32.3 0.1 shard_map.97
  32.4 13.2 %collective-permute-start.2 = (f32[24,8,128]{2,1,0:T(8,128)S(1)}, f32[24,8,128]{2,1,0:T(8,128)S(1)}, u32[]{:S(2)}, u32[]{:S(2)}) collective-permute-start(f32[24,8,128]{2,1,0:T(8,128)S(1)} %get-tuple-element.27), channel_id=1, source_target_pairs={{8,16},{16,8},{24,32},{32,24},{9,17},{17,9},{25,33},{33,25},{10,18... | collective-permute-start | bytes 294920 | tf_op jit(solution)/shard_map/ppermute | solution.py:599
  45.6 1.9 %collective-permute-start.3 = (f32[24,8,128]{2,1,0:T(8,128)S(1)}, f32[24,8,128]{2,1,0:T(8,128)S(1)}, u32[]{:S(2)}, u32[]{:S(2)}) collective-permute-start(f32[24,8,128]{2,1,0:T(8,128)S(1)} %get-tuple-element.28), channel_id=1, source_target_pairs={{0,8},{8,0},{16,24},{24,16},{32,40},{40,32},{1,9},{9,1},{17,25},{2... | collective-permute-start | bytes 294920 | tf_op jit(solution)/shard_map/ppermute | solution.py:600
  47.5 0.0 copy-start.3
  47.5 0.7 copy-done.3
  48.2 0.0 copy-start.1
  48.2 1.9 %shard_map.98 = (f32[2,39,8,384]{3,2,1,0:T(8,128)S(1)}, f32[6,64,128]{2,1,0:T(8,128)S(1)}, bf16[256,512]{1,0:T(8,128)(2,1)S(1)}) custom-call(f32[15,64,128]{2,1,0:T(8,128)S(1)} %get-tuple-element.26.turned, f32[2,39,8,384]{3,2,1,0:T(8,128)S(1)} %get-tuple-element.29.left_in, f32[6,64,128]{2,1,0:T(8,128)S(1)} %get-tuple-element.30.keep_in, s32[1,512]{1,0:T(1,128)S(1)} %bitcast.11), custom_call_target="tpu_custom_call" | custom-call | flops 10000000 | bytes 1000000 | tf_op jit(solution)/shard_map/pallas_call | solution.py:605
  50.1 0.0 collective-permute-done.2.got_second
  50.1 0.0 collective-permute-done.3.got_first
  50.2 0.0 copy-done.1
  50.2 1.2 %shard_map.99 = (f32[6,64,128]{2,1,0:T(8,128)S(1)}, f32[48,1,128]{2,1,0:T(1,128)S(1)}) custom-call(f32[15,64,128]{2,1,0:T(8,128)S(1)} %get-tuple-element.26.turned, f32[24,8,128]{2,1,0:T(8,128)S(1)} %collective-permute-done.2.got_second, f32[24,8,128]{2,1,0:T(8,128)S(1)} %collective-permute-done.3.got_first, f32[2,39,8,384]{3,2,1,0:T(8,128)S(1)} %get-tuple-element.31.left, ...), custom_call_target="tpu_custom_call" | custom-call | flops 1000000 | bytes 1000000 | tf_op jit(solution)/shard_map/pallas_call | solution.py:612
  51.4 19.0 %all_to_all.11.parts = f32[48,1,128]{2,1,0:T(1,128)S(1)} all-to-all(f32[48,1,128]{2,1,0:T(1,128)S(1)} %get-tuple-element.35), channel_id=1, replica_groups=mesh['circ'=16,'rad'=6,'mode'=8] {'rad','mode'}, dimensions={0} | all-to-all | bytes 49152 | tf_op jit(solution)/shard_map/all_to_all | solution.py:618
  70.4 0.7 shard_map.100
Async XLA Ops:
  2.7 15.4 %copy-start = (f32[3,4,8,256]{3,2,1,0:T(8,128)S(1)}, f32[3,4,8,256]{3,2,1,0:T(8,128)}, u32[]{:S(2)}) copy-start(f32[3,4,8,256]{3,2,1,0:T(8,128)} %prev.3) | copy-start | bytes 294916
  2.7 15.4 %copy-start.2 = (f32[4,8,256]{2,1,0:T(8,128)S(1)}, f32[4,8,256]{2,1,0:T(8,128)}, u32[]{:S(2)}) copy-start(f32[4,8,256]{2,1,0:T(8,128)} %get-tuple-element.20.e) | copy-start | bytes 98308
  18.9 11.9 %collective-permute-start = (f32[24,8,128]{2,1,0:T(8,128)S(1)}, f32[24,8,128]{2,1,0:T(8,128)S(1)}, u32[]{:S(2)}, u32[]{:S(2)}) collective-permute-start(f32[24,8,128]{2,1,0:T(8,128)S(1)} %get-tuple-element.24), channel_id=1, source_target_pairs={{0,48},{48,96},{96,144},{144,192},{192,240},{240,288},{288,336},{3... | collective-permute-start | bytes 294920 | tf_op jit(solution)/shard_map/ppermute | solution.py:590
  22.9 9.4 %collective-permute-start.1 = (f32[24,8,128]{2,1,0:T(8,128)S(1)}, f32[24,8,128]{2,1,0:T(8,128)S(1)}, u32[]{:S(2)}, u32[]{:S(2)}) collective-permute-start(f32[24,8,128]{2,1,0:T(8,128)S(1)} %get-tuple-element.25), channel_id=1, source_target_pairs={{48,0},{96,48},{144,96},{192,144},{240,192},{288,240},{336,288},{3... | collective-permute-start | bytes 294920 | tf_op jit(solution)/shard_map/ppermute | solution.py:591
  32.4 17.7 %collective-permute-start.2 = (f32[24,8,128]{2,1,0:T(8,128)S(1)}, f32[24,8,128]{2,1,0:T(8,128)S(1)}, u32[]{:S(2)}, u32[]{:S(2)}) collective-permute-start(f32[24,8,128]{2,1,0:T(8,128)S(1)} %get-tuple-element.27), channel_id=1, source_target_pairs={{8,16},{16,8},{24,32},{32,24},{9,17},{17,9},{25,33},{33,25},{10,18... | collective-permute-start | bytes 294920 | tf_op jit(solution)/shard_map/ppermute | solution.py:599
  45.6 4.6 %collective-permute-start.3 = (f32[24,8,128]{2,1,0:T(8,128)S(1)}, f32[24,8,128]{2,1,0:T(8,128)S(1)}, u32[]{:S(2)}, u32[]{:S(2)}) collective-permute-start(f32[24,8,128]{2,1,0:T(8,128)S(1)} %get-tuple-element.28), channel_id=1, source_target_pairs={{0,8},{8,0},{16,24},{24,16},{32,40},{40,32},{1,9},{9,1},{17,25},{2... | collective-permute-start | bytes 294920 | tf_op jit(solution)/shard_map/ppermute | solution.py:600
  47.5 0.7 copy-start.3
  48.2 2.0 %copy-start.1 = (f32[1,1,1,24,3,512]{5,3,4,2,1,0:T(8,128)S(1)}, f32[1,1,1,24,3,512]{5,3,4,2,1,0:T(8,128)}, u32[]{:S(2)}) copy-start(f32[1,1,1,24,3,512]{5,3,4,2,1,0:T(8,128)} %param.15) | copy-start | bytes 442372

commit v7 on v6

--- a/solution.py
+++ b/solution.py
@@ -343,7 +343,7 @@
 
 
 def works_ahead():
-    return lax.axis_index("circ") % 4 != 0
+    return (lax.axis_index("circ") % 4 != 0) | (lax.axis_index("rad") % 2 == 1)
 
 
 def inner_work(turned, left, keep):

time: 71.5 us -> 71.5 us (level)
  starting transfers between devices: 26.8 us -> 25 us
  waiting for transfers between devices: 1.62 us -> 3.25 us
    ppermute x1, starting transfers between devices: 13.2 us -> 11.3 us  [on_device(): second = lax.ppermute(second, 'rad', swaps('rad', 1, False))]
    pallas_call x1, Pallas kernels: 0.12 us -> 1.99 us  [on_device(): call(turn_kernel, [VMEM] * 6, [(15, 8 * nrad, 128), message, message, lef...]
    pallas_call x1, Pallas kernels: 1.94 us -> 0.14 us  [on_device(): call(inner_kernel, [VMEM] * 3 + [HBM], [left.shape, kept, jax.ShapeDtypeS...]
    ppermute x1, waiting for transfers between devices: 0.01 us -> 1.63 us  [on_device(): second = lax.ppermute(second, 'rad', swaps('rad', 1, False))]
  transfers between devices with their start and end apart: 4 -> 4, of which waited for: 2 -> 3; matrix products, arithmetic and copies ran while one was open for 0% -> 0% of each run, Pallas kernels for 3% -> 0%
where the time goes in v7:
time: 71.5 us; the launch traced here: 71.1 us
  blocking collectives  34.6 us (48%)
  starting transfers between devices  25 us (35%)
  Pallas kernels  6.86 us (10%)
  waiting for transfers between devices  3.25 us (5%)
  between operations  0.73 us (1%)
    all_to_all x1, blocking collectives, on_device(): lax.all_to_all(force, ('rad', 'mode'), split_axis=0, concat_axis=0, tiled...  19.2 us
    all_to_all x1, blocking collectives, on_device(): got = lax.all_to_all(send, 'mode', split_axis=0, concat_axis=0, tiled=True)  15.4 us
    ppermute x1, starting transfers between devices, on_device(): second = lax.ppermute(second, 'rad', swaps('rad', 1, False))  11.3 us
    ppermute x1, starting transfers between devices, on_device(): lax.ppermute(second, 'circ', [((i + 1) % n_circ, i) for i in range(n_circ)])  7.73 us
    ppermute x1, starting transfers between devices, on_device(): lax.ppermute(first, 'circ', [(i, (i + 1) % n_circ) for i in range(n_circ)])  4.04 us
    pallas_call x1, Pallas kernels, on_device(): call(pack_kernel, [HBM] * 6, [(n_mode, 24, 128), cells], [pltpu.SMEM(x.sh...  2.06 us
    pallas_call x1, Pallas kernels, on_device(): call(turn_kernel, [VMEM] * 6, [(15, 8 * nrad, 128), message, message, lef...  1.99 us
    ppermute x1, starting transfers between devices, on_device(): first = lax.ppermute(first, 'rad', swaps('rad', 0, False))  1.92 us
  transfers between devices with their start and end apart: 4, of which 3 were waited for; matrix products, arithmetic and copies ran while one was open for 0% of the time, Pallas kernels for 0%

profile of v7, /device:TPU:1, one launch (start us, length us, event | category | flops | bytes accessed | tf_op | source)
XLA Modules:
  0.0 71.1 jit_solution(4230750310218804180)
XLA Ops:
  0.6 2.1 %shard_map.95 = (f32[8,24,128]{2,1,0:T(8,128)}, f32[4,8,256]{2,1,0:T(8,128)}) custom-call(f32[8]{0:T(128)} %moduli_in.1, s32[8]{0:T(128)} %bitcast.15, f32[3,4,8,256]{3,2,1,0:T(8,128)} %prev.3, s32[4,8,256]{2,1,0:T(8,128)} %cls_in.1, f32[3,8,512]{2,1,0:T(8,128)} %bitcast.13, s32[8,512]{1,0:T(8,128)} %bitcast.14), custom_call_target="tpu_custom_call" | custom-call | flops 1000000 | bytes 1000000 | tf_op jit(solution)/shard_map/pallas_call | solution.py:574
  2.7 0.0 copy-start
  2.7 0.0 copy-start.2
  2.7 15.4 %all_to_all.10.got = f32[8,24,128]{2,1,0:T(8,128)S(1)} all-to-all(f32[8,24,128]{2,1,0:T(8,128)} %get-tuple-element.21), channel_id=1, replica_groups=mesh['circ'=16,'rad'=6,'mode'=8] {'mode'}, dimensions={0} | all-to-all | bytes 196608 | tf_op jit(solution)/shard_map/all_to_all | solution.py:583
  18.1 0.0 copy-done
  18.1 0.0 copy-done.2
  18.1 0.8 %shard_map.96 = (f32[3,4,8,256]{3,2,1,0:T(8,128)S(1)}, f32[4,8,128]{2,1,0:T(8,128)S(1)}, f32[24,8,128]{2,1,0:T(8,128)S(1)}, f32[24,8,128]{2,1,0:T(8,128)S(1)}) custom-call(f32[8,24,128]{2,1,0:T(8,128)S(1)} %all_to_all.10.got, f32[3,4,8,256]{3,2,1,0:T(8,128)S(1)} %copy-done, f32[4,8,256]{2,1,0:T(8,128)S(1)} %copy-done.2), custom_call_target="tpu_custom_call" | custom-call | flops 1000000 | bytes 1000000 | tf_op jit(solution)/shard_map/pallas_call | solution.py:584
  18.9 4.0 %collective-permute-start = (f32[24,8,128]{2,1,0:T(8,128)S(1)}, f32[24,8,128]{2,1,0:T(8,128)S(1)}, u32[]{:S(2)}, u32[]{:S(2)}) collective-permute-start(f32[24,8,128]{2,1,0:T(8,128)S(1)} %get-tuple-element.24), channel_id=1, source_target_pairs={{0,48},{48,96},{96,144},{144,192},{192,240},{240,288},{288,336},{3... | collective-permute-start | bytes 294920 | tf_op jit(solution)/shard_map/ppermute | solution.py:590
  22.9 7.7 %collective-permute-start.1 = (f32[24,8,128]{2,1,0:T(8,128)S(1)}, f32[24,8,128]{2,1,0:T(8,128)S(1)}, u32[]{:S(2)}, u32[]{:S(2)}) collective-permute-start(f32[24,8,128]{2,1,0:T(8,128)S(1)} %get-tuple-element.25), channel_id=1, source_target_pairs={{48,0},{96,48},{144,96},{192,144},{240,192},{288,240},{336,288},{3... | collective-permute-start | bytes 294920 | tf_op jit(solution)/shard_map/ppermute | solution.py:591
  30.7 0.1 collective-permute-done.got_first
  30.8 1.5 %collective-permute-done.1.got_second = f32[24,8,128]{2,1,0:T(8,128)S(1)} collective-permute-done((f32[24,8,128]{2,1,0:T(8,128)S(1)}, f32[24,8,128]{2,1,0:T(8,128)S(1)}, u32[]{:S(2)}, u32[]{:S(2)}) %collective-permute-start.1) | collective-permute-done | bytes 98336 | tf_op jit(solution)/shard_map/ppermute | solution.py:591
  32.3 2.0 %shard_map.97 = (f32[15,64,128]{2,1,0:T(8,128)S(1)}, f32[24,8,128]{2,1,0:T(8,128)S(1)}, f32[24,8,128]{2,1,0:T(8,128)S(1)}, f32[2,39,8,384]{3,2,1,0:T(8,128)S(1)}, f32[6,64,128]{2,1,0:T(8,128)S(1)}) custom-call(f32[3,4,8,256]{3,2,1,0:T(8,128)S(1)} %copy-done, f32[4,8,256]{2,1,0:T(8,128)S(1)} %copy-done.2, f32[3,4,8,256]{3,2,1,0:T(8,128)S(1)} %get-tuple-element.22.rhs, ...), custom_call_target="tpu_custom_call" | custom-call | flops 1000000 | bytes 1000000 | tf_op jit(solution)/shard_map/pallas_call | solution.py:594
  34.3 11.3 %collective-permute-start.2 = (f32[24,8,128]{2,1,0:T(8,128)S(1)}, f32[24,8,128]{2,1,0:T(8,128)S(1)}, u32[]{:S(2)}, u32[]{:S(2)}) collective-permute-start(f32[24,8,128]{2,1,0:T(8,128)S(1)} %get-tuple-element.27), channel_id=1, source_target_pairs={{8,16},{16,8},{24,32},{32,24},{9,17},{17,9},{25,33},{33,25},{10,18... | collective-permute-start | bytes 294920 | tf_op jit(solution)/shard_map/ppermute | solution.py:599
  45.6 1.9 %collective-permute-start.3 = (f32[24,8,128]{2,1,0:T(8,128)S(1)}, f32[24,8,128]{2,1,0:T(8,128)S(1)}, u32[]{:S(2)}, u32[]{:S(2)}) collective-permute-start(f32[24,8,128]{2,1,0:T(8,128)S(1)} %get-tuple-element.28), channel_id=1, source_target_pairs={{0,8},{8,0},{16,24},{24,16},{32,40},{40,32},{1,9},{9,1},{17,25},{2... | collective-permute-start | bytes 294920 | tf_op jit(solution)/shard_map/ppermute | solution.py:600
  47.5 0.0 copy-start.3
  47.5 0.7 copy-done.3
  48.2 0.0 copy-start.1
  48.2 0.1 shard_map.98
  48.3 1.6 %collective-permute-done.2.got_second = f32[24,8,128]{2,1,0:T(8,128)S(1)} collective-permute-done((f32[24,8,128]{2,1,0:T(8,128)S(1)}, f32[24,8,128]{2,1,0:T(8,128)S(1)}, u32[]{:S(2)}, u32[]{:S(2)}) %collective-permute-start.2) | collective-permute-done | bytes 98336 | tf_op jit(solution)/shard_map/ppermute | solution.py:599
  50.0 0.0 collective-permute-done.3.got_first
  50.0 0.0 copy-done.1
  50.0 1.2 %shard_map.99 = (f32[6,64,128]{2,1,0:T(8,128)S(1)}, f32[48,1,128]{2,1,0:T(1,128)S(1)}) custom-call(f32[15,64,128]{2,1,0:T(8,128)S(1)} %get-tuple-element.26.turned, f32[24,8,128]{2,1,0:T(8,128)S(1)} %collective-permute-done.2.got_second, f32[24,8,128]{2,1,0:T(8,128)S(1)} %collective-permute-done.3.got_first, f32[2,39,8,384]{3,2,1,0:T(8,128)S(1)} %get-tuple-element.31.left, ...), custom_call_target="tpu_custom_call" | custom-call | flops 1000000 | bytes 1000000 | tf_op jit(solution)/shard_map/pallas_call | solution.py:612
  51.2 19.2 %all_to_all.11.parts = f32[48,1,128]{2,1,0:T(1,128)S(1)} all-to-all(f32[48,1,128]{2,1,0:T(1,128)S(1)} %get-tuple-element.35), channel_id=1, replica_groups=mesh['circ'=16,'rad'=6,'mode'=8] {'rad','mode'}, dimensions={0} | all-to-all | bytes 49152 | tf_op jit(solution)/shard_map/all_to_all | solution.py:618
  70.4 0.7 shard_map.100
Async XLA Ops:
  2.7 15.4 %copy-start = (f32[3,4,8,256]{3,2,1,0:T(8,128)S(1)}, f32[3,4,8,256]{3,2,1,0:T(8,128)}, u32[]{:S(2)}) copy-start(f32[3,4,8,256]{3,2,1,0:T(8,128)} %prev.3) | copy-start | bytes 294916
  2.7 15.4 %copy-start.2 = (f32[4,8,256]{2,1,0:T(8,128)S(1)}, f32[4,8,256]{2,1,0:T(8,128)}, u32[]{:S(2)}) copy-start(f32[4,8,256]{2,1,0:T(8,128)} %get-tuple-element.20.e) | copy-start | bytes 98308
  18.9 11.9 %collective-permute-start = (f32[24,8,128]{2,1,0:T(8,128)S(1)}, f32[24,8,128]{2,1,0:T(8,128)S(1)}, u32[]{:S(2)}, u32[]{:S(2)}) collective-permute-start(f32[24,8,128]{2,1,0:T(8,128)S(1)} %get-tuple-element.24), channel_id=1, source_target_pairs={{0,48},{48,96},{96,144},{144,192},{192,240},{240,288},{288,336},{3... | collective-permute-start | bytes 294920 | tf_op jit(solution)/shard_map/ppermute | solution.py:590
  22.9 9.4 %collective-permute-start.1 = (f32[24,8,128]{2,1,0:T(8,128)S(1)}, f32[24,8,128]{2,1,0:T(8,128)S(1)}, u32[]{:S(2)}, u32[]{:S(2)}) collective-permute-start(f32[24,8,128]{2,1,0:T(8,128)S(1)} %get-tuple-element.25), channel_id=1, source_target_pairs={{48,0},{96,48},{144,96},{192,144},{240,192},{288,240},{336,288},{3... | collective-permute-start | bytes 294920 | tf_op jit(solution)/shard_map/ppermute | solution.py:591
  34.3 15.7 %collective-permute-start.2 = (f32[24,8,128]{2,1,0:T(8,128)S(1)}, f32[24,8,128]{2,1,0:T(8,128)S(1)}, u32[]{:S(2)}, u32[]{:S(2)}) collective-permute-start(f32[24,8,128]{2,1,0:T(8,128)S(1)} %get-tuple-element.27), channel_id=1, source_target_pairs={{8,16},{16,8},{24,32},{32,24},{9,17},{17,9},{25,33},{33,25},{10,18... | collective-permute-start | bytes 294920 | tf_op jit(solution)/shard_map/ppermute | solution.py:599
  45.6 4.4 %collective-permute-start.3 = (f32[24,8,128]{2,1,0:T(8,128)S(1)}, f32[24,8,128]{2,1,0:T(8,128)S(1)}, u32[]{:S(2)}, u32[]{:S(2)}) collective-permute-start(f32[24,8,128]{2,1,0:T(8,128)S(1)} %get-tuple-element.28), channel_id=1, source_target_pairs={{0,8},{8,0},{16,24},{24,16},{32,40},{40,32},{1,9},{9,1},{17,25},{2... | collective-permute-start | bytes 294920 | tf_op jit(solution)/shard_map/ppermute | solution.py:600
  47.5 0.7 copy-start.3
  48.2 1.8 %copy-start.1 = (f32[1,1,1,24,3,512]{5,3,4,2,1,0:T(8,128)S(1)}, f32[1,1,1,24,3,512]{5,3,4,2,1,0:T(8,128)}, u32[]{:S(2)}) copy-start(f32[1,1,1,24,3,512]{5,3,4,2,1,0:T(8,128)} %param.15) | copy-start | bytes 442372

commit v8 on v7

--- a/solution.py
+++ b/solution.py
@@ -28,15 +28,15 @@
 
 
 def pack_kernel(
-    moduli_in, count_in, prev_in, cls_in, sens_in, nodes_in, send, e_out,
-    moduli, count, prev, cls, sens, nodes, sems,
+    moduli_in, count_in, prev_in, cls_in, sens_in, nodes_in, ids_in, send, e_out,
+    moduli, count, prev, cls, sens, nodes, ids, sems,
 ):
     copies = [
         pltpu.make_async_copy(source, target, sems.at[i])
         for i, (source, target) in enumerate(
             (
                 (sens_in, sens), (nodes_in, nodes), (prev_in, prev), (cls_in, cls),
-                (count_in, count), (moduli_in, moduli),
+                (count_in, count), (moduli_in, moduli), (ids_in, ids),
             )
         )
     ]
@@ -45,6 +45,9 @@
     for copy in copies:
         copy.wait()
     _, blocks, slots = sens.shape
+    e_out[cls.shape[0]] = jnp.zeros(e_out.shape[1:], F32)
+    for q in range(ids.shape[1] // cls.shape[2]):
+        e_out[cls.shape[0], q : q + 1, :] = ids[:, cls.shape[2] * q : cls.shape[2] * (q + 1)].astype(F32)
     ncirc, nrad, naxial = cls.shape
     lines = ncirc * nrad
     k = lax.axis_index("mode")
@@ -403,9 +406,12 @@
                 leave(side, SCALE, stiff[at][1])
 
 
-def inner_kernel(turned, left_in, keep_in, ids, left, keep, pick, nodes, sem):
-    copy = pltpu.make_async_copy(ids, nodes, sem)
-    copy.start()
+def listed(e, count):
+    last, width = e.shape[0] - 1, e.shape[2]
+    return jnp.concatenate([e[last, q : q + 1, :] for q in range(count // width)], axis=1).astype(jnp.int32)
+
+
+def inner_kernel(turned, left_in, keep_in, e, left, keep, pick):
     ahead = works_ahead()
 
     @pl.when(ahead)
@@ -417,13 +423,12 @@
     def _():
         inner_work(turned, left, keep)
 
-    copy.wait()
     cell = lax.broadcasted_iota(jnp.int32, pick.shape, 0)
-    pick[...] = jnp.where(cell == nodes[...] % 256, 1.0, 0.0).astype(BF16)
+    pick[...] = jnp.where(cell == listed(e, pick.shape[1]) % 256, 1.0, 0.0).astype(BF16)
 
 
 def sweep_kernel(
-    devices, ncirc, turned, got_second, got_first, left, kept, pick, ids, shapes, keep, force, sums_of
+    devices, ncirc, turned, got_second, got_first, left, kept, pick, riding, shapes, keep, force, sums_of
 ):
     nrad = turned.shape[1] // 8
     rad = lax.axis_index("rad")
@@ -480,7 +485,7 @@
     inside = slice(16, 8 * (nrad - 2))
     for index in range(6):
         keep[index, inside, :] = kept[index, inside, :]
-    force_of(devices, ncirc, keep, pick, ids, shapes, force, sums_of)
+    force_of(devices, ncirc, keep, pick, riding, shapes, force, sums_of)
 
 def plane_of(keep, i, c, nrad):
     both = [keep[2 * i + t, pl.ds(c, nrad, stride=8), :] for t in range(2)]
@@ -505,13 +510,13 @@
     second.wait()
 
 
-def force_of(devices, ncirc, keep, pick, ids, shapes, force, sums_of):
+def force_of(devices, ncirc, keep, pick, riding, shapes, force, sums_of):
     nrad = keep.shape[1] // 8
     lines = ncirc * nrad
     flat = jnp.concatenate([plane_of(keep, i, c, nrad) for i in range(3) for c in range(ncirc)], axis=0)
     high, low = split(flat)
     table = jnp.concatenate([high, low], axis=0).astype(BF16)
-    node = ids[...]
+    node = listed(riding, pick.shape[1])
     rows = jnp.dot(table, pick[...], preferred_element_type=F32)
     rows = rows[: 3 * lines] + rows[3 * lines :]
     line = lax.broadcasted_iota(jnp.int32, (lines, node.shape[1]), 0)
@@ -569,15 +574,15 @@
     message = (24, 8, 128)
     args = (
         class_moduli, flow_count[0, 0, 0], adjoint_prev, cell_class,
-        jnp.swapaxes(flow_sens[0, 0, 0], 0, 1), flow_nodes[0, 0, 0],
+        jnp.swapaxes(flow_sens[0, 0, 0], 0, 1), flow_nodes[0, 0, 0], surf_ids[0, 0],
     )
     send, e = call(
         pack_kernel,
-        [HBM] * 6,
-        [(n_mode, 24, 128), cells],
+        [HBM] * 7,
+        [(n_mode, 24, 128), (ncirc + 1, nrad, naxial)],
         [pltpu.SMEM(x.shape, x.dtype) for x in args[:2]]
         + [pltpu.VMEM(x.shape, x.dtype) for x in args[2:]]
-        + [pltpu.SemaphoreType.DMA((6,))],
+        + [pltpu.SemaphoreType.DMA((7,))],
         limit=63 * 1024 * 1024 + 512 * 1024,
     )(*args)
     got = lax.all_to_all(send, "mode", split_axis=0, concat_axis=0, tiled=True)
@@ -600,21 +605,19 @@
     first = lax.ppermute(first, "rad", swaps("rad", 0, False))
     modes = mode_shapes.shape[3]
     owned = modes // n_mode
-    ids = surf_ids[0, 0]
     shapes = jnp.swapaxes(mode_shapes[0, 0, 0], 0, 1)
     left, keep, pick = call(
         inner_kernel,
-        [VMEM] * 3 + [HBM],
-        [left.shape, kept, jax.ShapeDtypeStruct((naxial, ids.shape[1]), BF16)],
-        [pltpu.VMEM(ids.shape, ids.dtype), pltpu.SemaphoreType.DMA],
+        [VMEM] * 4,
+        [left.shape, kept, jax.ShapeDtypeStruct((naxial, surf_ids.shape[-1]), BF16)],
         flops=10_000_000,
-    )(turned, left, keep, ids)
+    )(turned, left, keep, e)
     keep, force = call(
         functools.partial(sweep_kernel, n_mode, ncirc),
         [VMEM] * 8,
         [kept, (n_rad * n_mode, 1, 128)],
         [pltpu.VMEM((modes, 128), F32)],
-    )(turned, second, first, left, keep, pick, ids, shapes)
+    )(turned, second, first, left, keep, pick, e, shapes)
     parts = lax.all_to_all(force, ("rad", "mode"), split_axis=0, concat_axis=0, tiled=True)
     final, own_force = call(
         finish_kernel,

time: 71.5 us -> 71.4 us (level)
  no operation moved by 1% of the time
where the time goes in v8:
time: 71.4 us; the launch traced here: 71.1 us
  blocking collectives  34.6 us (48%)
  starting transfers between devices  25 us (35%)
  Pallas kernels  6.89 us (10%)
  waiting for transfers between devices  3.91 us (5%)
  between operations  0.73 us (1%)
    all_to_all x1, blocking collectives, on_device(): lax.all_to_all(force, ('rad', 'mode'), split_axis=0, concat_axis=0, tiled...  19.2 us
    all_to_all x1, blocking collectives, on_device(): got = lax.all_to_all(send, 'mode', split_axis=0, concat_axis=0, tiled=True)  15.4 us
    ppermute x1, starting transfers between devices, on_device(): second = lax.ppermute(second, 'rad', swaps('rad', 1, False))  11.3 us
    ppermute x1, starting transfers between devices, on_device(): lax.ppermute(second, 'circ', [((i + 1) % n_circ, i) for i in range(n_circ)])  7.73 us
    ppermute x1, starting transfers between devices, on_device(): lax.ppermute(first, 'circ', [(i, (i + 1) % n_circ) for i in range(n_circ)])  4.04 us
    ppermute x1, waiting for transfers between devices, on_device(): second = lax.ppermute(second, 'rad', swaps('rad', 1, False))  2.29 us
    pallas_call x1, Pallas kernels, on_device(): call(pack_kernel, [HBM] * 7, [(n_mode, 24, 128), (ncirc + 1, nrad, naxial...  2.07 us
    pallas_call x1, Pallas kernels, on_device(): call(turn_kernel, [VMEM] * 6, [(15, 8 * nrad, 128), message, message, lef...  2 us
  transfers between devices with their start and end apart: 4, of which 3 were waited for; matrix products, arithmetic and copies ran while one was open for 0% of the time, Pallas kernels for 0%

profile of v8, /device:TPU:1, one launch (start us, length us, event | category | flops | bytes accessed | tf_op | source)
XLA Modules:
  0.0 71.1 jit_solution(2091488336180587137)
XLA Ops:
  0.6 2.1 %shard_map.95 = (f32[8,24,128]{2,1,0:T(8,128)}, f32[5,8,256]{2,1,0:T(8,128)}) custom-call(f32[8]{0:T(128)} %moduli_in.1, s32[8]{0:T(128)} %bitcast.14, f32[3,4,8,256]{3,2,1,0:T(8,128)} %prev.3, s32[4,8,256]{2,1,0:T(8,128)} %cls_in.1, f32[3,8,512]{2,1,0:T(8,128)} %bitcast.11, s32[8,512]{1,0:T(8,128)} %bitcast.12, s32[1,512]{1,0:T(1,128)} %bitcast.13), custom_call_target="tpu_custom_call" | custom-call | flops 1000000 | bytes 1000000 | tf_op jit(solution)/shard_map/pallas_call | solution.py:579
  2.7 0.0 copy-start
  2.7 0.0 copy-start.1
  2.7 15.4 %all_to_all.10.got = f32[8,24,128]{2,1,0:T(8,128)S(1)} all-to-all(f32[8,24,128]{2,1,0:T(8,128)} %get-tuple-element.21), channel_id=1, replica_groups=mesh['circ'=16,'rad'=6,'mode'=8] {'mode'}, dimensions={0} | all-to-all | bytes 196608 | tf_op jit(solution)/shard_map/all_to_all | solution.py:588
  18.1 0.0 copy-done
  18.1 0.0 copy-done.1
  18.1 0.8 %shard_map.96 = (f32[3,4,8,256]{3,2,1,0:T(8,128)S(1)}, f32[4,8,128]{2,1,0:T(8,128)S(1)}, f32[24,8,128]{2,1,0:T(8,128)S(1)}, f32[24,8,128]{2,1,0:T(8,128)S(1)}) custom-call(f32[8,24,128]{2,1,0:T(8,128)S(1)} %all_to_all.10.got, f32[3,4,8,256]{3,2,1,0:T(8,128)S(1)} %copy-done, f32[5,8,256]{2,1,0:T(8,128)S(1)} %copy-done.1), custom_call_target="tpu_custom_call" | custom-call | flops 1000000 | bytes 1000000 | tf_op jit(solution)/shard_map/pallas_call | solution.py:589
  18.9 4.0 %collective-permute-start = (f32[24,8,128]{2,1,0:T(8,128)S(1)}, f32[24,8,128]{2,1,0:T(8,128)S(1)}, u32[]{:S(2)}, u32[]{:S(2)}) collective-permute-start(f32[24,8,128]{2,1,0:T(8,128)S(1)} %get-tuple-element.24), channel_id=1, source_target_pairs={{0,48},{48,96},{96,144},{144,192},{192,240},{240,288},{288,336},{3... | collective-permute-start | bytes 294920 | tf_op jit(solution)/shard_map/ppermute | solution.py:595
  22.9 7.7 %collective-permute-start.1 = (f32[24,8,128]{2,1,0:T(8,128)S(1)}, f32[24,8,128]{2,1,0:T(8,128)S(1)}, u32[]{:S(2)}, u32[]{:S(2)}) collective-permute-start(f32[24,8,128]{2,1,0:T(8,128)S(1)} %get-tuple-element.25), channel_id=1, source_target_pairs={{48,0},{96,48},{144,96},{192,144},{240,192},{288,240},{336,288},{3... | collective-permute-start | bytes 294920 | tf_op jit(solution)/shard_map/ppermute | solution.py:596
  30.7 0.1 collective-permute-done.got_first
  30.8 1.5 %collective-permute-done.1.got_second = f32[24,8,128]{2,1,0:T(8,128)S(1)} collective-permute-done((f32[24,8,128]{2,1,0:T(8,128)S(1)}, f32[24,8,128]{2,1,0:T(8,128)S(1)}, u32[]{:S(2)}, u32[]{:S(2)}) %collective-permute-start.1) | collective-permute-done | bytes 98336 | tf_op jit(solution)/shard_map/ppermute | solution.py:596
  32.3 2.0 %shard_map.97 = (f32[15,64,128]{2,1,0:T(8,128)S(1)}, f32[24,8,128]{2,1,0:T(8,128)S(1)}, f32[24,8,128]{2,1,0:T(8,128)S(1)}, f32[2,39,8,384]{3,2,1,0:T(8,128)S(1)}, f32[6,64,128]{2,1,0:T(8,128)S(1)}) custom-call(f32[3,4,8,256]{3,2,1,0:T(8,128)S(1)} %copy-done, f32[5,8,256]{2,1,0:T(8,128)S(1)} %copy-done.1, f32[3,4,8,256]{3,2,1,0:T(8,128)S(1)} %get-tuple-element.22.rhs, ...), custom_call_target="tpu_custom_call" | custom-call | flops 1000000 | bytes 1000000 | tf_op jit(solution)/shard_map/pallas_call | solution.py:599
  34.3 11.3 %collective-permute-start.2 = (f32[24,8,128]{2,1,0:T(8,128)S(1)}, f32[24,8,128]{2,1,0:T(8,128)S(1)}, u32[]{:S(2)}, u32[]{:S(2)}) collective-permute-start(f32[24,8,128]{2,1,0:T(8,128)S(1)} %get-tuple-element.27), channel_id=1, source_target_pairs={{8,16},{16,8},{24,32},{32,24},{9,17},{17,9},{25,33},{33,25},{10,18... | collective-permute-start | bytes 294920 | tf_op jit(solution)/shard_map/ppermute | solution.py:604
  45.6 1.9 %collective-permute-start.3 = (f32[24,8,128]{2,1,0:T(8,128)S(1)}, f32[24,8,128]{2,1,0:T(8,128)S(1)}, u32[]{:S(2)}, u32[]{:S(2)}) collective-permute-start(f32[24,8,128]{2,1,0:T(8,128)S(1)} %get-tuple-element.28), channel_id=1, source_target_pairs={{0,8},{8,0},{16,24},{24,16},{32,40},{40,32},{1,9},{9,1},{17,25},{2... | collective-permute-start | bytes 294920 | tf_op jit(solution)/shard_map/ppermute | solution.py:605
  47.5 0.0 copy-start.2
  47.5 0.2 shard_map.98
  47.7 2.3 %collective-permute-done.2.got_second = f32[24,8,128]{2,1,0:T(8,128)S(1)} collective-permute-done((f32[24,8,128]{2,1,0:T(8,128)S(1)}, f32[24,8,128]{2,1,0:T(8,128)S(1)}, u32[]{:S(2)}, u32[]{:S(2)}) %collective-permute-start.2) | collective-permute-done | bytes 98336 | tf_op jit(solution)/shard_map/ppermute | solution.py:604
  50.0 0.0 collective-permute-done.3.got_first
  50.0 0.0 copy-done.2
  50.0 1.2 %shard_map.99 = (f32[6,64,128]{2,1,0:T(8,128)S(1)}, f32[48,1,128]{2,1,0:T(1,128)S(1)}) custom-call(f32[15,64,128]{2,1,0:T(8,128)S(1)} %get-tuple-element.26.turned, f32[24,8,128]{2,1,0:T(8,128)S(1)} %collective-permute-done.2.got_second, f32[24,8,128]{2,1,0:T(8,128)S(1)} %collective-permute-done.3.got_first, f32[2,39,8,384]{3,2,1,0:T(8,128)S(1)} %get-tuple-element.31.left, ...), custom_call_target="tpu_custom_call" | custom-call | flops 1000000 | bytes 1000000 | tf_op jit(solution)/shard_map/pallas_call | solution.py:615
  51.2 19.2 %all_to_all.11.parts = f32[48,1,128]{2,1,0:T(1,128)S(1)} all-to-all(f32[48,1,128]{2,1,0:T(1,128)S(1)} %get-tuple-element.35), channel_id=1, replica_groups=mesh['circ'=16,'rad'=6,'mode'=8] {'rad','mode'}, dimensions={0} | all-to-all | bytes 49152 | tf_op jit(solution)/shard_map/all_to_all | solution.py:621
  70.4 0.7 shard_map.100
Async XLA Ops:
  2.7 15.4 %copy-start = (f32[3,4,8,256]{3,2,1,0:T(8,128)S(1)}, f32[3,4,8,256]{3,2,1,0:T(8,128)}, u32[]{:S(2)}) copy-start(f32[3,4,8,256]{3,2,1,0:T(8,128)} %prev.3) | copy-start | bytes 294916
  2.7 15.4 %copy-start.1 = (f32[5,8,256]{2,1,0:T(8,128)S(1)}, f32[5,8,256]{2,1,0:T(8,128)}, u32[]{:S(2)}) copy-start(f32[5,8,256]{2,1,0:T(8,128)} %get-tuple-element.20.e.riding) | copy-start | bytes 122884
  18.9 11.9 %collective-permute-start = (f32[24,8,128]{2,1,0:T(8,128)S(1)}, f32[24,8,128]{2,1,0:T(8,128)S(1)}, u32[]{:S(2)}, u32[]{:S(2)}) collective-permute-start(f32[24,8,128]{2,1,0:T(8,128)S(1)} %get-tuple-element.24), channel_id=1, source_target_pairs={{0,48},{48,96},{96,144},{144,192},{192,240},{240,288},{288,336},{3... | collective-permute-start | bytes 294920 | tf_op jit(solution)/shard_map/ppermute | solution.py:595
  22.9 9.4 %collective-permute-start.1 = (f32[24,8,128]{2,1,0:T(8,128)S(1)}, f32[24,8,128]{2,1,0:T(8,128)S(1)}, u32[]{:S(2)}, u32[]{:S(2)}) collective-permute-start(f32[24,8,128]{2,1,0:T(8,128)S(1)} %get-tuple-element.25), channel_id=1, source_target_pairs={{48,0},{96,48},{144,96},{192,144},{240,192},{288,240},{336,288},{3... | collective-permute-start | bytes 294920 | tf_op jit(solution)/shard_map/ppermute | solution.py:596
  34.3 15.7 %collective-permute-start.2 = (f32[24,8,128]{2,1,0:T(8,128)S(1)}, f32[24,8,128]{2,1,0:T(8,128)S(1)}, u32[]{:S(2)}, u32[]{:S(2)}) collective-permute-start(f32[24,8,128]{2,1,0:T(8,128)S(1)} %get-tuple-element.27), channel_id=1, source_target_pairs={{8,16},{16,8},{24,32},{32,24},{9,17},{17,9},{25,33},{33,25},{10,18... | collective-permute-start | bytes 294920 | tf_op jit(solution)/shard_map/ppermute | solution.py:604
  45.6 4.4 %collective-permute-start.3 = (f32[24,8,128]{2,1,0:T(8,128)S(1)}, f32[24,8,128]{2,1,0:T(8,128)S(1)}, u32[]{:S(2)}, u32[]{:S(2)}) collective-permute-start(f32[24,8,128]{2,1,0:T(8,128)S(1)} %get-tuple-element.28), channel_id=1, source_target_pairs={{0,8},{8,0},{16,24},{24,16},{32,40},{40,32},{1,9},{9,1},{17,25},{2... | collective-permute-start | bytes 294920 | tf_op jit(solution)/shard_map/ppermute | solution.py:605
  47.5 2.5 %copy-start.2 = (f32[1,1,1,24,3,512]{5,3,4,2,1,0:T(8,128)S(1)}, f32[1,1,1,24,3,512]{5,3,4,2,1,0:T(8,128)}, u32[]{:S(2)}) copy-start(f32[1,1,1,24,3,512]{5,3,4,2,1,0:T(8,128)} %param.15) | copy-start | bytes 442372

commit v9 on v7

--- a/solution.py
+++ b/solution.py
@@ -343,7 +343,8 @@
 
 
 def works_ahead():
-    return (lax.axis_index("circ") % 4 != 0) | (lax.axis_index("rad") % 2 == 1)
+    rad = lax.axis_index("rad")
+    return (lax.axis_index("circ") % 4 != 0) | (rad % 2 == 1) | (rad == 0)
 
 
 def inner_work(turned, left, keep):

time: 71.5 us -> 71.5 us (level)
  no operation moved by 1% of the time
where the time goes in v9:
time: 71.5 us; the launch traced here: 71.1 us
  blocking collectives  34.6 us (48%)
  starting transfers between devices  25 us (35%)
  Pallas kernels  6.86 us (10%)
  waiting for transfers between devices  3.25 us (5%)
  between operations  0.73 us (1%)
    all_to_all x1, blocking collectives, on_device(): lax.all_to_all(force, ('rad', 'mode'), split_axis=0, concat_axis=0, tiled...  19.2 us
    all_to_all x1, blocking collectives, on_device(): got = lax.all_to_all(send, 'mode', split_axis=0, concat_axis=0, tiled=True)  15.4 us
    ppermute x1, starting transfers between devices, on_device(): second = lax.ppermute(second, 'rad', swaps('rad', 1, False))  11.3 us
    ppermute x1, starting transfers between devices, on_device(): lax.ppermute(second, 'circ', [((i + 1) % n_circ, i) for i in range(n_circ)])  7.73 us
    ppermute x1, starting transfers between devices, on_device(): lax.ppermute(first, 'circ', [(i, (i + 1) % n_circ) for i in range(n_circ)])  4.04 us
    pallas_call x1, Pallas kernels, on_device(): call(pack_kernel, [HBM] * 6, [(n_mode, 24, 128), cells], [pltpu.SMEM(x.sh...  2.06 us
    pallas_call x1, Pallas kernels, on_device(): call(turn_kernel, [VMEM] * 6, [(15, 8 * nrad, 128), message, message, lef...  1.99 us
    ppermute x1, starting transfers between devices, on_device(): first = lax.ppermute(first, 'rad', swaps('rad', 0, False))  1.92 us
  transfers between devices with their start and end apart: 4, of which 3 were waited for; matrix products, arithmetic and copies ran while one was open for 0% of the time, Pallas kernels for 0%

profile of v9, /device:TPU:1, one launch (start us, length us, event | category | flops | bytes accessed | tf_op | source)
XLA Modules:
  0.0 71.1 jit_solution(11582164674092068378)
XLA Ops:
  0.6 2.1 %shard_map.95 = (f32[8,24,128]{2,1,0:T(8,128)}, f32[4,8,256]{2,1,0:T(8,128)}) custom-call(f32[8]{0:T(128)} %moduli_in.1, s32[8]{0:T(128)} %bitcast.15, f32[3,4,8,256]{3,2,1,0:T(8,128)} %prev.3, s32[4,8,256]{2,1,0:T(8,128)} %cls_in.1, f32[3,8,512]{2,1,0:T(8,128)} %bitcast.13, s32[8,512]{1,0:T(8,128)} %bitcast.14), custom_call_target="tpu_custom_call" | custom-call | flops 1000000 | bytes 1000000 | tf_op jit(solution)/shard_map/pallas_call | solution.py:575
  2.7 0.0 copy-start
  2.7 0.0 copy-start.2
  2.7 15.4 %all_to_all.10.got = f32[8,24,128]{2,1,0:T(8,128)S(1)} all-to-all(f32[8,24,128]{2,1,0:T(8,128)} %get-tuple-element.21), channel_id=1, replica_groups=mesh['circ'=16,'rad'=6,'mode'=8] {'mode'}, dimensions={0} | all-to-all | bytes 196608 | tf_op jit(solution)/shard_map/all_to_all | solution.py:584
  18.1 0.0 copy-done
  18.1 0.0 copy-done.2
  18.1 0.8 %shard_map.96 = (f32[3,4,8,256]{3,2,1,0:T(8,128)S(1)}, f32[4,8,128]{2,1,0:T(8,128)S(1)}, f32[24,8,128]{2,1,0:T(8,128)S(1)}, f32[24,8,128]{2,1,0:T(8,128)S(1)}) custom-call(f32[8,24,128]{2,1,0:T(8,128)S(1)} %all_to_all.10.got, f32[3,4,8,256]{3,2,1,0:T(8,128)S(1)} %copy-done, f32[4,8,256]{2,1,0:T(8,128)S(1)} %copy-done.2), custom_call_target="tpu_custom_call" | custom-call | flops 1000000 | bytes 1000000 | tf_op jit(solution)/shard_map/pallas_call | solution.py:585
  18.9 4.0 %collective-permute-start = (f32[24,8,128]{2,1,0:T(8,128)S(1)}, f32[24,8,128]{2,1,0:T(8,128)S(1)}, u32[]{:S(2)}, u32[]{:S(2)}) collective-permute-start(f32[24,8,128]{2,1,0:T(8,128)S(1)} %get-tuple-element.24), channel_id=1, source_target_pairs={{0,48},{48,96},{96,144},{144,192},{192,240},{240,288},{288,336},{3... | collective-permute-start | bytes 294920 | tf_op jit(solution)/shard_map/ppermute | solution.py:591
  22.9 7.7 %collective-permute-start.1 = (f32[24,8,128]{2,1,0:T(8,128)S(1)}, f32[24,8,128]{2,1,0:T(8,128)S(1)}, u32[]{:S(2)}, u32[]{:S(2)}) collective-permute-start(f32[24,8,128]{2,1,0:T(8,128)S(1)} %get-tuple-element.25), channel_id=1, source_target_pairs={{48,0},{96,48},{144,96},{192,144},{240,192},{288,240},{336,288},{3... | collective-permute-start | bytes 294920 | tf_op jit(solution)/shard_map/ppermute | solution.py:592
  30.7 0.1 collective-permute-done.got_first
  30.8 1.5 %collective-permute-done.1.got_second = f32[24,8,128]{2,1,0:T(8,128)S(1)} collective-permute-done((f32[24,8,128]{2,1,0:T(8,128)S(1)}, f32[24,8,128]{2,1,0:T(8,128)S(1)}, u32[]{:S(2)}, u32[]{:S(2)}) %collective-permute-start.1) | collective-permute-done | bytes 98336 | tf_op jit(solution)/shard_map/ppermute | solution.py:592
  32.3 2.0 %shard_map.97 = (f32[15,64,128]{2,1,0:T(8,128)S(1)}, f32[24,8,128]{2,1,0:T(8,128)S(1)}, f32[24,8,128]{2,1,0:T(8,128)S(1)}, f32[2,39,8,384]{3,2,1,0:T(8,128)S(1)}, f32[6,64,128]{2,1,0:T(8,128)S(1)}) custom-call(f32[3,4,8,256]{3,2,1,0:T(8,128)S(1)} %copy-done, f32[4,8,256]{2,1,0:T(8,128)S(1)} %copy-done.2, f32[3,4,8,256]{3,2,1,0:T(8,128)S(1)} %get-tuple-element.22.rhs, ...), custom_call_target="tpu_custom_call" | custom-call | flops 1000000 | bytes 1000000 | tf_op jit(solution)/shard_map/pallas_call | solution.py:595
  34.3 11.3 %collective-permute-start.2 = (f32[24,8,128]{2,1,0:T(8,128)S(1)}, f32[24,8,128]{2,1,0:T(8,128)S(1)}, u32[]{:S(2)}, u32[]{:S(2)}) collective-permute-start(f32[24,8,128]{2,1,0:T(8,128)S(1)} %get-tuple-element.27), channel_id=1, source_target_pairs={{8,16},{16,8},{24,32},{32,24},{9,17},{17,9},{25,33},{33,25},{10,18... | collective-permute-start | bytes 294920 | tf_op jit(solution)/shard_map/ppermute | solution.py:600
  45.6 1.9 %collective-permute-start.3 = (f32[24,8,128]{2,1,0:T(8,128)S(1)}, f32[24,8,128]{2,1,0:T(8,128)S(1)}, u32[]{:S(2)}, u32[]{:S(2)}) collective-permute-start(f32[24,8,128]{2,1,0:T(8,128)S(1)} %get-tuple-element.28), channel_id=1, source_target_pairs={{0,8},{8,0},{16,24},{24,16},{32,40},{40,32},{1,9},{9,1},{17,25},{2... | collective-permute-start | bytes 294920 | tf_op jit(solution)/shard_map/ppermute | solution.py:601
  47.5 0.0 copy-start.3
  47.5 0.7 copy-done.3
  48.2 0.0 copy-start.1
  48.2 0.1 shard_map.98
  48.3 1.6 %collective-permute-done.2.got_second = f32[24,8,128]{2,1,0:T(8,128)S(1)} collective-permute-done((f32[24,8,128]{2,1,0:T(8,128)S(1)}, f32[24,8,128]{2,1,0:T(8,128)S(1)}, u32[]{:S(2)}, u32[]{:S(2)}) %collective-permute-start.2) | collective-permute-done | bytes 98336 | tf_op jit(solution)/shard_map/ppermute | solution.py:600
  50.0 0.0 collective-permute-done.3.got_first
  50.0 0.0 copy-done.1
  50.0 1.2 %shard_map.99 = (f32[6,64,128]{2,1,0:T(8,128)S(1)}, f32[48,1,128]{2,1,0:T(1,128)S(1)}) custom-call(f32[15,64,128]{2,1,0:T(8,128)S(1)} %get-tuple-element.26.turned, f32[24,8,128]{2,1,0:T(8,128)S(1)} %collective-permute-done.2.got_second, f32[24,8,128]{2,1,0:T(8,128)S(1)} %collective-permute-done.3.got_first, f32[2,39,8,384]{3,2,1,0:T(8,128)S(1)} %get-tuple-element.31.left, ...), custom_call_target="tpu_custom_call" | custom-call | flops 1000000 | bytes 1000000 | tf_op jit(solution)/shard_map/pallas_call | solution.py:613
  51.2 19.2 %all_to_all.11.parts = f32[48,1,128]{2,1,0:T(1,128)S(1)} all-to-all(f32[48,1,128]{2,1,0:T(1,128)S(1)} %get-tuple-element.35), channel_id=1, replica_groups=mesh['circ'=16,'rad'=6,'mode'=8] {'rad','mode'}, dimensions={0} | all-to-all | bytes 49152 | tf_op jit(solution)/shard_map/all_to_all | solution.py:619
  70.4 0.7 shard_map.100
Async XLA Ops:
  2.7 15.4 %copy-start = (f32[3,4,8,256]{3,2,1,0:T(8,128)S(1)}, f32[3,4,8,256]{3,2,1,0:T(8,128)}, u32[]{:S(2)}) copy-start(f32[3,4,8,256]{3,2,1,0:T(8,128)} %prev.3) | copy-start | bytes 294916
  2.7 15.4 %copy-start.2 = (f32[4,8,256]{2,1,0:T(8,128)S(1)}, f32[4,8,256]{2,1,0:T(8,128)}, u32[]{:S(2)}) copy-start(f32[4,8,256]{2,1,0:T(8,128)} %get-tuple-element.20.e) | copy-start | bytes 98308
  18.9 11.9 %collective-permute-start = (f32[24,8,128]{2,1,0:T(8,128)S(1)}, f32[24,8,128]{2,1,0:T(8,128)S(1)}, u32[]{:S(2)}, u32[]{:S(2)}) collective-permute-start(f32[24,8,128]{2,1,0:T(8,128)S(1)} %get-tuple-element.24), channel_id=1, source_target_pairs={{0,48},{48,96},{96,144},{144,192},{192,240},{240,288},{288,336},{3... | collective-permute-start | bytes 294920 | tf_op jit(solution)/shard_map/ppermute | solution.py:591
  22.9 9.4 %collective-permute-start.1 = (f32[24,8,128]{2,1,0:T(8,128)S(1)}, f32[24,8,128]{2,1,0:T(8,128)S(1)}, u32[]{:S(2)}, u32[]{:S(2)}) collective-permute-start(f32[24,8,128]{2,1,0:T(8,128)S(1)} %get-tuple-element.25), channel_id=1, source_target_pairs={{48,0},{96,48},{144,96},{192,144},{240,192},{288,240},{336,288},{3... | collective-permute-start | bytes 294920 | tf_op jit(solution)/shard_map/ppermute | solution.py:592
  34.3 15.7 %collective-permute-start.2 = (f32[24,8,128]{2,1,0:T(8,128)S(1)}, f32[24,8,128]{2,1,0:T(8,128)S(1)}, u32[]{:S(2)}, u32[]{:S(2)}) collective-permute-start(f32[24,8,128]{2,1,0:T(8,128)S(1)} %get-tuple-element.27), channel_id=1, source_target_pairs={{8,16},{16,8},{24,32},{32,24},{9,17},{17,9},{25,33},{33,25},{10,18... | collective-permute-start | bytes 294920 | tf_op jit(solution)/shard_map/ppermute | solution.py:600
  45.6 4.4 %collective-permute-start.3 = (f32[24,8,128]{2,1,0:T(8,128)S(1)}, f32[24,8,128]{2,1,0:T(8,128)S(1)}, u32[]{:S(2)}, u32[]{:S(2)}) collective-permute-start(f32[24,8,128]{2,1,0:T(8,128)S(1)} %get-tuple-element.28), channel_id=1, source_target_pairs={{0,8},{8,0},{16,24},{24,16},{32,40},{40,32},{1,9},{9,1},{17,25},{2... | collective-permute-start | bytes 294920 | tf_op jit(solution)/shard_map/ppermute | solution.py:601
  47.5 0.7 copy-start.3
  48.2 1.8 %copy-start.1 = (f32[1,1,1,24,3,512]{5,3,4,2,1,0:T(8,128)S(1)}, f32[1,1,1,24,3,512]{5,3,4,2,1,0:T(8,128)}, u32[]{:S(2)}) copy-start(f32[1,1,1,24,3,512]{5,3,4,2,1,0:T(8,128)} %param.15) | copy-start | bytes 442372

commit v10 on v7

--- a/solution.py
+++ b/solution.py
@@ -148,12 +148,27 @@
             cut = slice(128 * t, 128 * (t + 1))
             for f in range(4):
                 for j in range(2):
-                    source = prev[f, base + j] if f < 3 else e[base + j]
-                    out[4 * f + 2 * t + j] = source[:, cut]
+                    if base == 0:
+                        source = prev[f, base + j] if f < 3 else e[base + j]
+                        out[4 * f + 2 * t + j] = source[:, cut]
             for i in range(3):
-                out[16 + 2 * i + t] = rhs[i, edge][:, cut]
+                out[out.shape[0] - 8 + 2 * i + t] = rhs[i, edge][:, cut]
         for j in range(2):
-            out[22 + j] = ends[base + j]
+            out[out.shape[0] - 2 + j] = ends[base + j]
+
+
+def early_kernel(prev, e, up):
+    ncirc = prev.shape[1]
+    for f in range(4):
+        for t in range(2):
+            for j in range(2):
+                plane = prev[f, ncirc - 2 + j] if f < 3 else e[ncirc - 2 + j]
+                up[4 * f + 2 * t + j] = plane[:, 128 * t : 128 * (t + 1)]
+
+
+def join_kernel(early, late, whole):
+    whole[: early.shape[0]] = early[...]
+    whole[early.shape[0] :] = late[...]
 
 
 def turn_kernel(prev, e, rhs, ends, got_first, got_second, turned, first, second, left, keep):
@@ -584,11 +599,16 @@
     rhs, ends, first, second = call(
         scatter_kernel,
         [VMEM] * 3,
-        [(3,) + cells, (ncirc, nrad, 128), message, message],
+        [(3,) + cells, (ncirc, nrad, 128), (8, 8, 128), message],
+        flops=1,
     )(got, adjoint_prev, e)
     n_circ = lax.axis_size("circ")
-    first = lax.ppermute(first, "circ", [(i, (i + 1) % n_circ) for i in range(n_circ)])
-    second = lax.ppermute(second, "circ", [((i + 1) % n_circ, i) for i in range(n_circ)])
+    upward = [(i, (i + 1) % n_circ) for i in range(n_circ)]
+    (up,) = call(early_kernel, [VMEM] * 2, [(16, 8, 128)])(adjoint_prev, e)
+    up = lax.ppermute(up, "circ", upward)
+    first = lax.ppermute(first, "circ", upward)
+    (first,) = call(join_kernel, [VMEM] * 2, [message], flops=20_000_000_000)(up, first)
+    second = lax.ppermute(second, "circ", [(j, i) for i, j in upward])
     kept = (6, 8 * nrad, 128)
     left = (2, COUNT, 8, 384)
     turned, first, second, left, keep = call(

time: 71.5 us -> 71.5 us (level)
  blocking collectives: 34.6 us -> 19.2 us
  starting transfers between devices: 25 us -> 36.8 us
  waiting for transfers between devices: 3.25 us -> 6.76 us
    all_to_all x1 -> x0, blocking collectives: 15.4 us -> none  [on_device(): got = lax.all_to_all(send, 'mode', split_axis=0, concat_axis=0, tiled=True)]
    all_to_all x0 -> x1, starting transfers between devices: none -> 7.79 us  [on_device(): got = lax.all_to_all(send, 'mode', split_axis=0, concat_axis=0, tiled=True)]
    ppermute x2 -> x3, starting transfers between devices: 11.8 us -> 15.8 us  [the longest x1 7.73 us: on_device(): second = lax.ppermute(second, 'circ', [(j, i) for i, j in upward])]
    all_to_all x0 -> x1, waiting for transfers between devices: none -> 3.54 us  [on_device(): got = lax.all_to_all(send, 'mode', split_axis=0, concat_axis=0, tiled=True)]
    ppermute x2 -> x3, waiting for transfers between devices: 1.62 us -> 1.59 us  [the longest x1 1.58 us: on_device(): second = lax.ppermute(second, 'circ', [(j, i) for i, j in upward])]
  transfers between devices with their start and end apart: 4 -> 6, of which waited for: 3 -> 3; matrix products, arithmetic and copies ran while one was open for 0% -> 0% of each run, Pallas kernels for 0% -> 1%
where the time goes in v10:
time: 71.5 us; the launch traced here: 71.1 us
  starting transfers between devices  36.8 us (51%)
  blocking collectives  19.2 us (27%)
  Pallas kernels  6.85 us (10%)
  waiting for transfers between devices  6.76 us (9%)
  between operations  0.78 us (1%)
    all_to_all x1, blocking collectives, on_device(): lax.all_to_all(force, ('rad', 'mode'), split_axis=0, concat_axis=0, tiled...  19.2 us
    ppermute x1, starting transfers between devices, on_device(): second = lax.ppermute(second, 'rad', swaps('rad', 1, False))  11.3 us
    all_to_all x1, starting transfers between devices, on_device(): got = lax.all_to_all(send, 'mode', split_axis=0, concat_axis=0, tiled=True)  7.79 us
    ppermute x1, starting transfers between devices, on_device(): second = lax.ppermute(second, 'circ', [(j, i) for i, j in upward])  7.73 us
    ppermute x1, starting transfers between devices, on_device(): first = lax.ppermute(first, 'circ', upward)  4.04 us
    ppermute x1, starting transfers between devices, on_device(): up = lax.ppermute(up, 'circ', upward)  4 us
    all_to_all x1, waiting for transfers between devices, on_device(): got = lax.all_to_all(send, 'mode', split_axis=0, concat_axis=0, tiled=True)  3.54 us
    pallas_call x1, Pallas kernels, on_device(): call(pack_kernel, [HBM] * 6, [(n_mode, 24, 128), cells], [pltpu.SMEM(x.sh...  2.06 us
  transfers between devices with their start and end apart: 6, of which 3 were waited for; matrix products, arithmetic and copies ran while one was open for 0% of the time, Pallas kernels for 1%

profile of v10, /device:TPU:1, one launch (start us, length us, event | category | flops | bytes accessed | tf_op | source)
XLA Modules:
  0.0 71.1 jit_solution(7008679143990199878)
XLA Ops:
  0.6 2.1 %shard_map.95 = (f32[8,24,128]{2,1,0:T(8,128)}, f32[4,8,256]{2,1,0:T(8,128)}) custom-call(f32[8]{0:T(128)} %moduli_in.1, s32[8]{0:T(128)} %bitcast.15, f32[3,4,8,256]{3,2,1,0:T(8,128)} %prev.5, s32[4,8,256]{2,1,0:T(8,128)} %cls_in.1, f32[3,8,512]{2,1,0:T(8,128)} %bitcast.13, s32[8,512]{1,0:T(8,128)} %bitcast.14), custom_call_target="tpu_custom_call" | custom-call | flops 1000000 | bytes 1000000 | tf_op jit(solution)/shard_map/pallas_call | solution.py:589
  2.7 0.0 copy-start
  2.7 0.0 copy-start.1
  2.7 7.8 %all-to-all-start = ((f32[8,24,128]{2,1,0:T(8,128)}), f32[8,24,128]{2,1,0:T(8,128)S(1)}, u32[]{:S(2)}, u32[]{:S(2)}) async-start(f32[8,24,128]{2,1,0:T(8,128)} %get-tuple-element.21), calls=%async_computation | async-start | bytes 196608 | tf_op jit(solution)/shard_map/all_to_all | solution.py:598
  10.5 0.0 copy-done
  10.5 0.0 copy-done.1
  10.5 4.0 %collective-permute-start = (f32[16,8,128]{2,1,0:T(8,128)S(1)}, f32[16,8,128]{2,1,0:T(8,128)S(1)}, u32[]{:S(2)}, u32[]{:S(2)}) collective-permute-start(f32[16,8,128]{2,1,0:T(8,128)S(1)} %shard_map.97), channel_id=1, source_target_pairs={{0,48},{48,96},{96,144},{144,192},{192,240},{240,288},{288,336},{3... | collective-permute-start | bytes 196616 | tf_op jit(solution)/shard_map/ppermute | solution.py:608
  14.6 3.5 %all-to-all-done.got = f32[8,24,128]{2,1,0:T(8,128)S(1)} async-done(((f32[8,24,128]{2,1,0:T(8,128)}), f32[8,24,128]{2,1,0:T(8,128)S(1)}, u32[]{:S(2)}, u32[]{:S(2)}) %all-to-all-start) | async-done | bytes 98336 | tf_op jit(solution)/shard_map/all_to_all | solution.py:598
  18.1 0.8 %shard_map.96 = (f32[3,4,8,256]{3,2,1,0:T(8,128)S(1)}, f32[4,8,128]{2,1,0:T(8,128)S(1)}, f32[8,8,128]{2,1,0:T(8,128)S(1)}, f32[24,8,128]{2,1,0:T(8,128)S(1)}) custom-call(f32[8,24,128]{2,1,0:T(8,128)S(1)} %all-to-all-done.got, f32[3,4,8,256]{3,2,1,0:T(8,128)S(1)} %copy-done, f32[4,8,256]{2,1,0:T(8,128)S(1)} %copy-done.1), custom_call_target="tpu_custom_call" | custom-call | flops 1 | bytes 1000000 | tf_op jit(solution)/shard_map/pallas_call | solution.py:599
  18.9 4.0 %collective-permute-start.1 = (f32[8,8,128]{2,1,0:T(8,128)S(1)}, f32[8,8,128]{2,1,0:T(8,128)S(1)}, u32[]{:S(2)}, u32[]{:S(2)}) collective-permute-start(f32[8,8,128]{2,1,0:T(8,128)S(1)} %get-tuple-element.24), channel_id=1, source_target_pairs={{0,48},{48,96},{96,144},{144,192},{192,240},{240,288},{288,336},{3... | collective-permute-start | bytes 98312 | tf_op jit(solution)/shard_map/ppermute | solution.py:609
  22.9 7.7 %collective-permute-start.2 = (f32[24,8,128]{2,1,0:T(8,128)S(1)}, f32[24,8,128]{2,1,0:T(8,128)S(1)}, u32[]{:S(2)}, u32[]{:S(2)}) collective-permute-start(f32[24,8,128]{2,1,0:T(8,128)S(1)} %get-tuple-element.25), channel_id=1, source_target_pairs={{48,0},{96,48},{144,96},{192,144},{240,192},{288,240},{336,288},{3... | collective-permute-start | bytes 294920 | tf_op jit(solution)/shard_map/ppermute | solution.py:611
  30.7 0.0 collective-permute-done.early
  30.7 0.0 collective-permute-done.1.late
  30.7 1.6 %collective-permute-done.2.got_second = f32[24,8,128]{2,1,0:T(8,128)S(1)} collective-permute-done((f32[24,8,128]{2,1,0:T(8,128)S(1)}, f32[24,8,128]{2,1,0:T(8,128)S(1)}, u32[]{:S(2)}, u32[]{:S(2)}) %collective-permute-start.2) | collective-permute-done | bytes 98336 | tf_op jit(solution)/shard_map/ppermute | solution.py:611
  32.3 2.0 %shard_map.99 = (f32[15,64,128]{2,1,0:T(8,128)S(1)}, f32[24,8,128]{2,1,0:T(8,128)S(1)}, f32[24,8,128]{2,1,0:T(8,128)S(1)}, f32[2,39,8,384]{3,2,1,0:T(8,128)S(1)}, f32[6,64,128]{2,1,0:T(8,128)S(1)}) custom-call(f32[3,4,8,256]{3,2,1,0:T(8,128)S(1)} %copy-done, f32[4,8,256]{2,1,0:T(8,128)S(1)} %copy-done.1, f32[3,4,8,256]{3,2,1,0:T(8,128)S(1)} %get-tuple-element.22.rhs, ...), custom_call_target="tpu_custom_call" | custom-call | flops 1000000 | bytes 1000000 | tf_op jit(solution)/shard_map/pallas_call | solution.py:614
  34.3 11.3 %collective-permute-start.3 = (f32[24,8,128]{2,1,0:T(8,128)S(1)}, f32[24,8,128]{2,1,0:T(8,128)S(1)}, u32[]{:S(2)}, u32[]{:S(2)}) collective-permute-start(f32[24,8,128]{2,1,0:T(8,128)S(1)} %get-tuple-element.27), channel_id=1, source_target_pairs={{8,16},{16,8},{24,32},{32,24},{9,17},{17,9},{25,33},{33,25},{10,18... | collective-permute-start | bytes 294920 | tf_op jit(solution)/shard_map/ppermute | solution.py:619
  45.6 1.9 %collective-permute-start.4 = (f32[24,8,128]{2,1,0:T(8,128)S(1)}, f32[24,8,128]{2,1,0:T(8,128)S(1)}, u32[]{:S(2)}, u32[]{:S(2)}) collective-permute-start(f32[24,8,128]{2,1,0:T(8,128)S(1)} %get-tuple-element.28), channel_id=1, source_target_pairs={{0,8},{8,0},{16,24},{24,16},{32,40},{40,32},{1,9},{9,1},{17,25},{2... | collective-permute-start | bytes 294920 | tf_op jit(solution)/shard_map/ppermute | solution.py:620
  47.5 0.0 copy-start.3
  47.5 0.7 copy-done.3
  48.2 0.0 copy-start.2
  48.2 0.1 shard_map.100
  48.3 1.6 %collective-permute-done.3.got_second = f32[24,8,128]{2,1,0:T(8,128)S(1)} collective-permute-done((f32[24,8,128]{2,1,0:T(8,128)S(1)}, f32[24,8,128]{2,1,0:T(8,128)S(1)}, u32[]{:S(2)}, u32[]{:S(2)}) %collective-permute-start.3) | collective-permute-done | bytes 98336 | tf_op jit(solution)/shard_map/ppermute | solution.py:619
  50.0 0.0 collective-permute-done.4.got_first
  50.0 0.0 copy-done.2
  50.0 1.2 %shard_map.101 = (f32[6,64,128]{2,1,0:T(8,128)S(1)}, f32[48,1,128]{2,1,0:T(1,128)S(1)}) custom-call(f32[15,64,128]{2,1,0:T(8,128)S(1)} %get-tuple-element.26.turned, f32[24,8,128]{2,1,0:T(8,128)S(1)} %collective-permute-done.3.got_second, f32[24,8,128]{2,1,0:T(8,128)S(1)} %collective-permute-done.4.got_first, f32[2,39,8,384]{3,2,1,0:T(8,128)S(1)} %get-tuple-element.31.left, ...), custom_call_target="tpu_custom_call" | custom-call | flops 1000000 | bytes 1000000 | tf_op jit(solution)/shard_map/pallas_call | solution.py:632
  51.2 19.2 %all_to_all.10.parts = f32[48,1,128]{2,1,0:T(1,128)S(1)} all-to-all(f32[48,1,128]{2,1,0:T(1,128)S(1)} %get-tuple-element.35), channel_id=1, replica_groups=mesh['circ'=16,'rad'=6,'mode'=8] {'rad','mode'}, dimensions={0} | all-to-all | bytes 49152 | tf_op jit(solution)/shard_map/all_to_all | solution.py:638
  70.4 0.7 shard_map.102
  (2 shorter events, 0.0 us)
Async XLA Ops:
  2.7 7.8 %copy-start = (f32[3,4,8,256]{3,2,1,0:T(8,128)S(1)}, f32[3,4,8,256]{3,2,1,0:T(8,128)}, u32[]{:S(2)}) copy-start(f32[3,4,8,256]{3,2,1,0:T(8,128)} %prev.5) | copy-start | bytes 294916
  2.7 7.8 %copy-start.1 = (f32[4,8,256]{2,1,0:T(8,128)S(1)}, f32[4,8,256]{2,1,0:T(8,128)}, u32[]{:S(2)}) copy-start(f32[4,8,256]{2,1,0:T(8,128)} %get-tuple-element.20.e) | copy-start | bytes 98308
  2.7 15.4 %all-to-all-start = ((f32[8,24,128]{2,1,0:T(8,128)}), f32[8,24,128]{2,1,0:T(8,128)S(1)}, u32[]{:S(2)}, u32[]{:S(2)}) async-start(f32[8,24,128]{2,1,0:T(8,128)} %get-tuple-element.21), calls=%async_computation | async-start | bytes 196608 | tf_op jit(solution)/shard_map/all_to_all | solution.py:598
  10.5 20.1 %collective-permute-start = (f32[16,8,128]{2,1,0:T(8,128)S(1)}, f32[16,8,128]{2,1,0:T(8,128)S(1)}, u32[]{:S(2)}, u32[]{:S(2)}) collective-permute-start(f32[16,8,128]{2,1,0:T(8,128)S(1)} %shard_map.97), channel_id=1, source_target_pairs={{0,48},{48,96},{96,144},{144,192},{192,240},{240,288},{288,336},{3... | collective-permute-start | bytes 196616 | tf_op jit(solution)/shard_map/ppermute | solution.py:608
  18.9 11.8 %collective-permute-start.1 = (f32[8,8,128]{2,1,0:T(8,128)S(1)}, f32[8,8,128]{2,1,0:T(8,128)S(1)}, u32[]{:S(2)}, u32[]{:S(2)}) collective-permute-start(f32[8,8,128]{2,1,0:T(8,128)S(1)} %get-tuple-element.24), channel_id=1, source_target_pairs={{0,48},{48,96},{96,144},{144,192},{192,240},{240,288},{288,336},{3... | collective-permute-start | bytes 98312 | tf_op jit(solution)/shard_map/ppermute | solution.py:609
  22.9 9.4 %collective-permute-start.2 = (f32[24,8,128]{2,1,0:T(8,128)S(1)}, f32[24,8,128]{2,1,0:T(8,128)S(1)}, u32[]{:S(2)}, u32[]{:S(2)}) collective-permute-start(f32[24,8,128]{2,1,0:T(8,128)S(1)} %get-tuple-element.25), channel_id=1, source_target_pairs={{48,0},{96,48},{144,96},{192,144},{240,192},{288,240},{336,288},{3... | collective-permute-start | bytes 294920 | tf_op jit(solution)/shard_map/ppermute | solution.py:611
  34.3 15.7 %collective-permute-start.3 = (f32[24,8,128]{2,1,0:T(8,128)S(1)}, f32[24,8,128]{2,1,0:T(8,128)S(1)}, u32[]{:S(2)}, u32[]{:S(2)}) collective-permute-start(f32[24,8,128]{2,1,0:T(8,128)S(1)} %get-tuple-element.27), channel_id=1, source_target_pairs={{8,16},{16,8},{24,32},{32,24},{9,17},{17,9},{25,33},{33,25},{10,18... | collective-permute-start | bytes 294920 | tf_op jit(solution)/shard_map/ppermute | solution.py:619
  45.6 4.4 %collective-permute-start.4 = (f32[24,8,128]{2,1,0:T(8,128)S(1)}, f32[24,8,128]{2,1,0:T(8,128)S(1)}, u32[]{:S(2)}, u32[]{:S(2)}) collective-permute-start(f32[24,8,128]{2,1,0:T(8,128)S(1)} %get-tuple-element.28), channel_id=1, source_target_pairs={{0,8},{8,0},{16,24},{24,16},{32,40},{40,32},{1,9},{9,1},{17,25},{2... | collective-permute-start | bytes 294920 | tf_op jit(solution)/shard_map/ppermute | solution.py:620
  47.5 0.7 copy-start.3
  48.2 1.8 %copy-start.2 = (f32[1,1,1,24,3,512]{5,3,4,2,1,0:T(8,128)S(1)}, f32[1,1,1,24,3,512]{5,3,4,2,1,0:T(8,128)}, u32[]{:S(2)}) copy-start(f32[1,1,1,24,3,512]{5,3,4,2,1,0:T(8,128)} %param.15) | copy-start | bytes 442372
